TPU v7x, 128 devices: a whole 4x4x4 slice. The times are simulated.
128 devices in a mesh: group: 8 (over y, x_lo), tp: 16 (over x_hi, z, core).
Axes of the slice: x: 4 (x_hi: 2, x_lo: 2; x = x_hi * 2 + x_lo), y: 4, z: 4, core: 2. Of those that a mesh axis runs over, the one named last changes fastest.
Arguments:
- tokens: bfloat16 [8192, 8192], P('group', 'tp'), may hold values from -6 to 6
- norm_gain: bfloat16 [1, 8192], P(None, 'tp'), may hold values from 0.5 to 1.5
- query_weight: bfloat16 [8192, 8192], P(None, 'tp'), may hold values from -0.0625 to 0.0625
- kv_weight: bfloat16 [8192, 2048], P(None, 'tp'), may hold values from -0.0625 to 0.0625
- out_weight: bfloat16 [8192, 8192], P('tp'), may hold values from -0.0625 to 0.0625
- prefix_cache: bfloat16 [8192, 2048], P('group', 'tp'), may hold values from -456 to 456
- prompt_len: int32 [8], P('group'), may hold values from 512 to 1024, as said below
- page_owner: int32 [2048, 1], P('group'), may hold values from 0 to 127; in each aligned block of 256 rows (0 to 255, 256 to 511, ...) at most 3 rows name the same one
- page_seq: int32 [2048], P('group'), may hold values from 0 to 7
- dec_queries: bfloat16 [64, 8192], P('group'), may hold values from -6 to 6
- dec_cache: bfloat16 [64, 2048, 2048], P('group', 'tp'), may hold values from -456 to 456
- dec_len: int32 [64], P('group'), may hold values from 1 to 2048, as said below
Outputs:
- hidden_out: bfloat16 [8192, 8192], P('group', 'tp')
- dec_out: bfloat16 [64, 8192], P('group')
Inputs may be any that keep to these rules, and one draw needn't show every extreme that they name: `page_owner`: in the 256 rows of one group no owner is named more than 3 times. `prompt_len`: some group's block is fully live. `dec_len`: some decode sequence uses every position.
All inputs are finite; a program needn't handle non-finite values.
Results may differ from a plain program's by a relative error of at most 0.011.
Values may be sent and summed in bfloat16 or wider, within the bound.
A program may use at most 192 MiB of HBM per device.

v0:
```python
import math

import jax
import jax.numpy as jnp
from jax import lax
from jax.sharding import PartitionSpec as P

HEADS = 64
KVH = 8
HD = 128
PAGE = 4


EPSILON = 1e-05
NEG_BIG = -1e30


def from_partner(block, axis, apart):
    count = lax.axis_size(axis)
    route = []
    for low in range(count):
        high = low | 1 << apart
        if high != low and high < count:
            route += [(low, high), (high, low)]
    return lax.ppermute(block, axis, route)


def combined_all(value, axis, combine):
    everything = jax.tree.map(lambda part: lax.all_gather(part, axis), value)
    first = jax.tree.map(lambda part: part[0], everything)

    def turn(k, so_far):
        return combine(so_far, jax.tree.map(lambda part: part[k], everything))

    return lax.fori_loop(1, lax.axis_size(axis), turn, first)


def normalize(rows, gain):
    wide = rows.astype(jnp.float32)
    power = jnp.sum(wide * wide, axis=-1, keepdims=True) / wide.shape[-1]
    return (wide * lax.rsqrt(power + EPSILON) * gain.astype(jnp.float32)).astype(jnp.bfloat16)


def block_attention(queries, key_rows, value_rows):
    count = queries.shape[0]
    total = key_rows.shape[0]
    factor = 1.0 / math.sqrt(queries.shape[-1])
    scores = (
        jnp.einsum("cgd,jd->gcj", queries, key_rows, preferred_element_type=jnp.float32) * factor
    )
    row_index = lax.broadcasted_iota(jnp.int32, (count, total), 0)
    column_index = lax.broadcasted_iota(jnp.int32, (count, total), 1)
    allowed = column_index <= row_index + (total - count)
    scores = jnp.where(allowed[None], scores, NEG_BIG)
    top_score = jnp.max(scores, axis=-1, keepdims=True)
    expo = jnp.exp(scores - top_score)
    weights = (expo / jnp.sum(expo, axis=-1, keepdims=True)).astype(jnp.bfloat16)
    return jnp.einsum(
        "gcj,jd->cgd", weights, value_rows, preferred_element_type=jnp.float32
    ).astype(jnp.bfloat16)


def shard_partial(queries, old_rows, old_valid, new_rows, new_valid):
    seqs = queries.shape[0]
    head_dim = queries.shape[-1] // HEADS
    factor = 1.0 / math.sqrt(head_dim)
    grouped = queries.reshape(seqs, KVH, HEADS // KVH, head_dim)
    old_split = old_rows.reshape(seqs, old_rows.shape[1], KVH, 2, head_dim)
    new_split = new_rows.reshape(new_rows.shape[0], KVH, 2, head_dim)
    old_scores = (
        jnp.einsum(
            "skgd,sjkd->skgj", grouped, old_split[:, :, :, 0], preferred_element_type=jnp.float32
        )
        * factor
    )
    new_scores = (
        jnp.einsum(
            "skgd,jkd->skgj", grouped, new_split[:, :, 0], preferred_element_type=jnp.float32
        )
        * factor
    )
    old_mask = old_valid[:, None, None, :]
    new_mask = new_valid[:, None, None, :]
    old_scores = jnp.where(old_mask, old_scores, NEG_BIG)
    new_scores = jnp.where(new_mask, new_scores, NEG_BIG)
    top_score = jnp.maximum(jnp.max(old_scores, axis=-1), jnp.max(new_scores, axis=-1))
    old_expo = jnp.where(old_mask, jnp.exp(old_scores - top_score[..., None]), 0.0)
    new_expo = jnp.where(new_mask, jnp.exp(new_scores - top_score[..., None]), 0.0)
    total = jnp.sum(old_expo, axis=-1) + jnp.sum(new_expo, axis=-1)
    accum = jnp.einsum(
        "skgj,sjkd->skgd",
        old_expo.astype(jnp.bfloat16),
        old_split[:, :, :, 1],
        preferred_element_type=jnp.float32,
    )
    accum = accum + jnp.einsum(
        "skgj,jkd->skgd",
        new_expo.astype(jnp.bfloat16),
        new_split[:, :, 1],
        preferred_element_type=jnp.float32,
    )
    return (top_score, total, accum)


def combine_softmax(first, second):
    best = jnp.maximum(first[0], second[0])
    scale_first = jnp.exp(first[0] - best)
    scale_second = jnp.exp(second[0] - best)
    total = first[1] * scale_first + second[1] * scale_second
    accum = first[2] * scale_first[..., None] + second[2] * scale_second[..., None]
    return (best, total, accum)


def per_device(
    tokens,
    norm_gain,
    query_weight,
    kv_weight,
    out_weight,
    prefix_cache,
    prompt_len,
    page_owner,
    page_seq,
    dec_queries,
    dec_cache,
    dec_len,
):
    group_count = lax.axis_size("group")
    shard_count = lax.axis_size("tp")
    device_count = group_count * shard_count
    shard_index = lax.axis_index("tp")
    span_rows = tokens.shape[0]
    kv_width = kv_weight.shape[1]
    head_cols = query_weight.shape[1]
    page_count = span_rows // PAGE
    capacity = max(2, 3 * page_count // (2 * device_count))
    whole, gain_whole = (
        lax.all_gather(tokens, "tp", axis=1, tiled=True),
        lax.all_gather(norm_gain, "tp", axis=1, tiled=True),
    )
    normed = normalize(whole, gain_whole[0])
    queries = jnp.dot(normed, query_weight, preferred_element_type=jnp.float32).astype(jnp.bfloat16)
    kv_own = jnp.dot(normed, kv_weight, preferred_element_type=jnp.float32).astype(jnp.bfloat16)
    local_rows = jnp.concatenate([prefix_cache, kv_own], 0)
    partner = from_partner(local_rows, "tp", 0)
    even_shard = shard_index % 2 == 0
    both = jnp.where(
        even_shard,
        jnp.concatenate([local_rows, partner], 1),
        jnp.concatenate([partner, local_rows], 1),
    )
    heads_here = head_cols // HD
    attended = block_attention(
        queries.reshape(span_rows, heads_here, HD), both[:, :HD], both[:, HD:]
    )
    attended_flat = attended.reshape(span_rows, head_cols)
    term = jnp.dot(attended_flat, out_weight, preferred_element_type=jnp.float32)
    projected = lax.psum_scatter(
        term.astype(jnp.bfloat16), "tp", scatter_dimension=1, tiled=True
    ).astype(jnp.float32)
    hidden_out = (tokens.astype(jnp.float32) + projected).astype(jnp.bfloat16)
    pages = kv_own.reshape(page_count, PAGE, kv_width)
    owner = page_owner[:, 0]
    onehot = (owner[:, None] == jnp.arange(device_count, dtype=jnp.int32)[None, :]).astype(
        jnp.int32
    )
    slot = jnp.sum((jnp.cumsum(onehot, axis=0) - onehot) * onehot, axis=1)
    starts = jnp.arange(page_count, dtype=jnp.int32) * PAGE
    live = starts < prompt_len[0]
    target = jnp.where(live, owner, device_count)
    buffer = (
        jnp.zeros((device_count, capacity, PAGE, kv_width), jnp.bfloat16)
        .at[target, slot]
        .set(pages, mode="drop")
    )
    meta_rows = jnp.stack(
        [
            page_seq.astype(jnp.float32),
            jnp.minimum(PAGE, prompt_len[0] - starts).astype(jnp.float32),
        ],
        -1,
    ).astype(jnp.bfloat16)
    meta = jnp.zeros((device_count, capacity, 2), jnp.bfloat16).at[:, :, 0].set(-1.0)
    meta = meta.at[target, slot].set(meta_rows, mode="drop")
    arrived = lax.all_to_all(buffer, ("group", "tp"), split_axis=0, concat_axis=0, tiled=True)
    arrived_meta = lax.all_to_all(meta, ("group", "tp"), split_axis=0, concat_axis=0, tiled=True)
    region = arrived.reshape(group_count, shard_count, capacity, PAGE, kv_width).transpose(
        0, 2, 3, 1, 4
    )
    region = region.reshape(group_count * capacity * PAGE, shard_count * kv_width)
    meta_source = arrived_meta.reshape(group_count, shard_count, capacity, 2)[:, 0].astype(
        jnp.float32
    )
    region, fresh_seq, fresh_count = (
        region,
        meta_source[..., 0].astype(jnp.int32),
        meta_source[..., 1].astype(jnp.int32),
    )
    fresh_rows = region.shape[0]
    position = jnp.arange(PAGE, dtype=jnp.int32)
    token_seq = jnp.broadcast_to(fresh_seq[..., None], fresh_seq.shape + (PAGE,)).reshape(
        fresh_rows
    )
    token_live = (position[None, None, :] < fresh_count[..., None]).reshape(fresh_rows)
    dec_seqs = dec_queries.shape[0]
    ctx_rows = dec_cache.shape[1]
    seq_ids = jnp.arange(dec_seqs, dtype=jnp.int32)
    old_pos = shard_index * ctx_rows + jnp.arange(ctx_rows, dtype=jnp.int32)
    old_valid = old_pos[None, :] < dec_len[:, None]
    new_valid = (token_seq[None, :] == seq_ids[:, None]) & token_live[None, :]
    partial_value = shard_partial(dec_queries, dec_cache, old_valid, region, new_valid)
    best, total, accum = combined_all(partial_value, "tp", combine_softmax)
    dec_out = (accum / total[..., None]).reshape(dec_seqs, HEADS * HD).astype(jnp.bfloat16)
    return (hidden_out, dec_out)


def solution(mesh):
    return jax.shard_map(
        per_device,
        mesh=mesh,
        in_specs=(
            P("group", "tp"),
            P(None, "tp"),
            P(None, "tp"),
            P(None, "tp"),
            P("tp", None),
            P("group", "tp"),
            P("group"),
            P("group", None),
            P("group"),
            P("group", None),
            P("group", "tp", None),
            P("group"),
        ),
        out_specs=(P("group", "tp"), P("group", None)),
        check_vma=False,
    )
```

profile of v0, /device:TPU:0, one launch (start us, length us, event | category | flops | bytes accessed | tf_op | source)
XLA Modules:
  0.0 422.9 jit_solution(5149928045129132867)
XLA Ops:
  7.3 0.7 all-gather.6.cloned.1.call-update
  8.6 0.7 convert_convert_fusion.1
  9.5 0.8 copy.113
  10.5 0.9 copy.179
  11.4 0.9 fusion.40
  12.3 0.7 or_select_fusion
  13.0 12.5 %scatter_fusion = bf16[128,3,2]{2,0,1:T(8,128)(2,1)S(1)} fusion(bf16[128,3,2]{2,0,1:T(8,128)(2,1)S(1)} %copy.179, s32[256]{0:T(256)S(1)} %bitcast.134, bf16[256,2]{1,0:T(8,128)(2,1)S(1)} %copy.115), kind=kCustom, calls=%fused_computation | custom fusion | bytes 5120 | tf_op jit(solution)/shard_map/scatter | solution.py:184
  25.6 1.5 copy.116
  27.1 11.1 %all-to-all-start = ((bf16[128,3,2]{1,2,0:T(2,128)(2,1)}), bf16[128,3,2]{1,2,0:T(2,128)(2,1)S(1)}, u32[]{:S(2)}, u32[]{:S(2)}) async-start(bf16[128,3,2]{1,2,0:T(2,128)(2,1)} %copy.116), calls=%async_computation.1 | async-start | bytes 131072 | tf_op jit(solution)/shard_map/all_to_all | solution.py:186
  38.2 6.5 %copy.110 = bf16[8,128,2048]{1,2,0:T(8,128)(2,1)} copy(bf16[8,128,2048]{2,1,0:T(8,128)(2,1)} %param.26) | data formatting | bytes 8388608 | tf_op args[10]
  44.7 2.3 fusion.58
  47.0 3.1 iota_compare_fusion
  50.1 24.5 %all_gather.21 = bf16[1,8192]{1,0:T(2,128)(2,1)S(1)} all-gather(bf16[1,512]{1,0:T(2,128)(2,1)S(1)} %copy-done.8), channel_id=1, replica_groups=mesh['group'=8,'tp'=16] {'tp'}, dimensions={1}, use_global_device_ids=true | all-gather | bytes 17408 | tf_op jit(solution)/shard_map/all_gather | solution.py:139
  75.4 57.4 %all-gather.6.cloned.1.call-done = bf16[1024,8192]{1,0:T(8,128)(2,1)} async-done(((bf16[1024,512]{1,0:T(8,128)(2,1)}), bf16[1024,8192]{1,0:T(8,128)(2,1)}) %all-gather.6.cloned.1.call-update) | async-done | bytes 16777232 | tf_op jit(solution)/shard_map/all_gather | solution.py:138
  132.8 7.2 %fusion.4 = f32[1024]{0:T(1024)S(1)} fusion(bf16[1024,8192]{1,0:T(8,128)(2,1)} %all-gather.6.cloned.1.call-done), kind=kLoop, calls=%fused_computation.13 | loop fusion | flops 25164800 | bytes 16781312 | tf_op jit(solution)/shard_map/reduce_sum | solution.py:40
  140.0 10.4 %fusion.24 = bf16[1024,128]{1,0:T(8,128)(2,1)S(1)} fusion(bf16[8192,128]{1,0:T(8,128)(2,1)S(1)} %copy-done, bf16[1024,8192]{1,0:T(8,128)(2,1)} %all-gather.6.cloned.1.call-done, f32[8192]{0:T(1024)S(1)} %bitcast.150, f32[1024]{0:T(1024)S(1)} %add_rsqrt_fusion), kind=kOutput, calls=%fused_computation.36 | convolution fusion | flops 2181169152 | bytes 19173376 | tf_op jit(solution)/shard_map/dot_general | solution.py:143
  150.4 0.9 broadcast_in_dim.99
  151.3 28.8 %scatter_fusion.1 = bf16[128,3,4,128]{3,2,1,0:T(4,128)(2,1)} fusion(bf16[128,3,4,128]{3,2,1,0:T(4,128)(2,1)} %broadcast_in_dim.99, s32[256]{0:T(256)S(1)} %bitcast.135, bf16[256,4,128]{2,1,0:T(4,128)(2,1)S(1)} %bitcast.139), kind=kCustom, calls=%fused_computation.1 | custom fusion | bytes 788480 | tf_op jit(solution)/shard_map/scatter | solution.py:174
  180.1 6.1 %all-to-all-start.1 = ((bf16[128,3,4,128]{3,2,1,0:T(4,128)(2,1)}), bf16[128,3,4,128]{3,2,1,0:T(4,128)(2,1)S(1)}, u32[]{:S(2)}, u32[]{:S(2)}) async-start(bf16[128,3,4,128]{3,2,1,0:T(4,128)(2,1)} %scatter_fusion.1), calls=%async_computation.2 | async-start | bytes 786432 | tf_op jit(solution)/shard_map/all_to_all | solution.py:185
  186.4 16.1 %fusion.20 = bf16[1024,512]{0,1:T(8,128)(2,1)} fusion(bf16[8192,512]{1,0:T(8,128)(2,1)} %param.18, bf16[1024,8192]{1,0:T(8,128)(2,1)} %all-gather.6.cloned.1.call-done, f32[8192]{0:T(1024)S(1)} %bitcast.151, f32[1024]{0:T(1024)S(1)} %add_rsqrt_fusion), kind=kOutput, calls=%fused_computation.34 | convolution fusion | flops 8624013312 | bytes 26251264 | tf_op jit(solution)/shard_map/dot_general | solution.py:142
  202.6 0.5 fusion.56
  204.0 3.6 fusion.29
  208.2 19.7 %fusion.57 = (f32[4,1024]{1,0:T(4,128)S(1)}, f32[4,1024,2048]{1,2,0:T(8,128)}) fusion(pred[1024,2048]{0,1:T(8,128)(4,1)} %iota_compare_fusion, bf16[1024,4,128]{0,2,1:T(8,128)(2,1)} %bitcast.158, bf16[2048,256]{1,0:T(8,128)(2,1)S(1)} %maximum_select_fusion), kind=kOutput, calls=%fused_computation.103 | convolution fusion | flops 2181040128 | bytes 37240832 | tf_op jit(solution)/shard_map/sub | solution.py:56
  227.9 12.2 %fusion.23 = bf16[128,4,1024]{2,0,1:T(8,128)(2,1)S(1)} fusion(f32[4,1024,2048]{1,2,0:T(8,128)} %get-tuple-element.218, f32[4,1024]{1,0:T(4,128)S(1)} %get-tuple-element.217, bf16[2048,256]{1,0:T(8,128)(2,1)S(1)} %maximum_select_fusion), kind=kOutput, calls=%fused_computation.35 | convolution fusion | flops 2164785152 | bytes 35143680 | tf_op jit(solution)/shard_map/gcj,jd->cgd/dot_general | solution.py:58
  240.1 16.5 %convolution_convert_fusion = bf16[1024,8192]{1,0:T(8,128)(2,1)} fusion(bf16[1024,512]{0,1:T(8,128)(2,1)S(1)} %bitcast.159, bf16[512,8192]{1,0:T(8,128)(2,1)} %param.20), kind=kOutput, calls=%fused_computation.24 | convolution fusion | flops 8598323200 | bytes 26214400 | tf_op jit(solution)/shard_map/dot_general | solution.py:157
  257.0 25.9 %all-gather.1 = f32[128,8,8]{2,1,0:T(8,128)S(1)} all-gather(f32[8,8,8]{2,1,0:T(8,128)S(1)} %copy_add_fusion), channel_id=3, replica_groups=mesh['group'=8,'tp'=16] {'tp'}, dimensions={0}, use_global_device_ids=true | all-gather | bytes 34816 | tf_op jit(solution)/shard_map/all_gather | solution.py:29
  282.8 0.8 copy-done.4
  283.6 20.7 %all-gather = f32[128,8,8]{2,1,0:T(8,128)S(1)} all-gather(f32[8,8,8]{2,1,0:T(8,128)S(1)} %copy_maximum_fusion), channel_id=2, replica_groups=mesh['group'=8,'tp'=16] {'tp'}, dimensions={0}, use_global_device_ids=true | all-gather | bytes 34816 | tf_op jit(solution)/shard_map/all_gather | solution.py:29
  304.3 0.8 copy-done.5
  305.1 1.0 slice.94
  306.1 30.9 %while.20 = (s32[]{:T(128)}, f32[8,8,8]{2,1,0:T(8,128)S(1)}, f32[8,8,8]{2,1,0:T(8,128)S(1)}, f32[8,8,8,128]{3,2,1,0:T(8,128)S(1)}, f32[16,8,8,8]{3,2,1,0:T(8,128...) while((s32[]{:T(128)}, f32[8,8,8]{2,1,0:T(8,128)S(1)}, ...), condition=%wide.region_14.15_spmd, body=%wide.region_13.14_spmd.sunk | while | flops 199685 | bytes 807055 | solution.py:35
  306.1 0.8 fusion.68
  306.9 1.2 fusion.69
  308.2 0.8 fusion.68
  309.0 1.2 fusion.69
  310.2 0.8 fusion.68
  311.1 1.2 fusion.69
  312.3 0.8 fusion.68
  313.1 1.2 fusion.69
  314.4 0.8 fusion.68
  315.2 1.2 fusion.69
  316.4 0.8 fusion.68
  317.2 1.2 fusion.69
  318.5 0.8 fusion.68
  319.3 1.2 fusion.69
  320.5 0.8 fusion.68
  321.3 1.2 fusion.69
  322.6 0.8 fusion.68
  323.4 1.2 fusion.69
  324.6 0.8 fusion.68
  325.5 1.2 fusion.69
  326.7 0.8 fusion.68
  327.5 1.2 fusion.69
  328.8 0.8 fusion.68
  329.6 1.2 fusion.69
  330.8 0.8 fusion.68
  331.6 1.2 fusion.69
  332.9 0.8 fusion.68
  333.7 1.2 fusion.69
  335.0 0.8 fusion.68
  335.8 1.2 fusion.69
  337.2 0.7 copy.162
  337.9 75.9 %reduce-scatter.2.cloned.1.call-done = bf16[1024,512]{1,0:T(8,128)(2,1)} async-done(((bf16[1024,8192]{1,0:T(8,128)(2,1)}), bf16[1024,512]{1,0:T(8,128)(2,1)}) %reduce-scatter.2.cloned.1.call-update) | async-done | bytes 1048592 | tf_op jit(solution)/shard_map/reduce_scatter | solution.py:158
  413.8 2.5 add_convert_fusion
  (69 shorter events, 3.5 us)
Async XLA Ops:
  7.2 132.8 %copy-start = (bf16[8192,128]{1,0:T(8,128)(2,1)S(1)}, bf16[8192,128]{1,0:T(8,128)(2,1)}, u32[]{:S(2)}) copy-start(bf16[8192,128]{1,0:T(8,128)(2,1)} %param.19) | copy-start | bytes 6291460
  7.2 37.5 %copy-start.9 = (s32[8]{0:T(128)S(1)}, s32[8]{0:T(128)}, u32[]{:S(2)}) copy-start(s32[8]{0:T(128)} %param.27) | copy-start | bytes 100
  7.2 37.5 %copy-start.6 = (bf16[8,8192]{1,0:T(8,128)(2,1)S(1)}, bf16[8,8192]{1,0:T(8,128)(2,1)}, u32[]{:S(2)}) copy-start(bf16[8,8192]{1,0:T(8,128)(2,1)} %param.25) | copy-start | bytes 393220
  7.2 42.9 %copy-start.8 = (bf16[1,512]{1,0:T(2,128)(2,1)S(1)}, bf16[1,512]{1,0:T(2,128)(2,1)}, u32[]{:S(2)}) copy-start(bf16[1,512]{1,0:T(2,128)(2,1)} %param.17) | copy-start | bytes 3076
  7.2 125.6 %all-gather.6.cloned.1.call-start = ((), (), s32[]{:S(2)}) async-start(), calls=%async_computation.3 | async-start | bytes 17825792 | tf_op jit(solution)/shard_map/all_gather | solution.py:138
  27.1 47.6 %all-to-all-start = ((bf16[128,3,2]{1,2,0:T(2,128)(2,1)}), bf16[128,3,2]{1,2,0:T(2,128)(2,1)S(1)}, u32[]{:S(2)}, u32[]{:S(2)}) async-start(bf16[128,3,2]{1,2,0:T(2,128)(2,1)} %copy.116), calls=%async_computation.1 | async-start | bytes 131072 | tf_op jit(solution)/shard_map/all_to_all | solution.py:186
  140.0 46.2 %copy-start.3 = (bf16[1024,128]{1,0:T(8,128)(2,1)S(1)}, bf16[1024,128]{1,0:T(8,128)(2,1)}, u32[]{:S(2)}) copy-start(bf16[1024,128]{1,0:T(8,128)(2,1)} %param.21) | copy-start | bytes 786436
  180.1 22.4 %all-to-all-start.1 = ((bf16[128,3,4,128]{3,2,1,0:T(4,128)(2,1)}), bf16[128,3,4,128]{3,2,1,0:T(4,128)(2,1)S(1)}, u32[]{:S(2)}, u32[]{:S(2)}) async-start(bf16[128,3,4,128]{3,2,1,0:T(4,128)(2,1)} %scatter_fusion.1), calls=%async_computation.2 | async-start | bytes 786432 | tf_op jit(solution)/shard_map/all_to_all | solution.py:185
  186.1 119.0 %all-gather.8.cloned.1.call-start = ((), (), s32[]{:S(2)}) async-start(), calls=%async_computation.5 | async-start | bytes 4456448 | tf_op jit(solution)/shard_map/all_gather | solution.py:29
  186.3 16.9 %copy-start.7 = (bf16[8,8192]{1,0:T(8,128)(2,1)S(1)}, bf16[8,8192]{1,0:T(8,128)(2,1)}, u32[]{:S(2)}) copy-start(bf16[8,8192]{1,0:T(8,128)(2,1)} %param.25) | copy-start | bytes 393220
  186.3 21.6 %collective-permute-start = (bf16[2048,128]{1,0:T(8,128)(2,1)S(1)}, bf16[2048,128]{1,0:T(8,128)(2,1)S(1)}, u32[]{:S(2)}, u32[]{:S(2)}) collective-permute-start(bf16[2048,128]{1,0:T(8,128)(2,1)S(1)} %pad_maximum_fusion), channel_id=1, source_target_pairs={{0,1},{1,0},{2,3},{3,2},{4,5},{5,4},{6,7},{7,6},{8,9},{9,8},{10,11... | collective-permute-start | bytes 1572872 | tf_op jit(solution)/shard_map/ppermute | solution.py:25
  207.6 206.3 %reduce-scatter.2.cloned.1.call-start = ((), (), s32[]{:S(2)}) async-start(), calls=%async_computation.4 | async-start | bytes 17825792 | tf_op jit(solution)/shard_map/reduce_scatter | solution.py:158
  256.6 157.2 %copy-start.2 = (bf16[1024,512]{1,0:T(8,128)(2,1)S(1)}, bf16[1024,512]{1,0:T(8,128)(2,1)}, u32[]{:S(2)}) copy-start(bf16[1024,512]{1,0:T(8,128)(2,1)} %param.16) | copy-start | bytes 3145732
  256.6 159.7 %copy-start.1 = (bf16[8192,128]{1,0:T(8,128)(2,1)S(1)}, bf16[8192,128]{1,0:T(8,128)(2,1)}, u32[]{:S(2)}) copy-start(bf16[8192,128]{1,0:T(8,128)(2,1)} %param.19) | copy-start | bytes 6291460
  282.8 0.8 copy-start.4
  304.3 0.8 copy-start.5
Sparse Core Ops, SparseCore 0:
  10.3 122.4 all-gather.5
  207.7 56.7 all-gather.7
  268.8 145.0 reduce-scatter.1
where the time goes:
time: 425 us; the launch traced here: 423 us
  waiting for transfers between devices  134 us (32%)
  matrix products  81.3 us (19%)
  blocking collectives  71.1 us (17%)
  local copies, waits for them, and re-layouts  56.6 us (13%)
  other arithmetic  47.2 us (11%)
  starting transfers between devices  17.6 us (4%)
  between operations  14.7 us (3%)
    reduce_scatter x1, waiting for transfers between devices, per_device(): lax.psum_scatter(term.astype(jnp.bfloat16), 'tp', scatter_dimension=1, ti...  75.9 us
    all_gather x1, waiting for transfers between devices, per_device(): lax.all_gather(tokens, 'tp', axis=1, tiled=True)  57.4 us
    all_gather x2, blocking collectives, combined_all(): everything = jax.tree.map(lambda part: lax.all_gather(part, axis), value)  46.6 us
    scatter x1, local copies, waits for them, and re-layouts, per_device(): buffer = jnp.zeros((device_count, capacity, PAGE, kv_width), jnp.bfloat16...  28.8 us
    all_gather x1, blocking collectives, per_device(): lax.all_gather(norm_gain, 'tp', axis=1, tiled=True)  24.5 us
    sub x1, matrix products, block_attention(): expo = jnp.exp(scores - top_score)  19.7 us
    add x15, other arithmetic, combine_softmax(): first[2] * scale_first[..., None] + second[2] * scale_second[..., None]  18.3 us
    dot_general x1, matrix products, per_device(): jnp.dot(attended_flat, out_weight, preferred_element_type=jnp.float32)  16.5 us
  transfers between devices with their start and end apart: 6, of which 2 were waited for; matrix products, arithmetic and copies ran while one was open for 32% of the time, Pallas kernels for 0%

commit v1 on v0

v1 whole, which is shorter than its diff:
```python
import math

import jax
import jax.numpy as jnp
from jax import lax
from jax.experimental import pallas as pl
from jax.experimental.pallas import tpu as pltpu
from jax.sharding import PartitionSpec as P

HEADS = 64
KVH = 8
HD = 128
PAGE = 4


EPSILON = 1e-05
NEG_BIG = -1e30


MESH = pl.DeviceIdType.MESH
BF = jnp.bfloat16
F32 = jnp.float32
MIB = 1024 * 1024
SIDES = 2
RING = 4


def here():
    t = lax.axis_index("tp")
    return t // (RING * 2), lax.rem(t // 2, RING), lax.rem(t, 2)


def shard_at(side, ring, core, far, step, other):
    s = lax.rem(side + far, SIDES)
    r = lax.rem(ring + step, RING)
    c = lax.rem(core + other, 2)
    return (s * RING + r) * 2 + c


def push(src, dst, send_sem, recv_sem, to):
    copy = pltpu.make_async_remote_copy(
        src_ref=src,
        dst_ref=dst,
        send_sem=send_sem,
        recv_sem=recv_sem,
        device_id={"tp": to},
        device_id_type=MESH,
    )
    copy.start()
    return copy


def landed(ref, recv_sem, to):
    pltpu.make_async_remote_copy(
        src_ref=ref,
        dst_ref=ref,
        send_sem=recv_sem,
        recv_sem=recv_sem,
        device_id={"tp": to},
        device_id_type=MESH,
    ).wait_recv()


def greet(peers):
    barrier = pltpu.get_barrier_semaphore()
    for peer in peers:
        pl.semaphore_signal(barrier, inc=1, device_id={"tp": peer}, device_id_type=MESH)
    pl.semaphore_wait(barrier, len(peers))


GATHER_CHUNKS = 4
GAIN_ROWS = 16


def gather_kernel(
    tok,
    gain,
    prefix,
    qw_hbm,
    kw_hbm,
    q_out,
    kv_out,
    xall,
    qw,
    kw,
    acc_q,
    acc_k,
    power,
    w_sem,
    recv_sem,
    sib_sem,
    x_send,
    up_send,
    down_send,
    sib_send,
    kv_send,
    kv_recv,
):
    side, ring, core = here()
    rows_all, width = tok.shape
    chunk = rows_all // GATHER_CHUNKS

    def at(far, step, other=0):
        return shard_at(side, ring, core, far, step, other)

    me, across, sib = at(0, 0), at(1, 0), at(0, 0, 1)
    up, down = at(0, 1), at(0, 3)

    load_q = pltpu.make_async_copy(qw_hbm, qw, w_sem.at[0])
    load_k = pltpu.make_async_copy(kw_hbm, kw, w_sem.at[1])
    load_q.start()
    load_k.start()
    xall[me, pl.ds(0, GAIN_ROWS), :] = jnp.broadcast_to(gain[...], (GAIN_ROWS, width))
    xall[me, pl.ds(GAIN_ROWS, rows_all), :] = tok[...]
    prefix_rows = prefix.shape[0]
    kv_out[core, pl.ds(0, prefix_rows), :] = prefix[...]
    acc_q[...] = jnp.zeros_like(acc_q)
    acc_k[...] = jnp.zeros_like(acc_k)
    power[...] = jnp.zeros_like(power)
    greet((across, up, down, sib))

    sends = []

    def span(i, half=None):
        low = 0 if i == 0 else GAIN_ROWS + i * chunk
        high = GAIN_ROWS + (i + 1) * chunk
        middle = high - chunk // 2
        if half == 0:
            high = middle
        if half == 1:
            low = middle
        return pl.ds(low, high - low)

    def send(slot, rows, send_sem, there_sem, to):
        ref = xall.at[slot, rows, :]
        sends.append(push(ref, ref, send_sem, there_sem, to))

    def to_sibling(far, step, i):
        kind = far * 4 + step
        send(at(far, step), span(i), sib_send.at[kind, i], sib_sem.at[kind, i], sib)

    def multiply(slot, i):
        rows = pl.ds(i * chunk, chunk)
        wide = xall[slot, pl.ds(GAIN_ROWS + i * chunk, chunk), :].astype(F32)
        weight = xall[slot, pl.ds(0, 1), :].astype(F32)
        square = wide * wide
        part = square[:, 0:HD]
        for k in range(1, width // HD):
            part = part + square[:, k * HD : (k + 1) * HD]
        power[rows, :] += part
        scaled = (wide * weight).astype(BF)
        depth = pl.ds(pl.multiple_of(slot * width, width), width)
        acc_q[rows, :] += jnp.dot(scaled, qw[depth, :], preferred_element_type=F32)
        acc_k[rows, :] += jnp.dot(scaled, kw[depth, :], preferred_element_type=F32)

    def from_sibling(far, step, i):
        kind = far * 4 + step
        slot = at(far, step, 1)
        landed(xall.at[slot, span(i), :], sib_sem.at[kind, i], sib)
        multiply(slot, i)

    def got(far, step, i):
        kind = far * 4 + step
        slot = at(far, step)
        if step == 2:
            landed(xall.at[slot, span(i, 0), :], recv_sem.at[kind, i], down)
            landed(xall.at[slot, span(i, 1), :], recv_sem.at[8 + far, i], up)
        else:
            landed(xall.at[slot, span(i), :], recv_sem.at[kind, i], up)

    for i in range(GATHER_CHUNKS):
        send(me, span(i), x_send.at[i], recv_sem.at[4, i], across)
        send(me, span(i), up_send.at[0, i], recv_sem.at[3, i], up)
        send(me, span(i), down_send.at[0, i], recv_sem.at[1, i], down)
        to_sibling(0, 0, i)
    early = kv_out.at[core, pl.ds(0, prefix_rows), :]
    sends.append(push(early, early, kv_send.at[0], kv_recv.at[0], sib))
    load_q.wait()
    load_k.wait()

    def event(name, i):
        if name == "O":
            multiply(me, i)
            return [(0, 0, i)]
        if name == "X":
            got(1, 0, i)
            send(across, span(i), up_send.at[1, i], recv_sem.at[7, i], up)
            send(across, span(i), down_send.at[1, i], recv_sem.at[5, i], down)
            to_sibling(1, 0, i)
            multiply(across, i)
            return [(1, 0, i)]
        far = 0 if name in ("Z", "F") else 1
        if name in ("Z", "P"):
            got(far, 3, i)
            send(at(far, 3), span(i, 0), up_send.at[2 + far, i], recv_sem.at[4 * far + 2, i], up)
            got(far, 1, i)
            send(at(far, 1), span(i, 1), down_send.at[2 + far, i], recv_sem.at[8 + far, i], down)
            to_sibling(far, 3, i)
            to_sibling(far, 1, i)
            multiply(at(far, 3), i)
            multiply(at(far, 1), i)
            return [(far, 3, i), (far, 1, i)]
        got(far, 2, i)
        to_sibling(far, 2, i)
        multiply(at(far, 2), i)
        return [(far, 2, i)]

    order = (
        ("O", 0), ("O", 1), ("O", 2), ("O", 3), ("Z", 0), ("Z", 1), ("X", 0), ("Z", 2),
        ("Z", 3), ("X", 1), ("F", 0), ("F", 1), ("P", 0), ("X", 2), ("F", 2), ("F", 3),
        ("P", 1), ("X", 3), ("P", 2), ("G", 0), ("P", 3), ("G", 1), ("G", 2), ("G", 3),
    )
    late = []
    for name, i in order:
        fresh = event(name, i)
        for item in late:
            from_sibling(*item)
        late = fresh
    for item in late:
        from_sibling(*item)

    for i in range(GATHER_CHUNKS):
        rows = pl.ds(i * chunk, chunk)
        total = jnp.sum(power[rows, :], axis=-1, keepdims=True) / (width * 2 * RING * SIDES)
        factor = lax.rsqrt(total + EPSILON)
        new = pl.ds(prefix_rows + i * chunk, chunk)
        kv_out[core, new, :] = (acc_k[rows, :] * factor).astype(BF)
        ref = kv_out.at[core, new, :]
        sends.append(push(ref, ref, kv_send.at[1 + i], kv_recv.at[1 + i], sib))
        q_out[rows, :] = (acc_q[rows, :] * factor).astype(BF)
    landed(kv_out.at[1 - core, pl.ds(0, prefix_rows), :], kv_recv.at[0], sib)
    for i in range(GATHER_CHUNKS):
        new = pl.ds(prefix_rows + i * chunk, chunk)
        landed(kv_out.at[1 - core, new, :], kv_recv.at[1 + i], sib)
    for copy in sends:
        copy.wait_send()


def gather_multiply(tokens, gain, prefix, query_weight, kv_weight):
    rows, width = tokens.shape
    shards = 2 * RING * SIDES
    kv_rows = prefix.shape[0] + rows
    vmem = pl.BlockSpec(memory_space=pltpu.VMEM)
    dma = pltpu.SemaphoreType.DMA
    n = GATHER_CHUNKS
    return pl.pallas_call(
        gather_kernel,
        out_shape=(
            jax.ShapeDtypeStruct((rows, query_weight.shape[1]), BF),
            jax.ShapeDtypeStruct((2, kv_rows, HD), BF),
        ),
        in_specs=[vmem, vmem, vmem, pl.BlockSpec(memory_space=pl.ANY), pl.BlockSpec(memory_space=pl.ANY)],
        out_specs=(vmem, vmem),
        scratch_shapes=[
            pltpu.VMEM((shards, rows + GAIN_ROWS, width), BF),
            pltpu.VMEM(query_weight.shape, BF),
            pltpu.VMEM(kv_weight.shape, BF),
            pltpu.VMEM((rows, query_weight.shape[1]), F32),
            pltpu.VMEM((rows, HD), F32),
            pltpu.VMEM((rows, HD), F32),
            dma((2,)),
            dma((10, n)),
            dma((8, n)),
            dma((n,)),
            dma((4, n)),
            dma((4, n)),
            dma((8, n)),
            dma((n + 1,)),
            dma((n + 1,)),
        ],
        compiler_params=pltpu.CompilerParams(
            collective_id=1, has_side_effects=True, vmem_limit_bytes=48 * MIB
        ),
        cost_estimate=pl.CostEstimate(
            flops=2 * rows * width * shards * (query_weight.shape[1] + HD),
            bytes_accessed=16 * MIB,
            transcendentals=0,
        ),
        name="gather_multiply",
    )(tokens, gain, prefix, query_weight, kv_weight)


SCATTER_CHUNKS = 8


def attend_kernel(
    tok,
    q,
    kv,
    pages,
    dec_q,
    dec_len,
    wo_hbm,
    cache_hbm,
    out,
    dec_out,
    wo,
    att,
    mine,
    lend,
    borrowed,
    mid,
    near,
    last,
    cache,
    first_stop,
    fresh,
    scores,
    partial,
    shares,
    w_sem,
    lend_send,
    lend_recv,
    mid_send,
    mid_recv,
    near_send,
    near_recv,
    last_send,
    last_recv,
    first_send,
    first_recv,
    fresh_send,
    fresh_recv,
    share_send,
    share_recv,
    done_send,
    done_recv,
):
    side, ring, core = here()
    rows_all, width = tok.shape
    chunk = rows_all // SCATTER_CHUNKS
    half = chunk // 2
    old = kv.shape[1] - rows_all
    n = SCATTER_CHUNKS

    def at(far, step, other=0):
        return shard_at(side, ring, core, far, step, other)

    across, sib, up, down = at(1, 0), at(0, 0, 1), at(0, 1), at(0, 3)
    load = pltpu.make_async_copy(wo_hbm, wo, w_sem.at[0])
    load.start()
    load_cache = pltpu.make_async_copy(cache_hbm, cache, w_sem.at[1])
    load_cache.start()
    shard = lax.axis_index("tp")
    group = lax.axis_index("group")
    shards = 2 * RING * SIDES
    groups = lax.axis_size("group")
    dec_seqs = cache.shape[0]
    barrier = pltpu.get_barrier_semaphore()

    def greet_shard(d, carry):
        pl.semaphore_signal(
            barrier, inc=1, device_id={"tp": lax.rem(shard + d, shards)}, device_id_type=MESH
        )
        return carry

    def greet_group(d, carry):
        pl.semaphore_signal(
            barrier, inc=1, device_id={"group": lax.rem(group + d, groups)}, device_id_type=MESH
        )
        return carry

    lax.fori_loop(1, shards, greet_shard, 0)
    lax.fori_loop(1, groups, greet_group, 0)
    pl.semaphore_wait(barrier, shards + groups - 2)

    def copy_to(src, dst, send_sem, recv_sem, to):
        return pltpu.make_async_remote_copy(
            src_ref=src,
            dst_ref=dst,
            send_sem=send_sem,
            recv_sem=recv_sem,
            device_id=to,
            device_id_type=MESH,
        )

    def first_copy(d):
        to = lax.rem(shard + d, shards)
        return copy_to(
            pages.at[to], first_stop.at[shard], first_send.at[d], first_recv.at[d], {"tp": to}
        )

    def fresh_copy(d):
        to = lax.rem(group + d, groups)
        return copy_to(
            first_stop.at[:, to], fresh.at[group], fresh_send.at[d], fresh_recv.at[d], {"group": to}
        )

    def share_of(shard_to):
        return partial.at[
            pl.ds(lax.rem(shard_to, 2) * 4, 5), pl.ds(pl.multiple_of(shard_to // 2 * 8, 8), 8), :
        ]

    def share_copy(d):
        to = lax.rem(shard + d, shards)
        return copy_to(
            share_of(to), shares.at[shard], share_send.at[d], share_recv.at[d], {"tp": to}
        )

    def result_of(of):
        return dec_out.at[of // 2, pl.ds(pl.multiple_of(lax.rem(of, 2) * 32, 32), 32), :]

    def done_copy(d):
        to = lax.rem(shard + d, shards)
        return copy_to(
            result_of(shard), result_of(shard), done_send.at[d], done_recv.at[d], {"tp": to}
        )

    def each(count, act):
        def body(d, carry):
            act(d)
            return carry

        lax.fori_loop(1, count, body, 0)

    def source(d, count, of):
        return lax.rem(of + count - d, count)

    def dec_begin():
        first_stop[shard] = pages[shard]
        each(shards, lambda d: first_copy(d).start())

    def dec_forward():
        def take(d):
            frm = source(d, shards, shard)
            ref = first_stop.at[frm]
            copy_to(ref, ref, first_send.at[d], first_recv.at[d], {"tp": frm}).wait_recv()

        each(shards, take)
        fresh[group] = first_stop[:, pl.ds(group, 1)].reshape(shards, 16, HD)
        each(groups, lambda d: fresh_copy(d).start())

    def dec_arrive():
        def take(d):
            frm = source(d, groups, group)
            ref = fresh.at[frm]
            copy_to(ref, ref, fresh_send.at[d], fresh_recv.at[d], {"group": frm}).wait_recv()

        each(groups, take)

    scale = math.log2(math.e) / math.sqrt(HD)
    contract = (((1,), (1,)), ((), ()))

    def head_cols(k, part):
        return pl.ds(pl.multiple_of(k * 2 * HD + part * HD, HD), HD)

    def dec_scores(k):
        ctx = cache.shape[1]
        position = lax.broadcasted_iota(jnp.int32, (8, ctx), 1) + shard * ctx
        for seq in range(dec_seqs):
            rows = pl.ds(seq * 8, 8)
            query = dec_q[k, rows, :].astype(BF)
            score = lax.dot_general(
                query, cache[seq, :, head_cols(k, 0)], contract, preferred_element_type=F32
            )
            scores[k, rows, :] = jnp.where(position < dec_len[seq], score * scale, NEG_BIG)

    def dec_settle(k):
        count = dec_seqs * 8
        spots = fresh.shape[0] * 16
        mark = fresh[0, 0].astype(F32)
        for g in range(1, fresh.shape[0]):
            mark = mark + fresh[g, 0].astype(F32)
        mark = mark[12:13, :]
        seq_of = lax.broadcasted_iota(jnp.int32, (count, spots), 0) // 8 + 1
        held = mark == seq_of.astype(F32)
        key = fresh[:, pl.ds(2 * k, 1)].reshape(spots, HD)
        value = fresh[:, pl.ds(2 * k + 1, 1)].reshape(spots, HD)
        new = lax.dot_general(dec_q[k].astype(BF), key, contract, preferred_element_type=F32)
        new = jnp.where(held, new * scale, NEG_BIG)
        old = scores[k]
        top = jnp.maximum(
            jnp.max(new, axis=-1, keepdims=True), jnp.max(old, axis=-1, keepdims=True)
        )
        new = jnp.where(held, jnp.exp2(new - top), 0.0)
        old = jnp.where(old > 0.5 * NEG_BIG, jnp.exp2(old - top), 0.0)
        total = jnp.sum(new, axis=-1, keepdims=True) + jnp.sum(old, axis=-1, keepdims=True)
        accum = jnp.dot(new.astype(BF), value, preferred_element_type=F32)
        place = k + k // 4
        for seq in range(dec_seqs):
            rows = slice(seq * 8, seq * 8 + 8)
            partial[place, pl.ds(seq * 8, 8), :] = accum[rows] + jnp.dot(
                old[rows].astype(BF), cache[seq, :, head_cols(k, 1)], preferred_element_type=F32
            )
        lane = lax.broadcasted_iota(jnp.int32, (count, HD), 1)
        stat = jnp.where(lax.rem(lane, 16) < 8, top, total)
        partial[4] = jnp.where(lane // 16 == k, stat, partial[4])

    def dec_share():
        shares[shard] = partial[
            pl.ds(core * 4, 5), pl.ds(pl.multiple_of(shard // 2 * 8, 8), 8), :
        ]
        each(shards, lambda d: share_copy(d).start())

    def dec_combine():
        def take(d):
            frm = source(d, shards, shard)
            ref = shares.at[frm]
            copy_to(ref, ref, share_send.at[d], share_recv.at[d], {"tp": frm}).wait_recv()

        each(shards, take)
        stat = shares[:, pl.ds(4 - 4 * core, 1)].reshape(shards, 8, HD)
        lane = lax.broadcasted_iota(jnp.int32, (shards, 8, HD), 2)
        parts = []
        for h in range(4):
            here_lane = lane // 16 == core * 4 + h
            low = lax.rem(lane, 16) < 8
            top = jnp.max(jnp.where(here_lane & low, stat, NEG_BIG), axis=-1, keepdims=True)
            total = jnp.max(
                jnp.where(here_lane & jnp.logical_not(low), stat, 0.0), axis=-1, keepdims=True
            )
            factor = jnp.exp2(top - jnp.max(top, axis=0, keepdims=True))
            whole = jnp.sum(factor * total, axis=0)
            accum = jnp.sum(
                factor * shares[:, pl.ds(core + h, 1)].reshape(shards, 8, HD), axis=0
            )
            parts.append(accum / whole)
        for pair in range(2):
            rows = pl.ds(pl.multiple_of(core * 32 + pair * 16, 16), 16)
            both = jnp.concatenate([parts[2 * pair], parts[2 * pair + 1]], axis=0)
            dec_out[shard // 2, rows, :] = both.astype(BF)
        each(shards, lambda d: done_copy(d).start())

    def dec_end():
        def take(d):
            frm = source(d, shards, shard)
            ref = result_of(frm)
            copy_to(ref, ref, done_send.at[d], done_recv.at[d], {"tp": frm}).wait_recv()

        each(shards, take)
        for copy in (first_copy, share_copy, done_copy):
            each(shards, lambda d, copy=copy: copy(d).wait_send())
        each(groups, lambda d: fresh_copy(d).wait_send())

    dec_begin()
    partial[4] = jnp.zeros_like(partial[4])
    load.wait()
    load_cache.wait()

    def rows_of(j):
        return pl.ds(pl.multiple_of(j * chunk, chunk), chunk)

    def half_of(j, k):
        return pl.ds(pl.multiple_of(j * chunk + k * half, half), half)

    def attention(j):
        rows = rows_of(j)
        row = lax.broadcasted_iota(jnp.int32, (chunk, rows_all), 0) + j * chunk
        column = lax.broadcasted_iota(jnp.int32, (chunk, rows_all), 1)
        seen = column <= row
        for h in range(width // HD):
            cols = pl.ds(h * HD, HD)
            query = q[rows, cols]
            first = lax.dot_general(
                query, kv[0, pl.ds(0, old), :], contract, preferred_element_type=F32
            )
            second = lax.dot_general(
                query, kv[0, pl.ds(old, rows_all), :], contract, preferred_element_type=F32
            )
            first = first * scale
            second = jnp.where(seen, second * scale, NEG_BIG)
            top = jnp.maximum(
                jnp.max(first, axis=-1, keepdims=True), jnp.max(second, axis=-1, keepdims=True)
            )
            first = jnp.exp2(first - top)
            second = jnp.exp2(second - top)
            total = jnp.sum(first, axis=-1, keepdims=True) + jnp.sum(second, axis=-1, keepdims=True)
            value = jnp.dot(
                first.astype(BF), kv[1, pl.ds(0, old), :], preferred_element_type=F32
            ) + jnp.dot(
                second.astype(BF), kv[1, pl.ds(old, rows_all), :], preferred_element_type=F32
            )
            att[:, cols] = (value / total).astype(BF)

    def term(far, step, other):
        slot = at(far, step, other)
        cols = pl.ds(pl.multiple_of(slot * width, width), width)
        return jnp.dot(att[...], wo[:, cols], preferred_element_type=F32).astype(BF)

    def add_into(dst, src):
        dst[...] = (dst[...].astype(F32) + src[...].astype(F32)).astype(BF)

    def lend_copy(kind, j):
        rows = rows_of(j)
        return pltpu.make_async_remote_copy(
            src_ref=lend.at[kind, rows, :],
            dst_ref=borrowed.at[kind, rows, :],
            send_sem=lend_send.at[kind, j],
            recv_sem=lend_recv.at[kind, j],
            device_id={"tp": sib},
            device_id_type=MESH,
        )

    def mid_copy(far, way, j):
        rows = half_of(j, way)
        return pltpu.make_async_remote_copy(
            src_ref=mine.at[far * 4 + 2, rows, :],
            dst_ref=mid.at[far, rows, :],
            send_sem=mid_send.at[far * 2 + way, j],
            recv_sem=mid_recv.at[far * 2 + way, j],
            device_id={"tp": down if way else up},
            device_id_type=MESH,
        )

    def near_copy(far, way, k, j):
        rows = half_of(j, k)
        return pltpu.make_async_remote_copy(
            src_ref=mine.at[far * 4 + (3 if way else 1), rows, :],
            dst_ref=near.at[far * 2 + way, rows, :],
            send_sem=near_send.at[far * 4 + way * 2 + k, j],
            recv_sem=near_recv.at[far * 4 + way * 2 + k, j],
            device_id={"tp": down if way else up},
            device_id_type=MESH,
        )

    def last_copy(j):
        rows = rows_of(j)
        return pltpu.make_async_remote_copy(
            src_ref=mine.at[4, rows, :],
            dst_ref=last.at[rows, :],
            send_sem=last_send.at[j],
            recv_sem=last_recv.at[j],
            device_id={"tp": across},
            device_id_type=MESH,
        )

    kinds = ((1, 2), (0, 2), (1, 1), (1, 3), (0, 1), (0, 3), (1, 0), (0, 0))
    lag = 2

    def produce(j):
        attention(j)
        rows = rows_of(j)
        for k in range(len(kinds) + lag):
            if k < len(kinds):
                far, step = kinds[k]
                kind = far * 4 + step
                lend[kind, rows, :] = term(far, step, 1)
                lend_copy(kind, j).start()
                mine[kind, rows, :] = term(far, step, 0)
            if k >= lag:
                far, step = kinds[k - lag]
                kind = far * 4 + step
                lend_copy(kind, j).wait_recv()
                add_into(mine.at[kind, rows, :], borrowed.at[kind, rows, :])
                if step == 2:
                    mid_copy(far, 0, j).start()
                    mid_copy(far, 1, j).start()
                if step == 1:
                    near_copy(far, 0, 1, j).start()
                if step == 3:
                    near_copy(far, 1, 0, j).start()

    def relay(j):
        for far in (1, 0):
            for way in (0, 1):
                mid_copy(far, way, j).wait_recv()
                rows = half_of(j, way)
                add_into(mine.at[far * 4 + (3 if way else 1), rows, :], mid.at[far, rows, :])
                near_copy(far, way, way, j).start()

    def near_wait(far, j):
        for way in (0, 1):
            for k in (0, 1):
                near_copy(far, way, k, j).wait_recv()

    def cross(j):
        near_wait(1, j)
        rows = rows_of(j)
        mine[4, rows, :] = (
            mine[4, rows, :].astype(F32) + near[2, rows, :].astype(F32) + near[3, rows, :].astype(F32)
        ).astype(BF)
        last_copy(j).start()

    def finish(j):
        near_wait(0, j)
        last_copy(j).wait_recv()
        rows = rows_of(j)
        out[rows, :] = (
            tok[rows, :].astype(F32)
            + (
                mine[0, rows, :].astype(F32)
                + near[0, rows, :].astype(F32)
                + near[1, rows, :].astype(F32)
                + last[rows, :].astype(F32)
            )
        ).astype(BF)

    def turn(j, carry):
        @pl.when(j < n)
        def _():
            produce(j)

        @pl.when((j >= 1) & (j < n + 1))
        def _():
            relay(j - 1)

        @pl.when((j >= 2) & (j < n + 2))
        def _():
            cross(j - 2)

        @pl.when(j >= 3)
        def _():
            finish(j - 3)

        @pl.when(j == 1)
        def _():
            dec_forward()

        @pl.when(j < 4)
        def _():
            dec_scores(2 * j)
            dec_scores(2 * j + 1)

        @pl.when(j == 4)
        def _():
            dec_arrive()

        @pl.when((j >= 4) & (j < 8))
        def _():
            dec_settle(2 * j - 8)
            dec_settle(2 * j - 7)

        @pl.when(j == 7)
        def _():
            dec_share()

        @pl.when(j == 8)
        def _():
            dec_combine()

        return carry

    lax.fori_loop(0, n + 3, turn, 0)

    def drain(j, carry):
        for kind in range(8):
            lend_copy(kind, j).wait_send()
        for far in (0, 1):
            for way in (0, 1):
                mid_copy(far, way, j).wait_send()
                for k in (0, 1):
                    near_copy(far, way, k, j).wait_send()
        last_copy(j).wait_send()
        return carry

    lax.fori_loop(0, n, drain, 0)
    dec_end()


def attend_scatter(tokens, queries, kv, pages, dec_q, dec_len, out_weight, cache):
    rows, width = tokens.shape
    vmem = pl.BlockSpec(memory_space=pltpu.VMEM)
    dma = pltpu.SemaphoreType.DMA
    n = SCATTER_CHUNKS
    seqs = cache.shape[0]
    shards = 2 * RING * SIDES
    groups = pages.shape[1]
    return pl.pallas_call(
        attend_kernel,
        out_shape=(
            jax.ShapeDtypeStruct((rows, width), BF),
            jax.ShapeDtypeStruct((seqs, HEADS, HD), BF),
        ),
        in_specs=[
            vmem,
            vmem,
            vmem,
            vmem,
            vmem,
            pl.BlockSpec(memory_space=pltpu.SMEM),
            pl.BlockSpec(memory_space=pl.ANY),
            pl.BlockSpec(memory_space=pl.ANY),
        ],
        out_specs=(vmem, vmem),
        scratch_shapes=[
            pltpu.VMEM(out_weight.shape, BF),
            pltpu.VMEM((rows // n, width), BF),
            pltpu.VMEM((8, rows, width), BF),
            pltpu.VMEM((8, rows, width), BF),
            pltpu.VMEM((8, rows, width), BF),
            pltpu.VMEM((2, rows, width), BF),
            pltpu.VMEM((4, rows, width), BF),
            pltpu.VMEM((rows, width), BF),
            pltpu.VMEM(cache.shape, BF),
            pltpu.VMEM(pages.shape, BF),
            pltpu.VMEM((groups, shards, 16, HD), BF),
            pltpu.VMEM((KVH, seqs * 8, HD), F32),
            pltpu.VMEM((KVH + 1, seqs * 8, HD), F32),
            pltpu.VMEM((shards, 5, 8, HD), F32),
            dma((2,)),
            dma((8, n)),
            dma((8, n)),
            dma((4, n)),
            dma((4, n)),
            dma((8, n)),
            dma((8, n)),
            dma((n,)),
            dma((n,)),
            dma((shards,)),
            dma((shards,)),
            dma((groups,)),
            dma((groups,)),
            dma((shards,)),
            dma((shards,)),
            dma((shards,)),
            dma((shards,)),
        ],
        compiler_params=pltpu.CompilerParams(
            collective_id=2, has_side_effects=True, vmem_limit_bytes=60 * MIB
        ),
        cost_estimate=pl.CostEstimate(
            flops=2 * rows * width * out_weight.shape[1] * 2,
            bytes_accessed=12 * MIB,
            transcendentals=4 * rows * kv.shape[1],
        ),
        name="attend_scatter",
    )(tokens, queries, kv, pages, dec_q, dec_len, out_weight, cache)


def per_device(
    tokens,
    norm_gain,
    query_weight,
    kv_weight,
    out_weight,
    prefix_cache,
    prompt_len,
    page_owner,
    page_seq,
    dec_queries,
    dec_cache,
    dec_len,
):
    group_count = lax.axis_size("group")
    shard_count = lax.axis_size("tp")
    device_count = group_count * shard_count
    shard_index = lax.axis_index("tp")
    span_rows = tokens.shape[0]
    kv_width = kv_weight.shape[1]
    page_count = span_rows // PAGE
    capacity = max(2, 3 * page_count // (2 * device_count))
    queries, kv_both = gather_multiply(tokens, norm_gain, prefix_cache, query_weight, kv_weight)
    kv_own = lax.dynamic_index_in_dim(kv_both, shard_index % 2, 0, keepdims=False)[-span_rows:]
    owner = page_owner[:, 0]
    index = jnp.arange(page_count, dtype=jnp.int32)
    earlier = (owner[:, None] == owner[None, :]) & (index[None, :] < index[:, None])
    slot = jnp.sum(earlier.astype(jnp.int32), axis=1)
    starts = index * PAGE
    live = starts < prompt_len[0]
    place = owner % shard_count * group_count + owner // shard_count
    target = jnp.where(live, place * capacity + slot, device_count * capacity)
    spots = jnp.arange(device_count * capacity, dtype=jnp.int32)
    choose = (target[None, :] == spots[:, None]).astype(jnp.bfloat16)
    sent = jnp.dot(
        choose, kv_own.reshape(page_count, PAGE * kv_width), preferred_element_type=jnp.float32
    ).astype(jnp.bfloat16)
    sent = sent.reshape(device_count, capacity * PAGE, kv_width)
    lane = jnp.arange(kv_width, dtype=jnp.int32)[None, :]
    count = jnp.minimum(PAGE, prompt_len[0] - starts)
    first = lax.axis_index("group") * 16 + slot[:, None] * PAGE
    held = (lane >= first) & (lane < first + count[:, None])
    marks = jnp.where(held, page_seq[:, None] + 1, 0).astype(jnp.bfloat16)
    devices = jnp.arange(device_count, dtype=jnp.int32)
    mine = ((place[None, :] == devices[:, None]) & live[None, :]).astype(jnp.bfloat16)
    mark_rows = jnp.dot(mine, marks, preferred_element_type=jnp.float32).astype(jnp.bfloat16)
    mark_rows = jnp.pad(mark_rows[:, None, :], ((0, 0), (0, 16 - capacity * PAGE - 1), (0, 0)))
    pages = jnp.concatenate([sent, mark_rows], 1)
    pages = pages.reshape(shard_count, group_count, 16, kv_width)
    dec_seqs = dec_queries.shape[0]
    dec_q = dec_queries.reshape(dec_seqs, KVH, HEADS // KVH, HD).transpose(1, 0, 2, 3)
    dec_q = dec_q.reshape(KVH, dec_seqs * (HEADS // KVH), HD).astype(jnp.float32)
    hidden_out, dec_out = attend_scatter(
        tokens, queries, kv_both, pages, dec_q, dec_len, out_weight, dec_cache
    )
    dec_out = dec_out.reshape(dec_seqs, HEADS * HD)
    return (hidden_out, dec_out)


def solution(mesh):
    return jax.shard_map(
        per_device,
        mesh=mesh,
        in_specs=(
            P("group", "tp"),
            P(None, "tp"),
            P(None, "tp"),
            P(None, "tp"),
            P("tp", None),
            P("group", "tp"),
            P("group"),
            P("group", None),
            P("group"),
            P("group", None),
            P("group", "tp", None),
            P("group"),
        ),
        out_specs=(P("group", "tp"), P("group", None)),
        check_vma=False,
    )
```

time: 425 us -> 193 us (0.45)
  Pallas kernels: 0 us -> 176 us
  waiting for transfers between devices: 134 us -> 0 us
  matrix products: 81.3 us -> 0.57 us
  blocking collectives: 71.1 us -> 0 us
  local copies, waits for them, and re-layouts: 56.6 us -> 11.6 us
  other arithmetic: 47.2 us -> 2.67 us
  starting transfers between devices: 17.6 us -> 0 us
  between operations: 14.7 us -> 1.37 us
    pallas_call x0 -> x2, Pallas kernels: none -> 176 us  [the longest x1 95.5 us: attend_scatter(): pl.pallas_call(attend_kernel, out_shape=(jax.ShapeDtypeStruct((rows, widt...]
    reduce_scatter x1 -> x0, waiting for transfers between devices: 75.9 us -> none  [per_device(): lax.psum_scatter(term.astype(jnp.bfloat16), 'tp', scatter_dimension=1, ti...]
    all_gather x3 -> x0, blocking collectives: 71.1 us -> none  [the longest x2 46.6 us: combined_all(): everything = jax.tree.map(lambda part: lax.all_gather(part, axis), value)]
    dot_general x8 -> x2, matrix products: 61.6 us -> 0.57 us  [the longest x1 0.3 us: per_device(): jnp.dot(mine, marks, preferred_element_type=jnp.float32)]
    all_gather x2 -> x0, waiting for transfers between devices: 57.4 us -> none  [the longest x1 57.4 us: per_device(): lax.all_gather(tokens, 'tp', axis=1, tiled=True)]
    scatter x3 -> x0, local copies, waits for them, and re-layouts: 42.8 us -> none  [the longest x1 28.8 us: per_device(): buffer = jnp.zeros((device_count, capacity, PAGE, kv_width), jnp.bfloat16...]
    add x33 -> x0, other arithmetic: 30.6 us -> none  [the longest x15 18.3 us: combine_softmax(): first[2] * scale_first[..., None] + second[2] * scale_second[..., None]]
    sub x1 -> x0, matrix products: 19.7 us -> none  [block_attention(): expo = jnp.exp(scores - top_score)]
  transfers between devices with their start and end apart: 6 -> 0, of which waited for: 2 -> 0; matrix products, arithmetic and copies ran while one was open for 32% -> 0% of each run, Pallas kernels for 0% -> 0%
where the time goes in v1:
time: 193 us
  Pallas kernels  176 us (91%)
  local copies, waits for them, and re-layouts  11.6 us (6%)
  other arithmetic  2.67 us (1%)
    pallas_call x1, Pallas kernels, attend_scatter(): pl.pallas_call(attend_kernel, out_shape=(jax.ShapeDtypeStruct((rows, widt...  95.5 us
    pallas_call x1, Pallas kernels, gather_multiply(): pl.pallas_call(gather_kernel, out_shape=(jax.ShapeDtypeStruct((rows, quer...  80.9 us
    unnamed x15, local copies, waits for them, and re-layouts  9.38 us

profile of v1, /device:TPU:0, one launch (start us, length us, event | category | flops | bytes accessed | tf_op | source)
XLA Modules:
  0.0 192.6 jit_solution(722031332460686188)
XLA Ops:
  1.3 0.9 convert_reduce_fusion
  2.2 0.7 add_select_fusion
  3.0 0.3 fusion
  3.3 0.1 copy.20
  3.3 0.1 pad.4.clone
  3.4 1.6 copy.24
  5.0 0.0 copy-start.1
  5.0 1.6 copy-done.1
  6.6 0.0 copy-start.2
  6.6 1.2 copy-done.2
  7.8 0.0 copy-start.3
  7.8 0.9 copy-done.3
  8.8 0.0 copy-start.4
  8.8 0.7 copy-done.4
  9.5 80.9 %gather_multiply.1 = (bf16[1024,512]{1,0:T(8,128)(2,1)S(1)}, bf16[2,2048,128]{2,1,0:T(8,128)(2,1)S(1)}) custom-call(bf16[1024,512]{1,0:T(8,128)(2,1)S(1)} %copy-done.2, bf16[1,512]{1,0:T(2,128)(2,1)S(1)} %copy-done.4, bf16[1024,128]{1,0:T(8,128)(2,1)S(1)} %copy-done.3, bf16[8192,512]{1,0:T(8,128)(2,1)} %qw_hbm.1, bf16[8192,128]{1,0:T(8,128)(2,1)S(1)} %copy-done.1), custom_call_target="tpu_custom_call" | custom-call | flops 10737418240 | bytes 16777216 | tf_op jit(solution)/shard_map/gather_multiply/pallas_call | solution.py:246
  90.3 0.0 copy-start.5
  90.4 1.0 copy-done.5
  91.3 0.0 copy-start
  91.3 0.2 reshape.119
  91.5 0.3 convolution_convert_fusion
  91.8 0.4 concatenate.8
  92.2 1.0 pad_maximum_fusion.pages
  93.2 0.0 copy-done
  93.2 95.5 %attend_scatter.1 = (bf16[1024,512]{1,0:T(8,128)(2,1)}, bf16[8,64,128]{2,1,0:T(8,128)(2,1)}) custom-call(bf16[1024,512]{1,0:T(8,128)(2,1)} %tok.3, bf16[1024,512]{1,0:T(8,128)(2,1)} %copy-done.5, bf16[2,2048,128]{2,1,0:T(8,128)(2,1)} %copy-done, bf16[16,8,16,128]{3,2,1,0:T(8,128)(2,1)} %pad_maximum_fusion.pages, f32[8,64,128]{2,1,0:T(8,128)} %bitcast.20, ...), custom_call_target="tpu_custom_call" | custom-call | flops 17179869184 | bytes 12582912 | tf_op jit(solution)/shard_map/attend_scatter/pallas_call | solution.py:758
  188.7 1.6 copy.25
  190.3 2.3 %copy.28 = bf16[1024,512]{1,0:T(8,128)(2,1)} copy(bf16[1024,512]{1,0:T(8,128)(2,1)} %get-tuple-element.19) | data formatting | bytes 2097152
  (2 shorter events, 0.0 us)
Async XLA Ops:
  5.0 1.6 copy-start.1
  6.6 1.2 copy-start.2
  7.8 0.9 copy-start.3
  8.8 0.7 copy-start.4
  90.3 1.0 copy-start.5
  91.3 1.9 copy-start

commit v2 on v1

--- a/solution.py
+++ b/solution.py
@@ -73,8 +73,8 @@
 
 
 def gather_kernel(
+    gain,
     tok,
-    gain,
     prefix,
     qw_hbm,
     kw_hbm,
@@ -108,16 +108,19 @@
 
     load_q = pltpu.make_async_copy(qw_hbm, qw, w_sem.at[0])
     load_k = pltpu.make_async_copy(kw_hbm, kw, w_sem.at[1])
+    prefix_rows = prefix.shape[0]
+    load_x = pltpu.make_async_copy(tok, xall.at[me, pl.ds(GAIN_ROWS, rows_all), :], w_sem.at[2])
+    load_x.start()
+    load_p = pltpu.make_async_copy(prefix, kv_out.at[core, pl.ds(0, prefix_rows), :], w_sem.at[3])
+    load_p.start()
     load_q.start()
     load_k.start()
     xall[me, pl.ds(0, GAIN_ROWS), :] = jnp.broadcast_to(gain[...], (GAIN_ROWS, width))
-    xall[me, pl.ds(GAIN_ROWS, rows_all), :] = tok[...]
-    prefix_rows = prefix.shape[0]
-    kv_out[core, pl.ds(0, prefix_rows), :] = prefix[...]
     acc_q[...] = jnp.zeros_like(acc_q)
     acc_k[...] = jnp.zeros_like(acc_k)
     power[...] = jnp.zeros_like(power)
     greet((across, up, down, sib))
+    load_x.wait()
 
     sends = []
 
@@ -162,9 +165,9 @@
     def got(far, step, i):
         kind = far * 4 + step
         slot = at(far, step)
-        if step == 2:
+        if step == 2 and far == 0:
             landed(xall.at[slot, span(i, 0), :], recv_sem.at[kind, i], down)
-            landed(xall.at[slot, span(i, 1), :], recv_sem.at[8 + far, i], up)
+            landed(xall.at[slot, span(i, 1), :], recv_sem.at[8, i], up)
         else:
             landed(xall.at[slot, span(i), :], recv_sem.at[kind, i], up)
 
@@ -173,6 +176,7 @@
         send(me, span(i), up_send.at[0, i], recv_sem.at[3, i], up)
         send(me, span(i), down_send.at[0, i], recv_sem.at[1, i], down)
         to_sibling(0, 0, i)
+    load_p.wait()
     early = kv_out.at[core, pl.ds(0, prefix_rows), :]
     sends.append(push(early, early, kv_send.at[0], kv_recv.at[0], sib))
     load_q.wait()
@@ -192,23 +196,27 @@
         far = 0 if name in ("Z", "F") else 1
         if name in ("Z", "P"):
             got(far, 3, i)
-            send(at(far, 3), span(i, 0), up_send.at[2 + far, i], recv_sem.at[4 * far + 2, i], up)
+            if far == 0:
+                send(at(0, 3), span(i, 0), up_send.at[2, i], recv_sem.at[2, i], up)
             got(far, 1, i)
-            send(at(far, 1), span(i, 1), down_send.at[2 + far, i], recv_sem.at[8 + far, i], down)
+            if far == 0:
+                send(at(0, 1), span(i, 1), down_send.at[2, i], recv_sem.at[8, i], down)
             to_sibling(far, 3, i)
             to_sibling(far, 1, i)
             multiply(at(far, 3), i)
             multiply(at(far, 1), i)
             return [(far, 3, i), (far, 1, i)]
         got(far, 2, i)
+        if far == 0:
+            send(at(0, 2), span(i), x_send.at[GATHER_CHUNKS + i], recv_sem.at[6, i], across)
         to_sibling(far, 2, i)
         multiply(at(far, 2), i)
         return [(far, 2, i)]
 
     order = (
-        ("O", 0), ("O", 1), ("O", 2), ("O", 3), ("Z", 0), ("Z", 1), ("X", 0), ("Z", 2),
-        ("Z", 3), ("X", 1), ("F", 0), ("F", 1), ("P", 0), ("X", 2), ("F", 2), ("F", 3),
-        ("P", 1), ("X", 3), ("P", 2), ("G", 0), ("P", 3), ("G", 1), ("G", 2), ("G", 3),
+        ("O", 0), ("O", 1), ("O", 2), ("O", 3), ("Z", 0), ("Z", 1), ("Z", 2), ("Z", 3),
+        ("X", 0), ("X", 1), ("X", 2), ("X", 3), ("F", 0), ("F", 1), ("F", 2), ("F", 3),
+        ("P", 0), ("P", 1), ("G", 0), ("P", 2), ("G", 1), ("G", 2), ("P", 3), ("G", 3),
     )
     late = []
     for name, i in order:
@@ -249,7 +257,7 @@
             jax.ShapeDtypeStruct((rows, query_weight.shape[1]), BF),
             jax.ShapeDtypeStruct((2, kv_rows, HD), BF),
         ),
-        in_specs=[vmem, vmem, vmem, pl.BlockSpec(memory_space=pl.ANY), pl.BlockSpec(memory_space=pl.ANY)],
+        in_specs=[vmem] + [pl.BlockSpec(memory_space=pl.ANY)] * 4,
         out_specs=(vmem, vmem),
         scratch_shapes=[
             pltpu.VMEM((shards, rows + GAIN_ROWS, width), BF),
@@ -258,12 +266,12 @@
             pltpu.VMEM((rows, query_weight.shape[1]), F32),
             pltpu.VMEM((rows, HD), F32),
             pltpu.VMEM((rows, HD), F32),
-            dma((2,)),
-            dma((10, n)),
+            dma((4,)),
+            dma((9, n)),
             dma((8, n)),
-            dma((n,)),
-            dma((4, n)),
-            dma((4, n)),
+            dma((2 * n,)),
+            dma((3, n)),
+            dma((3, n)),
             dma((8, n)),
             dma((n + 1,)),
             dma((n + 1,)),
@@ -277,19 +285,21 @@
             transcendentals=0,
         ),
         name="gather_multiply",
-    )(tokens, gain, prefix, query_weight, kv_weight)
+    )(gain, tokens, prefix, query_weight, kv_weight)
 
 
 SCATTER_CHUNKS = 8
 
 
 def attend_kernel(
-    tok,
     q,
     kv,
-    pages,
+    owner,
+    page_rows,
     dec_q,
     dec_len,
+    live_len,
+    tok_hbm,
     wo_hbm,
     cache_hbm,
     out,
@@ -302,12 +312,17 @@
     mid,
     near,
     last,
+    far_in,
+    tok,
     cache,
+    pages,
     first_stop,
     fresh,
+    heads,
     scores,
     partial,
     shares,
+    results,
     w_sem,
     lend_send,
     lend_recv,
@@ -317,6 +332,8 @@
     near_recv,
     last_send,
     last_recv,
+    far_send,
+    far_recv,
     first_send,
     first_recv,
     fresh_send,
@@ -327,7 +344,7 @@
     done_recv,
 ):
     side, ring, core = here()
-    rows_all, width = tok.shape
+    rows_all, width = out.shape
     chunk = rows_all // SCATTER_CHUNKS
     half = chunk // 2
     old = kv.shape[1] - rows_all
@@ -341,6 +358,8 @@
     load.start()
     load_cache = pltpu.make_async_copy(cache_hbm, cache, w_sem.at[1])
     load_cache.start()
+    load_tok = pltpu.make_async_copy(tok_hbm, tok, w_sem.at[2])
+    load_tok.start()
     shard = lax.axis_index("tp")
     group = lax.axis_index("group")
     shards = 2 * RING * SIDES
@@ -386,19 +405,14 @@
             first_stop.at[:, to], fresh.at[group], fresh_send.at[d], fresh_recv.at[d], {"group": to}
         )
 
-    def share_of(shard_to):
-        return partial.at[
-            pl.ds(lax.rem(shard_to, 2) * 4, 5), pl.ds(pl.multiple_of(shard_to // 2 * 8, 8), 8), :
-        ]
-
     def share_copy(d):
         to = lax.rem(shard + d, shards)
         return copy_to(
-            share_of(to), shares.at[shard], share_send.at[d], share_recv.at[d], {"tp": to}
+            partial.at[to], shares.at[shard], share_send.at[d], share_recv.at[d], {"tp": to}
         )
 
     def result_of(of):
-        return dec_out.at[of // 2, pl.ds(pl.multiple_of(lax.rem(of, 2) * 32, 32), 32), :]
+        return results.at[:, pl.ds(pl.multiple_of(of * width, width), width)]
 
     def done_copy(d):
         to = lax.rem(shard + d, shards)
@@ -417,6 +431,38 @@
         return lax.rem(of + count - d, count)
 
     def dec_begin():
+        old_rows = kv.shape[1] - rows_all
+        turn_of = lax.broadcasted_iota(jnp.int32, (1, rows_all), 1)
+        names, seqs = page_rows[0:1, :], page_rows[1:2, :]
+        count = owner.shape[0]
+        page = lax.broadcasted_iota(jnp.int32, (count, rows_all), 0)
+        before = page < lax.broadcasted_iota(jnp.int32, (count, rows_all), 1) // PAGE
+        slot = jnp.sum(
+            jnp.where((owner[...] == names) & before, 1, 0), axis=0, keepdims=True
+        )
+        place = (lax.rem(names, shards) * groups + names // shards) * 16
+        spot = slot * PAGE + lax.rem(turn_of, PAGE)
+        live = turn_of // PAGE * PAGE < live_len[0]
+        target = jnp.where(live, place + spot, -1)
+        tag = jnp.where(live, place + 12, -1)
+        lane = lax.broadcasted_iota(jnp.int32, (HD, rows_all), 0)
+        mark = jnp.where(
+            (lane == group * 16 + spot) & (turn_of < live_len[0]), seqs + 1, 0
+        )
+        mark = mark.astype(F32).astype(BF)
+        block = 16 * groups
+
+        def fill(b, carry):
+            row = lax.broadcasted_iota(jnp.int32, (block, rows_all), 0) + b * block
+            chosen = jnp.where(row == target, 1.0, 0.0).astype(BF)
+            tagged = jnp.where(row == tag, 1.0, 0.0).astype(BF)
+            made = jnp.dot(
+                chosen, kv[core, pl.ds(old_rows, rows_all), :], preferred_element_type=F32
+            ) + lax.dot_general(tagged, mark, contract, preferred_element_type=F32)
+            pages[b] = made.astype(BF).reshape(groups, 16, HD)
+            return carry
+
+        lax.fori_loop(0, shards, fill, 0)
         first_stop[shard] = pages[shard]
         each(shards, lambda d: first_copy(d).start())
 
@@ -444,29 +490,37 @@
     def head_cols(k, part):
         return pl.ds(pl.multiple_of(k * 2 * HD + part * HD, HD), HD)
 
+    count = dec_seqs * 8
+    seq_row = lax.rem(lax.broadcasted_iota(jnp.int32, (count, HD), 0), 8)
+
     def dec_scores(k):
         ctx = cache.shape[1]
-        position = lax.broadcasted_iota(jnp.int32, (8, ctx), 1) + shard * ctx
+        position = lax.broadcasted_iota(jnp.int32, (count, ctx), 1) + shard * ctx
+        parts = []
+        for h in range(8):
+            cols = pl.ds(pl.multiple_of(k * 8 * HD + h * HD, HD), HD)
+            parts.append(dec_q[:, cols].astype(F32))
+        query = jnp.concatenate(parts, axis=0).astype(BF)
+        heads[k] = query
+        found = jnp.full((count, ctx), NEG_BIG, F32)
         for seq in range(dec_seqs):
-            rows = pl.ds(seq * 8, 8)
-            query = dec_q[k, rows, :].astype(BF)
             score = lax.dot_general(
                 query, cache[seq, :, head_cols(k, 0)], contract, preferred_element_type=F32
             )
-            scores[k, rows, :] = jnp.where(position < dec_len[seq], score * scale, NEG_BIG)
+            valid = (position < dec_len[seq]) & (seq_row == seq)
+            found = jnp.where(valid, score * scale, found)
+        scores[k] = found
 
     def dec_settle(k):
-        count = dec_seqs * 8
         spots = fresh.shape[0] * 16
         mark = fresh[0, 0].astype(F32)
         for g in range(1, fresh.shape[0]):
             mark = mark + fresh[g, 0].astype(F32)
         mark = mark[12:13, :]
-        seq_of = lax.broadcasted_iota(jnp.int32, (count, spots), 0) // 8 + 1
-        held = mark == seq_of.astype(F32)
+        held = mark == (seq_row + 1).astype(F32)
         key = fresh[:, pl.ds(2 * k, 1)].reshape(spots, HD)
         value = fresh[:, pl.ds(2 * k + 1, 1)].reshape(spots, HD)
-        new = lax.dot_general(dec_q[k].astype(BF), key, contract, preferred_element_type=F32)
+        new = lax.dot_general(heads[k], key, contract, preferred_element_type=F32)
         new = jnp.where(held, new * scale, NEG_BIG)
         old = scores[k]
         top = jnp.maximum(
@@ -476,20 +530,24 @@
         old = jnp.where(old > 0.5 * NEG_BIG, jnp.exp2(old - top), 0.0)
         total = jnp.sum(new, axis=-1, keepdims=True) + jnp.sum(old, axis=-1, keepdims=True)
         accum = jnp.dot(new.astype(BF), value, preferred_element_type=F32)
-        place = k + k // 4
         for seq in range(dec_seqs):
-            rows = slice(seq * 8, seq * 8 + 8)
-            partial[place, pl.ds(seq * 8, 8), :] = accum[rows] + jnp.dot(
-                old[rows].astype(BF), cache[seq, :, head_cols(k, 1)], preferred_element_type=F32
+            own = jnp.where(seq_row == seq, old, 0.0).astype(BF)
+            accum = accum + jnp.dot(
+                own, cache[seq, :, head_cols(k, 1)], preferred_element_type=F32
             )
-        lane = lax.broadcasted_iota(jnp.int32, (count, HD), 1)
-        stat = jnp.where(lax.rem(lane, 16) < 8, top, total)
-        partial[4] = jnp.where(lane // 16 == k, stat, partial[4])
+        lane = lax.broadcasted_iota(jnp.int32, (8, HD), 1) // 16
+        for half_of_heads in range(2):
+            low = half_of_heads * 32
+            stat = jnp.zeros((8, HD), F32)
+            for h in range(4):
+                rows = slice(low + h * 8, low + h * 8 + 8)
+                stat = jnp.where(lane == h, top[rows], stat)
+                stat = jnp.where(lane == 4 + h, total[rows], stat)
+            partial[2 * k + half_of_heads, pl.ds(0, 32), :] = accum[low : low + 32]
+            partial[2 * k + half_of_heads, pl.ds(32, 8), :] = stat
 
     def dec_share():
-        shares[shard] = partial[
-            pl.ds(core * 4, 5), pl.ds(pl.multiple_of(shard // 2 * 8, 8), 8), :
-        ]
+        shares[shard] = partial[shard]
         each(shards, lambda d: share_copy(d).start())
 
     def dec_combine():
@@ -499,26 +557,16 @@
             copy_to(ref, ref, share_send.at[d], share_recv.at[d], {"tp": frm}).wait_recv()
 
         each(shards, take)
-        stat = shares[:, pl.ds(4 - 4 * core, 1)].reshape(shards, 8, HD)
-        lane = lax.broadcasted_iota(jnp.int32, (shards, 8, HD), 2)
-        parts = []
+        stat = shares[:, pl.ds(32, 8), :]
+        lane = lax.broadcasted_iota(jnp.int32, (shards, 8, HD), 2) // 16
         for h in range(4):
-            here_lane = lane // 16 == core * 4 + h
-            low = lax.rem(lane, 16) < 8
-            top = jnp.max(jnp.where(here_lane & low, stat, NEG_BIG), axis=-1, keepdims=True)
-            total = jnp.max(
-                jnp.where(here_lane & jnp.logical_not(low), stat, 0.0), axis=-1, keepdims=True
-            )
+            top = jnp.max(jnp.where(lane == h, stat, NEG_BIG), axis=-1, keepdims=True)
+            total = jnp.max(jnp.where(lane == 4 + h, stat, 0.0), axis=-1, keepdims=True)
             factor = jnp.exp2(top - jnp.max(top, axis=0, keepdims=True))
             whole = jnp.sum(factor * total, axis=0)
-            accum = jnp.sum(
-                factor * shares[:, pl.ds(core + h, 1)].reshape(shards, 8, HD), axis=0
-            )
-            parts.append(accum / whole)
-        for pair in range(2):
-            rows = pl.ds(pl.multiple_of(core * 32 + pair * 16, 16), 16)
-            both = jnp.concatenate([parts[2 * pair], parts[2 * pair + 1]], axis=0)
-            dec_out[shard // 2, rows, :] = both.astype(BF)
+            accum = jnp.sum(factor * shares[:, pl.ds(h * 8, 8), :], axis=0)
+            cols = pl.ds(pl.multiple_of(shard * width + h * HD, HD), HD)
+            results[:, cols] = accum / whole
         each(shards, lambda d: done_copy(d).start())
 
     def dec_end():
@@ -528,14 +576,14 @@
             copy_to(ref, ref, done_send.at[d], done_recv.at[d], {"tp": frm}).wait_recv()
 
         each(shards, take)
+        dec_out[...] = results[...].astype(BF)
         for copy in (first_copy, share_copy, done_copy):
             each(shards, lambda d, copy=copy: copy(d).wait_send())
         each(groups, lambda d: fresh_copy(d).wait_send())
 
-    dec_begin()
-    partial[4] = jnp.zeros_like(partial[4])
     load.wait()
     load_cache.wait()
+    load_tok.wait()
 
     def rows_of(j):
         return pl.ds(pl.multiple_of(j * chunk, chunk), chunk)
@@ -543,11 +591,10 @@
     def half_of(j, k):
         return pl.ds(pl.multiple_of(j * chunk + k * half, half), half)
 
-    def attention(j):
+    def attend(j, new):
         rows = rows_of(j)
-        row = lax.broadcasted_iota(jnp.int32, (chunk, rows_all), 0) + j * chunk
-        column = lax.broadcasted_iota(jnp.int32, (chunk, rows_all), 1)
-        seen = column <= row
+        row = lax.broadcasted_iota(jnp.int32, (chunk, new), 0) + j * chunk
+        seen = lax.broadcasted_iota(jnp.int32, (chunk, new), 1) <= row
         for h in range(width // HD):
             cols = pl.ds(h * HD, HD)
             query = q[rows, cols]
@@ -555,7 +602,7 @@
                 query, kv[0, pl.ds(0, old), :], contract, preferred_element_type=F32
             )
             second = lax.dot_general(
-                query, kv[0, pl.ds(old, rows_all), :], contract, preferred_element_type=F32
+                query, kv[0, pl.ds(old, new), :], contract, preferred_element_type=F32
             )
             first = first * scale
             second = jnp.where(seen, second * scale, NEG_BIG)
@@ -568,9 +615,16 @@
             value = jnp.dot(
                 first.astype(BF), kv[1, pl.ds(0, old), :], preferred_element_type=F32
             ) + jnp.dot(
-                second.astype(BF), kv[1, pl.ds(old, rows_all), :], preferred_element_type=F32
+                second.astype(BF), kv[1, pl.ds(old, new), :], preferred_element_type=F32
             )
             att[:, cols] = (value / total).astype(BF)
+
+    def attention(j):
+        for low, high in ((0, n // 4), (n // 4, n // 2), (n // 2, n)):
+
+            @pl.when((j >= low) & (j < high))
+            def _(high=high):
+                attend(j, high * chunk)
 
     def term(far, step, other):
         slot = at(far, step, other)
@@ -591,14 +645,25 @@
             device_id_type=MESH,
         )
 
-    def mid_copy(far, way, j):
+    def mid_copy(way, j):
         rows = half_of(j, way)
         return pltpu.make_async_remote_copy(
-            src_ref=mine.at[far * 4 + 2, rows, :],
-            dst_ref=mid.at[far, rows, :],
-            send_sem=mid_send.at[far * 2 + way, j],
-            recv_sem=mid_recv.at[far * 2 + way, j],
+            src_ref=mine.at[2, rows, :],
+            dst_ref=mid.at[rows, :],
+            send_sem=mid_send.at[way, j],
+            recv_sem=mid_recv.at[way, j],
             device_id={"tp": down if way else up},
+            device_id_type=MESH,
+        )
+
+    def far_copy(j):
+        rows = rows_of(j)
+        return pltpu.make_async_remote_copy(
+            src_ref=mine.at[6, rows, :],
+            dst_ref=far_in.at[rows, :],
+            send_sem=far_send.at[j],
+            recv_sem=far_recv.at[j],
+            device_id={"tp": across},
             device_id_type=MESH,
         )
 
@@ -642,21 +707,30 @@
                 kind = far * 4 + step
                 lend_copy(kind, j).wait_recv()
                 add_into(mine.at[kind, rows, :], borrowed.at[kind, rows, :])
-                if step == 2:
-                    mid_copy(far, 0, j).start()
-                    mid_copy(far, 1, j).start()
+                if (far, step) == (1, 2):
+                    far_copy(j).start()
                 if step == 1:
                     near_copy(far, 0, 1, j).start()
+                    if far:
+                        near_copy(far, 0, 0, j).start()
                 if step == 3:
                     near_copy(far, 1, 0, j).start()
+                    if far:
+                        near_copy(far, 1, 1, j).start()
+
+    def pass_on(j):
+        far_copy(j).wait_recv()
+        rows = rows_of(j)
+        add_into(mine.at[2, rows, :], far_in.at[rows, :])
+        mid_copy(0, j).start()
+        mid_copy(1, j).start()
 
     def relay(j):
-        for far in (1, 0):
-            for way in (0, 1):
-                mid_copy(far, way, j).wait_recv()
-                rows = half_of(j, way)
-                add_into(mine.at[far * 4 + (3 if way else 1), rows, :], mid.at[far, rows, :])
-                near_copy(far, way, way, j).start()
+        for way in (0, 1):
+            mid_copy(way, j).wait_recv()
+            rows = half_of(j, way)
+            add_into(mine.at[3 if way else 1, rows, :], mid.at[rows, :])
+            near_copy(0, way, way, j).start()
 
     def near_wait(far, j):
         for way in (0, 1):
@@ -694,6 +768,10 @@
         def _():
             relay(j - 1)
 
+        @pl.when(j < n)
+        def _():
+            pass_on(j)
+
         @pl.when((j >= 2) & (j < n + 2))
         def _():
             cross(j - 2)
@@ -702,7 +780,11 @@
         def _():
             finish(j - 3)
 
-        @pl.when(j == 1)
+        @pl.when(j == 0)
+        def _():
+            dec_begin()
+
+        @pl.when(j == 2)
         def _():
             dec_forward()
 
@@ -737,29 +819,32 @@
             lend_copy(kind, j).wait_send()
         for far in (0, 1):
             for way in (0, 1):
-                mid_copy(far, way, j).wait_send()
                 for k in (0, 1):
                     near_copy(far, way, k, j).wait_send()
         last_copy(j).wait_send()
+        far_copy(j).wait_send()
+        mid_copy(0, j).wait_send()
+        mid_copy(1, j).wait_send()
         return carry
 
     lax.fori_loop(0, n, drain, 0)
     dec_end()
 
 
-def attend_scatter(tokens, queries, kv, pages, dec_q, dec_len, out_weight, cache):
+def attend_scatter(
+    tokens, queries, kv, owner, page_rows, dec_q, dec_len, live_len, out_weight, cache, groups
+):
     rows, width = tokens.shape
     vmem = pl.BlockSpec(memory_space=pltpu.VMEM)
     dma = pltpu.SemaphoreType.DMA
     n = SCATTER_CHUNKS
     seqs = cache.shape[0]
     shards = 2 * RING * SIDES
-    groups = pages.shape[1]
     return pl.pallas_call(
         attend_kernel,
         out_shape=(
             jax.ShapeDtypeStruct((rows, width), BF),
-            jax.ShapeDtypeStruct((seqs, HEADS, HD), BF),
+            jax.ShapeDtypeStruct((seqs, HEADS * HD), BF),
         ),
         in_specs=[
             vmem,
@@ -768,6 +853,8 @@
             vmem,
             vmem,
             pl.BlockSpec(memory_space=pltpu.SMEM),
+            pl.BlockSpec(memory_space=pltpu.SMEM),
+            pl.BlockSpec(memory_space=pl.ANY),
             pl.BlockSpec(memory_space=pl.ANY),
             pl.BlockSpec(memory_space=pl.ANY),
         ],
@@ -778,22 +865,29 @@
             pltpu.VMEM((8, rows, width), BF),
             pltpu.VMEM((8, rows, width), BF),
             pltpu.VMEM((8, rows, width), BF),
-            pltpu.VMEM((2, rows, width), BF),
+            pltpu.VMEM((rows, width), BF),
             pltpu.VMEM((4, rows, width), BF),
             pltpu.VMEM((rows, width), BF),
+            pltpu.VMEM((rows, width), BF),
+            pltpu.VMEM((rows, width), BF),
             pltpu.VMEM(cache.shape, BF),
-            pltpu.VMEM(pages.shape, BF),
+            pltpu.VMEM((shards, groups, 16, HD), BF),
+            pltpu.VMEM((shards, groups, 16, HD), BF),
             pltpu.VMEM((groups, shards, 16, HD), BF),
+            pltpu.VMEM((KVH, seqs * 8, HD), BF),
             pltpu.VMEM((KVH, seqs * 8, HD), F32),
-            pltpu.VMEM((KVH + 1, seqs * 8, HD), F32),
-            pltpu.VMEM((shards, 5, 8, HD), F32),
-            dma((2,)),
+            pltpu.VMEM((shards, 40, HD), F32),
+            pltpu.VMEM((shards, 40, HD), F32),
+            pltpu.VMEM((seqs, HEADS * HD), F32),
+            dma((3,)),
             dma((8, n)),
             dma((8, n)),
-            dma((4, n)),
-            dma((4, n)),
+            dma((2, n)),
+            dma((2, n)),
             dma((8, n)),
             dma((8, n)),
+            dma((n,)),
+            dma((n,)),
             dma((n,)),
             dma((n,)),
             dma((shards,)),
@@ -814,7 +908,7 @@
             transcendentals=4 * rows * kv.shape[1],
         ),
         name="attend_scatter",
-    )(tokens, queries, kv, pages, dec_q, dec_len, out_weight, cache)
+    )(queries, kv, owner, page_rows, dec_q, dec_len, live_len, tokens, out_weight, cache)
 
 
 def per_device(
@@ -831,48 +925,21 @@
     dec_cache,
     dec_len,
 ):
-    group_count = lax.axis_size("group")
-    shard_count = lax.axis_size("tp")
-    device_count = group_count * shard_count
-    shard_index = lax.axis_index("tp")
-    span_rows = tokens.shape[0]
-    kv_width = kv_weight.shape[1]
-    page_count = span_rows // PAGE
-    capacity = max(2, 3 * page_count // (2 * device_count))
     queries, kv_both = gather_multiply(tokens, norm_gain, prefix_cache, query_weight, kv_weight)
-    kv_own = lax.dynamic_index_in_dim(kv_both, shard_index % 2, 0, keepdims=False)[-span_rows:]
-    owner = page_owner[:, 0]
-    index = jnp.arange(page_count, dtype=jnp.int32)
-    earlier = (owner[:, None] == owner[None, :]) & (index[None, :] < index[:, None])
-    slot = jnp.sum(earlier.astype(jnp.int32), axis=1)
-    starts = index * PAGE
-    live = starts < prompt_len[0]
-    place = owner % shard_count * group_count + owner // shard_count
-    target = jnp.where(live, place * capacity + slot, device_count * capacity)
-    spots = jnp.arange(device_count * capacity, dtype=jnp.int32)
-    choose = (target[None, :] == spots[:, None]).astype(jnp.bfloat16)
-    sent = jnp.dot(
-        choose, kv_own.reshape(page_count, PAGE * kv_width), preferred_element_type=jnp.float32
-    ).astype(jnp.bfloat16)
-    sent = sent.reshape(device_count, capacity * PAGE, kv_width)
-    lane = jnp.arange(kv_width, dtype=jnp.int32)[None, :]
-    count = jnp.minimum(PAGE, prompt_len[0] - starts)
-    first = lax.axis_index("group") * 16 + slot[:, None] * PAGE
-    held = (lane >= first) & (lane < first + count[:, None])
-    marks = jnp.where(held, page_seq[:, None] + 1, 0).astype(jnp.bfloat16)
-    devices = jnp.arange(device_count, dtype=jnp.int32)
-    mine = ((place[None, :] == devices[:, None]) & live[None, :]).astype(jnp.bfloat16)
-    mark_rows = jnp.dot(mine, marks, preferred_element_type=jnp.float32).astype(jnp.bfloat16)
-    mark_rows = jnp.pad(mark_rows[:, None, :], ((0, 0), (0, 16 - capacity * PAGE - 1), (0, 0)))
-    pages = jnp.concatenate([sent, mark_rows], 1)
-    pages = pages.reshape(shard_count, group_count, 16, kv_width)
-    dec_seqs = dec_queries.shape[0]
-    dec_q = dec_queries.reshape(dec_seqs, KVH, HEADS // KVH, HD).transpose(1, 0, 2, 3)
-    dec_q = dec_q.reshape(KVH, dec_seqs * (HEADS // KVH), HD).astype(jnp.float32)
+    page_rows = jnp.repeat(jnp.stack([page_owner[:, 0], page_seq]), PAGE, axis=1)
     hidden_out, dec_out = attend_scatter(
-        tokens, queries, kv_both, pages, dec_q, dec_len, out_weight, dec_cache
+        tokens,
+        queries,
+        kv_both,
+        page_owner,
+        page_rows,
+        dec_queries,
+        dec_len,
+        prompt_len,
+        out_weight,
+        dec_cache,
+        lax.axis_size("group"),
     )
-    dec_out = dec_out.reshape(dec_seqs, HEADS * HD)
     return (hidden_out, dec_out)
 
 

time: 193 us -> 203 us (1.052)
  Pallas kernels: 176 us -> 188 us
    pallas_call x1, Pallas kernels: 95.5 us -> 118 us  [attend_scatter(): pl.pallas_call(attend_kernel, out_shape=(jax.ShapeDtypeStruct((rows, widt...]
    pallas_call x1, Pallas kernels: 80.9 us -> 70.2 us  [gather_multiply(): pl.pallas_call(gather_kernel, out_shape=(jax.ShapeDtypeStruct((rows, quer...]
    unnamed x15, local copies, waits for them, and re-layouts: 9.38 us -> 11.7 us
where the time goes in v2:
time: 203 us
  Pallas kernels  188 us (93%)
  local copies, waits for them, and re-layouts  12.6 us (6%)
    pallas_call x1, Pallas kernels, attend_scatter(): pl.pallas_call(attend_kernel, out_shape=(jax.ShapeDtypeStruct((rows, widt...  118 us
    pallas_call x1, Pallas kernels, gather_multiply(): pl.pallas_call(gather_kernel, out_shape=(jax.ShapeDtypeStruct((rows, quer...  70.2 us
    unnamed x15, local copies, waits for them, and re-layouts  11.7 us

profile of v2, /device:TPU:0, one launch (start us, length us, event | category | flops | bytes accessed | tf_op | source)
XLA Modules:
  0.0 202.5 jit_solution(4882352487153053031)
XLA Ops:
  1.3 0.7 pad_add_fusion
  2.0 1.5 copy.15.owner
  3.5 0.1 broadcast_in_dim.3
  3.6 0.8 reshape.7.page_rows
  4.4 0.0 copy-start
  4.4 1.6 copy-done
  5.9 0.0 copy-start.1
  5.9 1.2 copy-done.1
  7.2 0.0 copy-start.2
  7.2 0.9 copy-done.2
  8.1 0.0 copy-start.3
  8.1 0.7 copy-done.3
  8.8 70.2 %gather_multiply.1 = (bf16[1024,512]{1,0:T(8,128)(2,1)S(1)}, bf16[2,2048,128]{2,1,0:T(8,128)(2,1)S(1)}) custom-call(bf16[1,512]{1,0:T(2,128)(2,1)S(1)} %copy-done.3, bf16[1024,512]{1,0:T(8,128)(2,1)S(1)} %copy-done.1, bf16[1024,128]{1,0:T(8,128)(2,1)S(1)} %copy-done.2, bf16[8192,512]{1,0:T(8,128)(2,1)} %qw_hbm.1, bf16[8192,128]{1,0:T(8,128)(2,1)S(1)} %copy-done), custom_call_target="tpu_custom_call" | custom-call | flops 10737418240 | bytes 16777216 | tf_op jit(solution)/shard_map/gather_multiply/pallas_call | solution.py:254
  79.1 0.0 copy-start.4
  79.1 1.0 copy-done.4
  80.0 0.0 copy-start.5
  80.0 1.0 copy-done.5
  81.0 117.7 %attend_scatter.1 = (bf16[1024,512]{1,0:T(8,128)(2,1)}, bf16[8,8192]{1,0:T(8,128)(2,1)}) custom-call(bf16[1024,512]{1,0:T(8,128)(2,1)} %copy-done.4, bf16[2,2048,128]{2,1,0:T(8,128)(2,1)} %copy-done.5, s32[256,1]{1,0:T(8,128)} %copy.15.owner, s32[2,1024]{1,0:T(2,128)} %reshape.7.page_rows, bf16[8,8192]{1,0:T(8,128)(2,1)} %dec_q.1, s32[8]{0:T(128)} %dec_len.1, ...), custom_call_target="tpu_custom_call" | custom-call | flops 17179869184 | bytes 12582912 | tf_op jit(solution)/shard_map/attend_scatter/pallas_call | solution.py:843
  198.7 2.3 %copy.19 = bf16[1024,512]{1,0:T(8,128)(2,1)} copy(bf16[1024,512]{1,0:T(8,128)(2,1)} %get-tuple-element.8) | data formatting | bytes 2097152
  200.9 1.6 copy.20
Async XLA Ops:
  4.4 1.6 copy-start
  5.9 1.2 copy-start.1
  7.2 0.9 copy-start.2
  8.1 0.7 copy-start.3
  79.1 1.0 copy-start.4
  80.0 1.0 copy-start.5

commit v3 on v2

--- a/solution.py
+++ b/solution.py
@@ -70,17 +70,25 @@
 
 GATHER_CHUNKS = 4
 GAIN_ROWS = 16
+LOG_SCALE = math.log2(math.e) / math.sqrt(HD)
 
 
 def gather_kernel(
     gain,
+    dec_q,
+    dec_len,
     tok,
     prefix,
     qw_hbm,
     kw_hbm,
+    cache_hbm,
     q_out,
     kv_out,
+    heads,
+    old_sum,
+    old_stat,
     xall,
+    cache,
     qw,
     kw,
     acc_q,
@@ -115,6 +123,8 @@
     load_p.start()
     load_q.start()
     load_k.start()
+    load_cache = pltpu.make_async_copy(cache_hbm, cache, w_sem.at[4])
+    load_cache.start()
     xall[me, pl.ds(0, GAIN_ROWS), :] = jnp.broadcast_to(gain[...], (GAIN_ROWS, width))
     acc_q[...] = jnp.zeros_like(acc_q)
     acc_k[...] = jnp.zeros_like(acc_k)
@@ -181,6 +191,39 @@
     sends.append(push(early, early, kv_send.at[0], kv_recv.at[0], sib))
     load_q.wait()
     load_k.wait()
+    load_cache.wait()
+    dec_seqs, ctx = cache.shape[0], cache.shape[1]
+    contract = (((1,), (1,)), ((), ()))
+
+    def dec_old(k):
+        count = dec_seqs * 8
+        seq_row = lax.rem(lax.broadcasted_iota(jnp.int32, (count, ctx), 0), 8)
+        position = lax.broadcasted_iota(jnp.int32, (count, ctx), 1) + me * ctx
+        parts = [dec_q[:, pl.ds((k * 8 + h) * HD, HD)].astype(F32) for h in range(8)]
+        query = jnp.concatenate(parts, axis=0).astype(BF)
+        heads[k] = query
+        found = jnp.full((count, ctx), NEG_BIG, F32)
+        for seq in range(dec_seqs):
+            score = lax.dot_general(
+                query,
+                cache[seq, :, pl.ds(2 * k * HD, HD)],
+                contract,
+                preferred_element_type=F32,
+            )
+            valid = (position < dec_len[seq]) & (seq_row == seq)
+            found = jnp.where(valid, score * LOG_SCALE, found)
+        top = jnp.max(found, axis=-1, keepdims=True)
+        expo = jnp.where(found > 0.5 * NEG_BIG, jnp.exp2(found - top), 0.0)
+        accum = jnp.zeros((count, HD), F32)
+        for seq in range(dec_seqs):
+            own = jnp.where(seq_row == seq, expo, 0.0).astype(BF)
+            accum = accum + jnp.dot(
+                own, cache[seq, :, pl.ds((2 * k + 1) * HD, HD)], preferred_element_type=F32
+            )
+        old_sum[k] = accum
+        lane = lax.broadcasted_iota(jnp.int32, (count, HD), 1)
+        total = jnp.sum(expo, axis=-1, keepdims=True)
+        old_stat[k] = jnp.where(lane < HD // 2, top, total)
 
     def event(name, i):
         if name == "O":
@@ -221,6 +264,8 @@
     late = []
     for name, i in order:
         fresh = event(name, i)
+        if name in ("Z", "X"):
+            dec_old(i + (4 if name == "X" else 0))
         for item in late:
             from_sibling(*item)
         late = fresh
@@ -235,7 +280,9 @@
         kv_out[core, new, :] = (acc_k[rows, :] * factor).astype(BF)
         ref = kv_out.at[core, new, :]
         sends.append(push(ref, ref, kv_send.at[1 + i], kv_recv.at[1 + i], sib))
-        q_out[rows, :] = (acc_q[rows, :] * factor).astype(BF)
+        queries = (acc_q[rows, :] * (factor * LOG_SCALE)).astype(BF)
+        for h in range(q_out.shape[0]):
+            q_out[h, rows, :] = queries[:, h * HD : (h + 1) * HD]
     landed(kv_out.at[1 - core, pl.ds(0, prefix_rows), :], kv_recv.at[0], sib)
     for i in range(GATHER_CHUNKS):
         new = pl.ds(prefix_rows + i * chunk, chunk)
@@ -244,29 +291,35 @@
         copy.wait_send()
 
 
-def gather_multiply(tokens, gain, prefix, query_weight, kv_weight):
+def gather_multiply(tokens, gain, prefix, query_weight, kv_weight, dec_q, dec_len, cache):
     rows, width = tokens.shape
     shards = 2 * RING * SIDES
     kv_rows = prefix.shape[0] + rows
     vmem = pl.BlockSpec(memory_space=pltpu.VMEM)
     dma = pltpu.SemaphoreType.DMA
     n = GATHER_CHUNKS
+    dec_rows = cache.shape[0] * 8
     return pl.pallas_call(
         gather_kernel,
         out_shape=(
-            jax.ShapeDtypeStruct((rows, query_weight.shape[1]), BF),
+            jax.ShapeDtypeStruct((query_weight.shape[1] // HD, rows, HD), BF),
             jax.ShapeDtypeStruct((2, kv_rows, HD), BF),
+            jax.ShapeDtypeStruct((KVH, dec_rows, HD), BF),
+            jax.ShapeDtypeStruct((KVH, dec_rows, HD), F32),
+            jax.ShapeDtypeStruct((KVH, dec_rows, HD), F32),
         ),
-        in_specs=[vmem] + [pl.BlockSpec(memory_space=pl.ANY)] * 4,
-        out_specs=(vmem, vmem),
+        in_specs=[vmem, vmem, pl.BlockSpec(memory_space=pltpu.SMEM)]
+        + [pl.BlockSpec(memory_space=pltpu.HBM)] * 5,
+        out_specs=(vmem,) * 5,
         scratch_shapes=[
             pltpu.VMEM((shards, rows + GAIN_ROWS, width), BF),
+            pltpu.VMEM(cache.shape, BF),
             pltpu.VMEM(query_weight.shape, BF),
             pltpu.VMEM(kv_weight.shape, BF),
             pltpu.VMEM((rows, query_weight.shape[1]), F32),
             pltpu.VMEM((rows, HD), F32),
             pltpu.VMEM((rows, HD), F32),
-            dma((4,)),
+            dma((5,)),
             dma((9, n)),
             dma((8, n)),
             dma((2 * n,)),
@@ -277,7 +330,7 @@
             dma((n + 1,)),
         ],
         compiler_params=pltpu.CompilerParams(
-            collective_id=1, has_side_effects=True, vmem_limit_bytes=48 * MIB
+            collective_id=1, has_side_effects=True, vmem_limit_bytes=62 * MIB
         ),
         cost_estimate=pl.CostEstimate(
             flops=2 * rows * width * shards * (query_weight.shape[1] + HD),
@@ -285,7 +338,7 @@
             transcendentals=0,
         ),
         name="gather_multiply",
-    )(gain, tokens, prefix, query_weight, kv_weight)
+    )(gain, dec_q, dec_len, tokens, prefix, query_weight, kv_weight, cache)
 
 
 SCATTER_CHUNKS = 8
@@ -294,14 +347,14 @@
 def attend_kernel(
     q,
     kv,
+    heads,
+    old_sum,
+    old_stat,
     owner,
-    page_rows,
-    dec_q,
-    dec_len,
+    seq_of_page,
     live_len,
     tok_hbm,
     wo_hbm,
-    cache_hbm,
     out,
     dec_out,
     wo,
@@ -314,12 +367,9 @@
     last,
     far_in,
     tok,
-    cache,
     pages,
     first_stop,
     fresh,
-    heads,
-    scores,
     partial,
     shares,
     results,
@@ -356,15 +406,13 @@
     across, sib, up, down = at(1, 0), at(0, 0, 1), at(0, 1), at(0, 3)
     load = pltpu.make_async_copy(wo_hbm, wo, w_sem.at[0])
     load.start()
-    load_cache = pltpu.make_async_copy(cache_hbm, cache, w_sem.at[1])
-    load_cache.start()
-    load_tok = pltpu.make_async_copy(tok_hbm, tok, w_sem.at[2])
+    load_tok = pltpu.make_async_copy(tok_hbm, tok, w_sem.at[1])
     load_tok.start()
     shard = lax.axis_index("tp")
     group = lax.axis_index("group")
     shards = 2 * RING * SIDES
     groups = lax.axis_size("group")
-    dec_seqs = cache.shape[0]
+    dec_seqs = dec_out.shape[0]
     barrier = pltpu.get_barrier_semaphore()
 
     def greet_shard(d, carry):
@@ -433,12 +481,24 @@
     def dec_begin():
         old_rows = kv.shape[1] - rows_all
         turn_of = lax.broadcasted_iota(jnp.int32, (1, rows_all), 1)
-        names, seqs = page_rows[0:1, :], page_rows[1:2, :]
-        count = owner.shape[0]
+        count = owner.shape[1]
+        both = jnp.concatenate(
+            [
+                jnp.broadcast_to(owner[...], (8, count)),
+                jnp.broadcast_to(seq_of_page[...], (8, count)),
+            ],
+            axis=0,
+        ).astype(F32)
         page = lax.broadcasted_iota(jnp.int32, (count, rows_all), 0)
-        before = page < lax.broadcasted_iota(jnp.int32, (count, rows_all), 1) // PAGE
+        page_of = lax.broadcasted_iota(jnp.int32, (count, rows_all), 1) // PAGE
+        spread = jnp.where(page == page_of, 1.0, 0.0).astype(BF)
+        by_token = jnp.dot(both.astype(BF), spread, preferred_element_type=F32).astype(jnp.int32)
+        names, seqs = by_token[0:1, :], by_token[8:9, :]
+        column = jnp.transpose(jnp.broadcast_to(owner[...].astype(F32), (HD, count)))
+        column = column[:, 0:1].astype(jnp.int32)
+        before = page < page_of
         slot = jnp.sum(
-            jnp.where((owner[...] == names) & before, 1, 0), axis=0, keepdims=True
+            jnp.where((column == names) & before, 1, 0), axis=0, keepdims=True
         )
         place = (lax.rem(names, shards) * groups + names // shards) * 16
         spot = slot * PAGE + lax.rem(turn_of, PAGE)
@@ -484,32 +544,10 @@
 
         each(groups, take)
 
-    scale = math.log2(math.e) / math.sqrt(HD)
     contract = (((1,), (1,)), ((), ()))
-
-    def head_cols(k, part):
-        return pl.ds(pl.multiple_of(k * 2 * HD + part * HD, HD), HD)
 
     count = dec_seqs * 8
     seq_row = lax.rem(lax.broadcasted_iota(jnp.int32, (count, HD), 0), 8)
-
-    def dec_scores(k):
-        ctx = cache.shape[1]
-        position = lax.broadcasted_iota(jnp.int32, (count, ctx), 1) + shard * ctx
-        parts = []
-        for h in range(8):
-            cols = pl.ds(pl.multiple_of(k * 8 * HD + h * HD, HD), HD)
-            parts.append(dec_q[:, cols].astype(F32))
-        query = jnp.concatenate(parts, axis=0).astype(BF)
-        heads[k] = query
-        found = jnp.full((count, ctx), NEG_BIG, F32)
-        for seq in range(dec_seqs):
-            score = lax.dot_general(
-                query, cache[seq, :, head_cols(k, 0)], contract, preferred_element_type=F32
-            )
-            valid = (position < dec_len[seq]) & (seq_row == seq)
-            found = jnp.where(valid, score * scale, found)
-        scores[k] = found
 
     def dec_settle(k):
         spots = fresh.shape[0] * 16
@@ -521,20 +559,14 @@
         key = fresh[:, pl.ds(2 * k, 1)].reshape(spots, HD)
         value = fresh[:, pl.ds(2 * k + 1, 1)].reshape(spots, HD)
         new = lax.dot_general(heads[k], key, contract, preferred_element_type=F32)
-        new = jnp.where(held, new * scale, NEG_BIG)
-        old = scores[k]
-        top = jnp.maximum(
-            jnp.max(new, axis=-1, keepdims=True), jnp.max(old, axis=-1, keepdims=True)
-        )
+        new = jnp.where(held, new * LOG_SCALE, NEG_BIG)
+        old_top = old_stat[k, :, pl.ds(0, 1)]
+        old_total = old_stat[k, :, pl.ds(HD // 2, 1)]
+        top = jnp.maximum(jnp.max(new, axis=-1, keepdims=True), old_top)
         new = jnp.where(held, jnp.exp2(new - top), 0.0)
-        old = jnp.where(old > 0.5 * NEG_BIG, jnp.exp2(old - top), 0.0)
-        total = jnp.sum(new, axis=-1, keepdims=True) + jnp.sum(old, axis=-1, keepdims=True)
-        accum = jnp.dot(new.astype(BF), value, preferred_element_type=F32)
-        for seq in range(dec_seqs):
-            own = jnp.where(seq_row == seq, old, 0.0).astype(BF)
-            accum = accum + jnp.dot(
-                own, cache[seq, :, head_cols(k, 1)], preferred_element_type=F32
-            )
+        keep = jnp.exp2(old_top - top)
+        total = jnp.sum(new, axis=-1, keepdims=True) + keep * old_total
+        accum = jnp.dot(new.astype(BF), value, preferred_element_type=F32) + keep * old_sum[k]
         lane = lax.broadcasted_iota(jnp.int32, (8, HD), 1) // 16
         for half_of_heads in range(2):
             low = half_of_heads * 32
@@ -581,9 +613,6 @@
             each(shards, lambda d, copy=copy: copy(d).wait_send())
         each(groups, lambda d: fresh_copy(d).wait_send())
 
-    load.wait()
-    load_cache.wait()
-    load_tok.wait()
 
     def rows_of(j):
         return pl.ds(pl.multiple_of(j * chunk, chunk), chunk)
@@ -591,40 +620,39 @@
     def half_of(j, k):
         return pl.ds(pl.multiple_of(j * chunk + k * half, half), half)
 
-    def attend(j, new):
+    def attend(j, plain, edge):
         rows = rows_of(j)
-        row = lax.broadcasted_iota(jnp.int32, (chunk, new), 0) + j * chunk
-        seen = lax.broadcasted_iota(jnp.int32, (chunk, new), 1) <= row
-        for h in range(width // HD):
-            cols = pl.ds(h * HD, HD)
-            query = q[rows, cols]
-            first = lax.dot_general(
-                query, kv[0, pl.ds(0, old), :], contract, preferred_element_type=F32
-            )
-            second = lax.dot_general(
-                query, kv[0, pl.ds(old, new), :], contract, preferred_element_type=F32
-            )
-            first = first * scale
-            second = jnp.where(seen, second * scale, NEG_BIG)
-            top = jnp.maximum(
-                jnp.max(first, axis=-1, keepdims=True), jnp.max(second, axis=-1, keepdims=True)
-            )
-            first = jnp.exp2(first - top)
-            second = jnp.exp2(second - top)
-            total = jnp.sum(first, axis=-1, keepdims=True) + jnp.sum(second, axis=-1, keepdims=True)
-            value = jnp.dot(
-                first.astype(BF), kv[1, pl.ds(0, old), :], preferred_element_type=F32
-            ) + jnp.dot(
-                second.astype(BF), kv[1, pl.ds(old, new), :], preferred_element_type=F32
-            )
-            att[:, cols] = (value / total).astype(BF)
+        count = width // HD
+        query = q[:, rows, :].reshape(count * chunk, HD)
+        row = lax.rem(lax.broadcasted_iota(jnp.int32, (count * chunk, edge), 0), chunk)
+        column = lax.broadcasted_iota(jnp.int32, (count * chunk, edge), 1)
+        seen = column + plain <= row + old + j * chunk
+        first = lax.dot_general(
+            query, kv[0, pl.ds(0, plain), :], contract, preferred_element_type=F32
+        )
+        second = lax.dot_general(
+            query, kv[0, pl.ds(plain, edge), :], contract, preferred_element_type=F32
+        )
+        second = jnp.where(seen, second, NEG_BIG)
+        top = jnp.maximum(
+            jnp.max(first, axis=-1, keepdims=True), jnp.max(second, axis=-1, keepdims=True)
+        )
+        first = jnp.exp2(first - top)
+        second = jnp.exp2(second - top)
+        total = jnp.sum(first, axis=-1, keepdims=True) + jnp.sum(second, axis=-1, keepdims=True)
+        value = jnp.dot(
+            first.astype(BF), kv[1, pl.ds(0, plain), :], preferred_element_type=F32
+        ) + jnp.dot(second.astype(BF), kv[1, pl.ds(plain, edge), :], preferred_element_type=F32)
+        value = value / total
+        for h in range(count):
+            att[:, h * HD : (h + 1) * HD] = value[h * chunk : (h + 1) * chunk].astype(BF)
 
     def attention(j):
-        for low, high in ((0, n // 4), (n // 4, n // 2), (n // 2, n)):
-
-            @pl.when((j >= low) & (j < high))
-            def _(high=high):
-                attend(j, high * chunk)
+        for pair in range(n // 2):
+
+            @pl.when(j // 2 == pair)
+            def _(pair=pair):
+                attend(j, old + 2 * pair * chunk, 2 * chunk)
 
     def term(far, step, other):
         slot = at(far, step, other)
@@ -693,7 +721,6 @@
     lag = 2
 
     def produce(j):
-        attention(j)
         rows = rows_of(j)
         for k in range(len(kinds) + lag):
             if k < len(kinds):
@@ -762,47 +789,54 @@
     def turn(j, carry):
         @pl.when(j < n)
         def _():
+            attention(j)
+
+        @pl.when(j == 0)
+        def _():
+            load.wait()
+            load_tok.wait()
+
+        @pl.when((j >= 1) & (j < n + 1))
+        def _():
+            pass_on(j - 1)
+
+        @pl.when(j < n)
+        def _():
             produce(j)
 
-        @pl.when((j >= 1) & (j < n + 1))
-        def _():
-            relay(j - 1)
-
-        @pl.when(j < n)
-        def _():
-            pass_on(j)
-
         @pl.when((j >= 2) & (j < n + 2))
         def _():
-            cross(j - 2)
-
-        @pl.when(j >= 3)
-        def _():
-            finish(j - 3)
-
-        @pl.when(j == 0)
+            relay(j - 2)
+
+        @pl.when((j >= 3) & (j < n + 3))
+        def _():
+            cross(j - 3)
+
+        @pl.when(j >= 4)
+        def _():
+            finish(j - 4)
+
+        @pl.when(j == 1)
         def _():
             dec_begin()
 
-        @pl.when(j == 2)
+        @pl.when(j == 3)
         def _():
             dec_forward()
 
-        @pl.when(j < 4)
-        def _():
-            dec_scores(2 * j)
-            dec_scores(2 * j + 1)
-
-        @pl.when(j == 4)
+        @pl.when(j == 5)
         def _():
             dec_arrive()
 
-        @pl.when((j >= 4) & (j < 8))
-        def _():
-            dec_settle(2 * j - 8)
-            dec_settle(2 * j - 7)
-
-        @pl.when(j == 7)
+        @pl.when((j >= 5) & (j < 7))
+        def _():
+            def settle(k, carry):
+                dec_settle(k)
+                return carry
+
+            lax.fori_loop((j - 5) * 4, (j - 4) * 4, settle, 0)
+
+        @pl.when(j == 6)
         def _():
             dec_share()
 
@@ -812,7 +846,7 @@
 
         return carry
 
-    lax.fori_loop(0, n + 3, turn, 0)
+    lax.fori_loop(0, n + 4, turn, 0)
 
     def drain(j, carry):
         for kind in range(8):
@@ -832,13 +866,13 @@
 
 
 def attend_scatter(
-    tokens, queries, kv, owner, page_rows, dec_q, dec_len, live_len, out_weight, cache, groups
+    tokens, queries, kv, heads, old_sum, old_stat, owner, seq_of_page, live_len, out_weight, groups
 ):
     rows, width = tokens.shape
     vmem = pl.BlockSpec(memory_space=pltpu.VMEM)
     dma = pltpu.SemaphoreType.DMA
     n = SCATTER_CHUNKS
-    seqs = cache.shape[0]
+    seqs = heads.shape[1] // 8
     shards = 2 * RING * SIDES
     return pl.pallas_call(
         attend_kernel,
@@ -852,11 +886,11 @@
             vmem,
             vmem,
             vmem,
+            vmem,
+            vmem,
             pl.BlockSpec(memory_space=pltpu.SMEM),
-            pl.BlockSpec(memory_space=pltpu.SMEM),
-            pl.BlockSpec(memory_space=pl.ANY),
-            pl.BlockSpec(memory_space=pl.ANY),
-            pl.BlockSpec(memory_space=pl.ANY),
+            pl.BlockSpec(memory_space=pltpu.HBM),
+            pl.BlockSpec(memory_space=pltpu.HBM),
         ],
         out_specs=(vmem, vmem),
         scratch_shapes=[
@@ -870,16 +904,13 @@
             pltpu.VMEM((rows, width), BF),
             pltpu.VMEM((rows, width), BF),
             pltpu.VMEM((rows, width), BF),
-            pltpu.VMEM(cache.shape, BF),
             pltpu.VMEM((shards, groups, 16, HD), BF),
             pltpu.VMEM((shards, groups, 16, HD), BF),
             pltpu.VMEM((groups, shards, 16, HD), BF),
-            pltpu.VMEM((KVH, seqs * 8, HD), BF),
-            pltpu.VMEM((KVH, seqs * 8, HD), F32),
             pltpu.VMEM((shards, 40, HD), F32),
             pltpu.VMEM((shards, 40, HD), F32),
             pltpu.VMEM((seqs, HEADS * HD), F32),
-            dma((3,)),
+            dma((2,)),
             dma((8, n)),
             dma((8, n)),
             dma((2, n)),
@@ -900,7 +931,7 @@
             dma((shards,)),
         ],
         compiler_params=pltpu.CompilerParams(
-            collective_id=2, has_side_effects=True, vmem_limit_bytes=60 * MIB
+            collective_id=2, has_side_effects=True, vmem_limit_bytes=62 * MIB
         ),
         cost_estimate=pl.CostEstimate(
             flops=2 * rows * width * out_weight.shape[1] * 2,
@@ -908,7 +939,32 @@
             transcendentals=4 * rows * kv.shape[1],
         ),
         name="attend_scatter",
-    )(queries, kv, owner, page_rows, dec_q, dec_len, live_len, tokens, out_weight, cache)
+    )(queries, kv, heads, old_sum, old_stat, owner, seq_of_page, live_len, tokens, out_weight)
+
+
+def hand_on_kernel(hidden, dec, hidden_out, dec_out, sem):
+    first = pltpu.make_async_copy(hidden, hidden_out, sem.at[0])
+    second = pltpu.make_async_copy(dec, dec_out, sem.at[1])
+    first.start()
+    second.start()
+    first.wait()
+    second.wait()
+
+
+def hand_on(hidden, dec):
+    vmem = pl.BlockSpec(memory_space=pltpu.VMEM)
+    hbm = pl.BlockSpec(memory_space=pltpu.HBM)
+    return pl.pallas_call(
+        hand_on_kernel,
+        out_shape=(
+            jax.ShapeDtypeStruct(hidden.shape, hidden.dtype),
+            jax.ShapeDtypeStruct(dec.shape, dec.dtype),
+        ),
+        in_specs=[vmem, vmem],
+        out_specs=(hbm, hbm),
+        scratch_shapes=[pltpu.SemaphoreType.DMA((2,))],
+        name="hand_on",
+    )(hidden, dec)
 
 
 def per_device(
@@ -925,22 +981,23 @@
     dec_cache,
     dec_len,
 ):
-    queries, kv_both = gather_multiply(tokens, norm_gain, prefix_cache, query_weight, kv_weight)
-    page_rows = jnp.repeat(jnp.stack([page_owner[:, 0], page_seq]), PAGE, axis=1)
+    queries, kv_both, heads, old_sum, old_stat = gather_multiply(
+        tokens, norm_gain, prefix_cache, query_weight, kv_weight, dec_queries, dec_len, dec_cache
+    )
     hidden_out, dec_out = attend_scatter(
         tokens,
         queries,
         kv_both,
-        page_owner,
-        page_rows,
-        dec_queries,
-        dec_len,
+        heads,
+        old_sum,
+        old_stat,
+        page_owner.reshape(1, -1),
+        page_seq.reshape(1, -1),
         prompt_len,
         out_weight,
-        dec_cache,
         lax.axis_size("group"),
     )
-    return (hidden_out, dec_out)
+    return hand_on(hidden_out, dec_out)
 
 
 def solution(mesh):

time: 203 us -> 179 us (0.88)
  local copies, waits for them, and re-layouts: 12.6 us -> 0 us
  Pallas kernels: 188 us -> 177 us
    pallas_call x1, Pallas kernels: 118 us -> 102 us  [attend_scatter(): pl.pallas_call(attend_kernel, out_shape=(jax.ShapeDtypeStruct((rows, widt...]
    unnamed x15 -> x0, local copies, waits for them, and re-layouts: 11.7 us -> none
    pallas_call x1 -> x2, Pallas kernels: 70.2 us -> 74.8 us  [the longest x1 72.6 us: gather_multiply(): pl.pallas_call(gather_kernel, out_shape=(jax.ShapeDtypeStruct((query_weig...]
where the time goes in v3:
time: 179 us; the launch traced here: 178 us
  Pallas kernels  177 us (99%)
    pallas_call x1, Pallas kernels, attend_scatter(): pl.pallas_call(attend_kernel, out_shape=(jax.ShapeDtypeStruct((rows, widt...  102 us
    pallas_call x1, Pallas kernels, gather_multiply(): pl.pallas_call(gather_kernel, out_shape=(jax.ShapeDtypeStruct((query_weig...  72.6 us

profile of v3, /device:TPU:0, one launch (start us, length us, event | category | flops | bytes accessed | tf_op | source)
XLA Modules:
  0.0 178.3 jit_solution(8682190220260554445)
XLA Ops:
  1.3 72.6 %gather_multiply.1 = (bf16[4,1024,128]{2,1,0:T(8,128)(2,1)}, bf16[2,2048,128]{2,1,0:T(8,128)(2,1)}, bf16[8,64,128]{2,1,0:T(8,128)(2,1)}, f32[8,64,128]{2,1,0:T(8,128)}, f32[8,64,128]{2,1,0:T(8,128)}) custom-call(bf16[1,512]{1,0:T(2,128)(2,1)} %gain.1, bf16[8,8192]{1,0:T(8,128)(2,1)} %dec_q.1, s32[8]{0:T(128)} %dec_len.1, bf16[1024,512]{1,0:T(8,128)(2,1)} %tok_hbm.1, ...), custom_call_target="tpu_custom_call" | custom-call | flops 10737418240 | bytes 16777216 | tf_op jit(solution)/shard_map/gather_multiply/pallas_call | solution.py:302
  73.9 102.1 %attend_scatter.1 = (bf16[1024,512]{1,0:T(8,128)(2,1)}, bf16[8,8192]{1,0:T(8,128)(2,1)}) custom-call(bf16[4,1024,128]{2,1,0:T(8,128)(2,1)} %get-tuple-element.9.q, bf16[2,2048,128]{2,1,0:T(8,128)(2,1)} %get-tuple-element.10.kv, bf16[8,64,128]{2,1,0:T(8,128)(2,1)} %get-tuple-element.11.heads, f32[8,64,128]{2,1,0:T(8,128)} %get-tuple-element.12.old_sum, ...), custom_call_target="tpu_custom_call" | custom-call | flops 17179869184 | bytes 12582912 | tf_op jit(solution)/shard_map/attend_scatter/pallas_call | solution.py:877
  175.9 2.2 %hand_on.1 = (bf16[1024,512]{1,0:T(8,128)(2,1)}, bf16[8,8192]{1,0:T(8,128)(2,1)}) custom-call(bf16[1024,512]{1,0:T(8,128)(2,1)} %get-tuple-element.14.hidden, bf16[8,8192]{1,0:T(8,128)(2,1)} %get-tuple-element.15.dec), custom_call_target="tpu_custom_call" | custom-call | tf_op jit(solution)/shard_map/hand_on/pallas_call | solution.py:957

commit v4 on v3

--- a/solution.py
+++ b/solution.py
@@ -70,13 +70,17 @@
 
 GATHER_CHUNKS = 4
 GAIN_ROWS = 16
+PACK_PARTS = 8
 LOG_SCALE = math.log2(math.e) / math.sqrt(HD)
 
 
 def gather_kernel(
     gain,
     dec_q,
+    owner,
+    seq_of_page,
     dec_len,
+    live_len,
     tok,
     prefix,
     qw_hbm,
@@ -87,8 +91,11 @@
     heads,
     old_sum,
     old_stat,
+    pages,
     xall,
     cache,
+    choice,
+    tags,
     qw,
     kw,
     acc_q,
@@ -103,10 +110,15 @@
     sib_send,
     kv_send,
     kv_recv,
+    split_send,
+    split_recv,
 ):
     side, ring, core = here()
     rows_all, width = tok.shape
     chunk = rows_all // GATHER_CHUNKS
+    group = lax.axis_index("group")
+    groups = lax.axis_size("group")
+    shards = 2 * RING * SIDES
 
     def at(far, step, other=0):
         return shard_at(side, ring, core, far, step, other)
@@ -133,6 +145,7 @@
     load_x.wait()
 
     sends = []
+    split = GATHER_CHUNKS - 1
 
     def span(i, half=None):
         low = 0 if i == 0 else GAIN_ROWS + i * chunk
@@ -178,6 +191,9 @@
         if step == 2 and far == 0:
             landed(xall.at[slot, span(i, 0), :], recv_sem.at[kind, i], down)
             landed(xall.at[slot, span(i, 1), :], recv_sem.at[8, i], up)
+        elif i == split and far == 1 and step in (1, 3):
+            landed(xall.at[slot, span(i, 0), :], recv_sem.at[kind, i], up)
+            landed(xall.at[slot, span(i, 1), :], split_recv.at[step // 2], across)
         else:
             landed(xall.at[slot, span(i), :], recv_sem.at[kind, i], up)
 
@@ -225,14 +241,56 @@
         total = jnp.sum(expo, axis=-1, keepdims=True)
         old_stat[k] = jnp.where(lane < HD // 2, top, total)
 
+    turn_of = lax.broadcasted_iota(jnp.int32, (1, rows_all), 1)
+    count = owner.shape[1]
+    both = jnp.concatenate(
+        [
+            jnp.broadcast_to(owner[...], (8, count)),
+            jnp.broadcast_to(seq_of_page[...], (8, count)),
+        ],
+        axis=0,
+    ).astype(F32)
+    page = lax.broadcasted_iota(jnp.int32, (count, rows_all), 0)
+    page_of = lax.broadcasted_iota(jnp.int32, (count, rows_all), 1) // PAGE
+    spread = jnp.where(page == page_of, 1.0, 0.0).astype(BF)
+    by_token = jnp.dot(both.astype(BF), spread, preferred_element_type=F32).astype(jnp.int32)
+    names, seqs = by_token[0:1, :], by_token[8:9, :]
+    column = jnp.transpose(jnp.broadcast_to(owner[...].astype(F32), (HD, count)))
+    column = column[:, 0:1].astype(jnp.int32)
+    before = page < page_of
+    slot = jnp.sum(
+        jnp.where((column == names) & before, 1, 0), axis=0, keepdims=True
+    )
+    place = (lax.rem(names, shards) * groups + names // shards) * 16
+    spot = slot * PAGE + lax.rem(turn_of, PAGE)
+    live = turn_of // PAGE * PAGE < live_len[0]
+    target = jnp.where(live, place + spot, -1)
+    tag = jnp.where(live, place + 12, -1)
+    lane = lax.broadcasted_iota(jnp.int32, (HD, rows_all), 0)
+    mark = jnp.where(
+        (lane == group * 16 + spot) & (turn_of < live_len[0]), seqs + 1, 0
+    )
+    mark = mark.astype(F32).astype(BF)
+    block = tags.shape[0] // PACK_PARTS
+
+    def pack(part):
+        row = lax.broadcasted_iota(jnp.int32, (block, rows_all), 0) + part * block
+        rows = pl.ds(part * block, block)
+        choice[rows, :] = jnp.where(row == target, 1.0, 0.0).astype(BF)
+        tagged = jnp.where(row == tag, 1.0, 0.0).astype(BF)
+        tags[rows, :] = lax.dot_general(
+            tagged, mark, contract, preferred_element_type=F32
+        ).astype(BF)
+
     def event(name, i):
         if name == "O":
             multiply(me, i)
             return [(0, 0, i)]
         if name == "X":
             got(1, 0, i)
-            send(across, span(i), up_send.at[1, i], recv_sem.at[7, i], up)
-            send(across, span(i), down_send.at[1, i], recv_sem.at[5, i], down)
+            rows = span(i, 0) if i == split else span(i)
+            send(across, rows, up_send.at[1, i], recv_sem.at[7, i], up)
+            send(across, rows, down_send.at[1, i], recv_sem.at[5, i], down)
             to_sibling(1, 0, i)
             multiply(across, i)
             return [(1, 0, i)]
@@ -241,9 +299,13 @@
             got(far, 3, i)
             if far == 0:
                 send(at(0, 3), span(i, 0), up_send.at[2, i], recv_sem.at[2, i], up)
+                if i == split:
+                    send(at(0, 3), span(i, 1), split_send.at[1], split_recv.at[1], across)
             got(far, 1, i)
             if far == 0:
                 send(at(0, 1), span(i, 1), down_send.at[2, i], recv_sem.at[8, i], down)
+                if i == split:
+                    send(at(0, 1), span(i, 1), split_send.at[0], split_recv.at[0], across)
             to_sibling(far, 3, i)
             to_sibling(far, 1, i)
             multiply(at(far, 3), i)
@@ -266,6 +328,9 @@
         fresh = event(name, i)
         if name in ("Z", "X"):
             dec_old(i + (4 if name == "X" else 0))
+        if name == "F":
+            pack(2 * i)
+            pack(2 * i + 1)
         for item in late:
             from_sibling(*item)
         late = fresh
@@ -283,6 +348,14 @@
         queries = (acc_q[rows, :] * (factor * LOG_SCALE)).astype(BF)
         for h in range(q_out.shape[0]):
             q_out[h, rows, :] = queries[:, h * HD : (h + 1) * HD]
+    for part in range(PACK_PARTS):
+        rows = pl.ds(part * block, block)
+        made = jnp.dot(
+            choice[rows, :],
+            kv_out[core, pl.ds(prefix_rows, rows_all), :],
+            preferred_element_type=F32,
+        )
+        pages[rows, :] = (made + tags[rows, :].astype(F32)).astype(BF)
     landed(kv_out.at[1 - core, pl.ds(0, prefix_rows), :], kv_recv.at[0], sib)
     for i in range(GATHER_CHUNKS):
         new = pl.ds(prefix_rows + i * chunk, chunk)
@@ -291,7 +364,20 @@
         copy.wait_send()
 
 
-def gather_multiply(tokens, gain, prefix, query_weight, kv_weight, dec_q, dec_len, cache):
+def gather_multiply(
+    tokens,
+    gain,
+    prefix,
+    query_weight,
+    kv_weight,
+    dec_q,
+    dec_len,
+    cache,
+    owner,
+    seq_of_page,
+    live_len,
+    groups,
+):
     rows, width = tokens.shape
     shards = 2 * RING * SIDES
     kv_rows = prefix.shape[0] + rows
@@ -299,6 +385,7 @@
     dma = pltpu.SemaphoreType.DMA
     n = GATHER_CHUNKS
     dec_rows = cache.shape[0] * 8
+    page_rows = shards * groups * 16
     return pl.pallas_call(
         gather_kernel,
         out_shape=(
@@ -307,13 +394,17 @@
             jax.ShapeDtypeStruct((KVH, dec_rows, HD), BF),
             jax.ShapeDtypeStruct((KVH, dec_rows, HD), F32),
             jax.ShapeDtypeStruct((KVH, dec_rows, HD), F32),
+            jax.ShapeDtypeStruct((page_rows, HD), BF),
         ),
-        in_specs=[vmem, vmem, pl.BlockSpec(memory_space=pltpu.SMEM)]
+        in_specs=[vmem] * 4
+        + [pl.BlockSpec(memory_space=pltpu.SMEM)] * 2
         + [pl.BlockSpec(memory_space=pltpu.HBM)] * 5,
-        out_specs=(vmem,) * 5,
+        out_specs=(vmem,) * 6,
         scratch_shapes=[
             pltpu.VMEM((shards, rows + GAIN_ROWS, width), BF),
             pltpu.VMEM(cache.shape, BF),
+            pltpu.VMEM((page_rows, rows), BF),
+            pltpu.VMEM((page_rows, HD), BF),
             pltpu.VMEM(query_weight.shape, BF),
             pltpu.VMEM(kv_weight.shape, BF),
             pltpu.VMEM((rows, query_weight.shape[1]), F32),
@@ -328,6 +419,8 @@
             dma((8, n)),
             dma((n + 1,)),
             dma((n + 1,)),
+            dma((2,)),
+            dma((2,)),
         ],
         compiler_params=pltpu.CompilerParams(
             collective_id=1, has_side_effects=True, vmem_limit_bytes=62 * MIB
@@ -338,7 +431,19 @@
             transcendentals=0,
         ),
         name="gather_multiply",
-    )(gain, dec_q, dec_len, tokens, prefix, query_weight, kv_weight, cache)
+    )(
+        gain,
+        dec_q,
+        owner,
+        seq_of_page,
+        dec_len,
+        live_len,
+        tokens,
+        prefix,
+        query_weight,
+        kv_weight,
+        cache,
+    )
 
 
 SCATTER_CHUNKS = 8
@@ -350,9 +455,7 @@
     heads,
     old_sum,
     old_stat,
-    owner,
-    seq_of_page,
-    live_len,
+    pages,
     tok_hbm,
     wo_hbm,
     out,
@@ -367,7 +470,6 @@
     last,
     far_in,
     tok,
-    pages,
     first_stop,
     fresh,
     partial,
@@ -429,7 +531,6 @@
 
     lax.fori_loop(1, shards, greet_shard, 0)
     lax.fori_loop(1, groups, greet_group, 0)
-    pl.semaphore_wait(barrier, shards + groups - 2)
 
     def copy_to(src, dst, send_sem, recv_sem, to):
         return pltpu.make_async_remote_copy(
@@ -479,50 +580,6 @@
         return lax.rem(of + count - d, count)
 
     def dec_begin():
-        old_rows = kv.shape[1] - rows_all
-        turn_of = lax.broadcasted_iota(jnp.int32, (1, rows_all), 1)
-        count = owner.shape[1]
-        both = jnp.concatenate(
-            [
-                jnp.broadcast_to(owner[...], (8, count)),
-                jnp.broadcast_to(seq_of_page[...], (8, count)),
-            ],
-            axis=0,
-        ).astype(F32)
-        page = lax.broadcasted_iota(jnp.int32, (count, rows_all), 0)
-        page_of = lax.broadcasted_iota(jnp.int32, (count, rows_all), 1) // PAGE
-        spread = jnp.where(page == page_of, 1.0, 0.0).astype(BF)
-        by_token = jnp.dot(both.astype(BF), spread, preferred_element_type=F32).astype(jnp.int32)
-        names, seqs = by_token[0:1, :], by_token[8:9, :]
-        column = jnp.transpose(jnp.broadcast_to(owner[...].astype(F32), (HD, count)))
-        column = column[:, 0:1].astype(jnp.int32)
-        before = page < page_of
-        slot = jnp.sum(
-            jnp.where((column == names) & before, 1, 0), axis=0, keepdims=True
-        )
-        place = (lax.rem(names, shards) * groups + names // shards) * 16
-        spot = slot * PAGE + lax.rem(turn_of, PAGE)
-        live = turn_of // PAGE * PAGE < live_len[0]
-        target = jnp.where(live, place + spot, -1)
-        tag = jnp.where(live, place + 12, -1)
-        lane = lax.broadcasted_iota(jnp.int32, (HD, rows_all), 0)
-        mark = jnp.where(
-            (lane == group * 16 + spot) & (turn_of < live_len[0]), seqs + 1, 0
-        )
-        mark = mark.astype(F32).astype(BF)
-        block = 16 * groups
-
-        def fill(b, carry):
-            row = lax.broadcasted_iota(jnp.int32, (block, rows_all), 0) + b * block
-            chosen = jnp.where(row == target, 1.0, 0.0).astype(BF)
-            tagged = jnp.where(row == tag, 1.0, 0.0).astype(BF)
-            made = jnp.dot(
-                chosen, kv[core, pl.ds(old_rows, rows_all), :], preferred_element_type=F32
-            ) + lax.dot_general(tagged, mark, contract, preferred_element_type=F32)
-            pages[b] = made.astype(BF).reshape(groups, 16, HD)
-            return carry
-
-        lax.fori_loop(0, shards, fill, 0)
         first_stop[shard] = pages[shard]
         each(shards, lambda d: first_copy(d).start())
 
@@ -657,7 +714,7 @@
     def term(far, step, other):
         slot = at(far, step, other)
         cols = pl.ds(pl.multiple_of(slot * width, width), width)
-        return jnp.dot(att[...], wo[:, cols], preferred_element_type=F32).astype(BF)
+        return jnp.dot(att[...], wo[:, cols], preferred_element_type=F32)
 
     def add_into(dst, src):
         dst[...] = (dst[...].astype(F32) + src[...].astype(F32)).astype(BF)
@@ -717,33 +774,36 @@
             device_id_type=MESH,
         )
 
-    kinds = ((1, 2), (0, 2), (1, 1), (1, 3), (0, 1), (0, 3), (1, 0), (0, 0))
-    lag = 2
+    kinds = ((1, 2), (1, 1), (1, 3), (0, 2), (0, 1), (0, 3), (1, 0), (0, 0))
+    ahead = 4
 
     def produce(j):
         rows = rows_of(j)
-        for k in range(len(kinds) + lag):
-            if k < len(kinds):
-                far, step = kinds[k]
-                kind = far * 4 + step
-                lend[kind, rows, :] = term(far, step, 1)
-                lend_copy(kind, j).start()
-                mine[kind, rows, :] = term(far, step, 0)
-            if k >= lag:
-                far, step = kinds[k - lag]
-                kind = far * 4 + step
-                lend_copy(kind, j).wait_recv()
-                add_into(mine.at[kind, rows, :], borrowed.at[kind, rows, :])
-                if (far, step) == (1, 2):
-                    far_copy(j).start()
-                if step == 1:
-                    near_copy(far, 0, 1, j).start()
-                    if far:
-                        near_copy(far, 0, 0, j).start()
-                if step == 3:
-                    near_copy(far, 1, 0, j).start()
-                    if far:
-                        near_copy(far, 1, 1, j).start()
+
+        def offer(far, step):
+            kind = far * 4 + step
+            lend[kind, rows, :] = term(far, step, 1).astype(BF)
+            lend_copy(kind, j).start()
+
+        for far, step in kinds[:ahead]:
+            offer(far, step)
+        for k, (far, step) in enumerate(kinds):
+            if k + ahead < len(kinds):
+                offer(*kinds[k + ahead])
+            kind = far * 4 + step
+            own = term(far, step, 0)
+            lend_copy(kind, j).wait_recv()
+            mine[kind, rows, :] = (own + borrowed[kind, rows, :].astype(F32)).astype(BF)
+            if (far, step) == (1, 2):
+                far_copy(j).start()
+            if step == 1:
+                near_copy(far, 0, 1, j).start()
+                if far:
+                    near_copy(far, 0, 0, j).start()
+            if step == 3:
+                near_copy(far, 1, 0, j).start()
+                if far:
+                    near_copy(far, 1, 1, j).start()
 
     def pass_on(j):
         far_copy(j).wait_recv()
@@ -786,8 +846,12 @@
             )
         ).astype(BF)
 
+    pl.semaphore_wait(barrier, shards + groups - 2)
+    dec_begin()
+    attend(0, old, 2 * chunk)
+
     def turn(j, carry):
-        @pl.when(j < n)
+        @pl.when((j >= 1) & (j < n))
         def _():
             attention(j)
 
@@ -816,31 +880,27 @@
         def _():
             finish(j - 4)
 
-        @pl.when(j == 1)
-        def _():
-            dec_begin()
-
-        @pl.when(j == 3)
+        @pl.when(j == 0)
         def _():
             dec_forward()
 
-        @pl.when(j == 5)
+        @pl.when(j == 2)
         def _():
             dec_arrive()
 
-        @pl.when((j >= 5) & (j < 7))
+        @pl.when((j >= 2) & (j < 4))
         def _():
             def settle(k, carry):
                 dec_settle(k)
                 return carry
 
-            lax.fori_loop((j - 5) * 4, (j - 4) * 4, settle, 0)
+            lax.fori_loop((j - 2) * 4, (j - 1) * 4, settle, 0)
+
+        @pl.when(j == 3)
+        def _():
+            dec_share()
 
         @pl.when(j == 6)
-        def _():
-            dec_share()
-
-        @pl.when(j == 8)
         def _():
             dec_combine()
 
@@ -866,12 +926,13 @@
 
 
 def attend_scatter(
-    tokens, queries, kv, heads, old_sum, old_stat, owner, seq_of_page, live_len, out_weight, groups
+    tokens, queries, kv, heads, old_sum, old_stat, pages, out_weight
 ):
     rows, width = tokens.shape
     vmem = pl.BlockSpec(memory_space=pltpu.VMEM)
     dma = pltpu.SemaphoreType.DMA
     n = SCATTER_CHUNKS
+    groups = pages.shape[1]
     seqs = heads.shape[1] // 8
     shards = 2 * RING * SIDES
     return pl.pallas_call(
@@ -887,8 +948,6 @@
             vmem,
             vmem,
             vmem,
-            vmem,
-            pl.BlockSpec(memory_space=pltpu.SMEM),
             pl.BlockSpec(memory_space=pltpu.HBM),
             pl.BlockSpec(memory_space=pltpu.HBM),
         ],
@@ -904,7 +963,6 @@
             pltpu.VMEM((rows, width), BF),
             pltpu.VMEM((rows, width), BF),
             pltpu.VMEM((rows, width), BF),
-            pltpu.VMEM((shards, groups, 16, HD), BF),
             pltpu.VMEM((shards, groups, 16, HD), BF),
             pltpu.VMEM((groups, shards, 16, HD), BF),
             pltpu.VMEM((shards, 40, HD), F32),
@@ -939,7 +997,7 @@
             transcendentals=4 * rows * kv.shape[1],
         ),
         name="attend_scatter",
-    )(queries, kv, heads, old_sum, old_stat, owner, seq_of_page, live_len, tokens, out_weight)
+    )(queries, kv, heads, old_sum, old_stat, pages, tokens, out_weight)
 
 
 def hand_on_kernel(hidden, dec, hidden_out, dec_out, sem):
@@ -981,21 +1039,24 @@
     dec_cache,
     dec_len,
 ):
-    queries, kv_both, heads, old_sum, old_stat = gather_multiply(
-        tokens, norm_gain, prefix_cache, query_weight, kv_weight, dec_queries, dec_len, dec_cache
-    )
-    hidden_out, dec_out = attend_scatter(
+    group_count = lax.axis_size("group")
+    queries, kv_both, heads, old_sum, old_stat, pages = gather_multiply(
         tokens,
-        queries,
-        kv_both,
-        heads,
-        old_sum,
-        old_stat,
+        norm_gain,
+        prefix_cache,
+        query_weight,
+        kv_weight,
+        dec_queries,
+        dec_len,
+        dec_cache,
         page_owner.reshape(1, -1),
         page_seq.reshape(1, -1),
         prompt_len,
-        out_weight,
-        lax.axis_size("group"),
+        group_count,
+    )
+    pages = pages.reshape(-1, group_count, 16, HD)
+    hidden_out, dec_out = attend_scatter(
+        tokens, queries, kv_both, heads, old_sum, old_stat, pages, out_weight
     )
     return hand_on(hidden_out, dec_out)
 

time: 179 us -> 171 us (0.955)
  Pallas kernels: 177 us -> 169 us
    pallas_call x1, Pallas kernels: 102 us -> 95.2 us  [attend_scatter(): pl.pallas_call(attend_kernel, out_shape=(jax.ShapeDtypeStruct((rows, widt...]
where the time goes in v4:
time: 171 us; the launch traced here: 170 us
  Pallas kernels  169 us (99%)
    pallas_call x1, Pallas kernels, attend_scatter(): pl.pallas_call(attend_kernel, out_shape=(jax.ShapeDtypeStruct((rows, widt...  95.2 us
    pallas_call x1, Pallas kernels, gather_multiply(): pl.pallas_call(gather_kernel, out_shape=(jax.ShapeDtypeStruct((query_weig...  71.5 us

profile of v4, /device:TPU:0, one launch (start us, length us, event | category | flops | bytes accessed | tf_op | source)
XLA Modules:
  0.0 170.3 jit_solution(7680420334500291173)
XLA Ops:
  1.3 71.5 %gather_multiply.1 = (bf16[4,1024,128]{2,1,0:T(8,128)(2,1)}, bf16[2,2048,128]{2,1,0:T(8,128)(2,1)}, bf16[8,64,128]{2,1,0:T(8,128)(2,1)}, f32[8,64,128]{2,1,0:T(8...) custom-call(bf16[1,512]{1,0:T(2,128)(2,1)} %gain.1, bf16[8,8192]{1,0:T(8,128)(2,1)} %dec_q.1, s32[1,256]{1,0:T(1,128)} %bitcast.3, ...), custom_call_target="tpu_custom_call" | custom-call | flops 10737418240 | bytes 16777216 | tf_op jit(solution)/shard_map/gather_multiply/pallas_call | solution.py:389
  72.7 95.2 %attend_scatter.1 = (bf16[1024,512]{1,0:T(8,128)(2,1)}, bf16[8,8192]{1,0:T(8,128)(2,1)}) custom-call(bf16[4,1024,128]{2,1,0:T(8,128)(2,1)} %get-tuple-element.10.q, bf16[2,2048,128]{2,1,0:T(8,128)(2,1)} %get-tuple-element.11.kv, bf16[8,64,128]{2,1,0:T(8,128)(2,1)} %get-tuple-element.12.heads, f32[8,64,128]{2,1,0:T(8,128)} %get-tuple-element.13.old_sum, ...), custom_call_target="tpu_custom_call" | custom-call | flops 17179869184 | bytes 12582912 | tf_op jit(solution)/shard_map/attend_scatter/pallas_call | solution.py:938
  167.9 2.2 %hand_on.1 = (bf16[1024,512]{1,0:T(8,128)(2,1)}, bf16[8,8192]{1,0:T(8,128)(2,1)}) custom-call(bf16[1024,512]{1,0:T(8,128)(2,1)} %get-tuple-element.16.hidden, bf16[8,8192]{1,0:T(8,128)(2,1)} %get-tuple-element.17.dec), custom_call_target="tpu_custom_call" | custom-call | tf_op jit(solution)/shard_map/hand_on/pallas_call | solution.py:1015

commit v5 on v3

--- a/solution.py
+++ b/solution.py
@@ -70,7 +70,19 @@
 
 GATHER_CHUNKS = 4
 GAIN_ROWS = 16
+SHARE_ROWS = 40
 LOG_SCALE = math.log2(math.e) / math.sqrt(HD)
+
+
+def write_share(share, accum, top, total, low):
+    lane = lax.broadcasted_iota(jnp.int32, (8, HD), 1) // 16
+    stat = jnp.zeros((8, HD), F32)
+    for h in range(4):
+        rows = slice(low + h * 8, low + h * 8 + 8)
+        stat = jnp.where(lane == h, top[rows], stat)
+        stat = jnp.where(lane == 4 + h, total[rows], stat)
+    share[pl.ds(0, 32), :] = accum[low : low + 32]
+    share[pl.ds(32, 8), :] = stat
 
 
 def gather_kernel(
@@ -84,9 +96,7 @@
     cache_hbm,
     q_out,
     kv_out,
-    heads,
-    old_sum,
-    old_stat,
+    old_share,
     xall,
     cache,
     qw,
@@ -103,6 +113,8 @@
     sib_send,
     kv_send,
     kv_recv,
+    split_send,
+    split_recv,
 ):
     side, ring, core = here()
     rows_all, width = tok.shape
@@ -133,6 +145,7 @@
     load_x.wait()
 
     sends = []
+    split = GATHER_CHUNKS - 1
 
     def span(i, half=None):
         low = 0 if i == 0 else GAIN_ROWS + i * chunk
@@ -178,6 +191,9 @@
         if step == 2 and far == 0:
             landed(xall.at[slot, span(i, 0), :], recv_sem.at[kind, i], down)
             landed(xall.at[slot, span(i, 1), :], recv_sem.at[8, i], up)
+        elif i == split and far == 1 and step in (1, 3):
+            landed(xall.at[slot, span(i, 0), :], recv_sem.at[kind, i], up)
+            landed(xall.at[slot, span(i, 1), :], split_recv.at[step // 2], across)
         else:
             landed(xall.at[slot, span(i), :], recv_sem.at[kind, i], up)
 
@@ -201,7 +217,6 @@
         position = lax.broadcasted_iota(jnp.int32, (count, ctx), 1) + me * ctx
         parts = [dec_q[:, pl.ds((k * 8 + h) * HD, HD)].astype(F32) for h in range(8)]
         query = jnp.concatenate(parts, axis=0).astype(BF)
-        heads[k] = query
         found = jnp.full((count, ctx), NEG_BIG, F32)
         for seq in range(dec_seqs):
             score = lax.dot_general(
@@ -220,10 +235,9 @@
             accum = accum + jnp.dot(
                 own, cache[seq, :, pl.ds((2 * k + 1) * HD, HD)], preferred_element_type=F32
             )
-        old_sum[k] = accum
-        lane = lax.broadcasted_iota(jnp.int32, (count, HD), 1)
         total = jnp.sum(expo, axis=-1, keepdims=True)
-        old_stat[k] = jnp.where(lane < HD // 2, top, total)
+        for part in range(2):
+            write_share(old_share.at[2 * k + part], accum, top, total, part * 32)
 
     def event(name, i):
         if name == "O":
@@ -231,8 +245,9 @@
             return [(0, 0, i)]
         if name == "X":
             got(1, 0, i)
-            send(across, span(i), up_send.at[1, i], recv_sem.at[7, i], up)
-            send(across, span(i), down_send.at[1, i], recv_sem.at[5, i], down)
+            rows = span(i, 0) if i == split else span(i)
+            send(across, rows, up_send.at[1, i], recv_sem.at[7, i], up)
+            send(across, rows, down_send.at[1, i], recv_sem.at[5, i], down)
             to_sibling(1, 0, i)
             multiply(across, i)
             return [(1, 0, i)]
@@ -241,9 +256,13 @@
             got(far, 3, i)
             if far == 0:
                 send(at(0, 3), span(i, 0), up_send.at[2, i], recv_sem.at[2, i], up)
+                if i == split:
+                    send(at(0, 3), span(i, 1), split_send.at[1], split_recv.at[1], across)
             got(far, 1, i)
             if far == 0:
                 send(at(0, 1), span(i, 1), down_send.at[2, i], recv_sem.at[8, i], down)
+                if i == split:
+                    send(at(0, 1), span(i, 1), split_send.at[0], split_recv.at[0], across)
             to_sibling(far, 3, i)
             to_sibling(far, 1, i)
             multiply(at(far, 3), i)
@@ -298,19 +317,16 @@
     vmem = pl.BlockSpec(memory_space=pltpu.VMEM)
     dma = pltpu.SemaphoreType.DMA
     n = GATHER_CHUNKS
-    dec_rows = cache.shape[0] * 8
     return pl.pallas_call(
         gather_kernel,
         out_shape=(
             jax.ShapeDtypeStruct((query_weight.shape[1] // HD, rows, HD), BF),
             jax.ShapeDtypeStruct((2, kv_rows, HD), BF),
-            jax.ShapeDtypeStruct((KVH, dec_rows, HD), BF),
-            jax.ShapeDtypeStruct((KVH, dec_rows, HD), F32),
-            jax.ShapeDtypeStruct((KVH, dec_rows, HD), F32),
+            jax.ShapeDtypeStruct((shards, SHARE_ROWS, HD), F32),
         ),
         in_specs=[vmem, vmem, pl.BlockSpec(memory_space=pltpu.SMEM)]
         + [pl.BlockSpec(memory_space=pltpu.HBM)] * 5,
-        out_specs=(vmem,) * 5,
+        out_specs=(vmem,) * 3,
         scratch_shapes=[
             pltpu.VMEM((shards, rows + GAIN_ROWS, width), BF),
             pltpu.VMEM(cache.shape, BF),
@@ -328,6 +344,8 @@
             dma((8, n)),
             dma((n + 1,)),
             dma((n + 1,)),
+            dma((2,)),
+            dma((2,)),
         ],
         compiler_params=pltpu.CompilerParams(
             collective_id=1, has_side_effects=True, vmem_limit_bytes=62 * MIB
@@ -347,9 +365,8 @@
 def attend_kernel(
     q,
     kv,
-    heads,
-    old_sum,
-    old_stat,
+    dec_q,
+    old_share,
     owner,
     seq_of_page,
     live_len,
@@ -367,10 +384,8 @@
     last,
     far_in,
     tok,
-    pages,
-    first_stop,
-    fresh,
-    partial,
+    asked,
+    answers,
     shares,
     results,
     w_sem,
@@ -384,10 +399,10 @@
     last_recv,
     far_send,
     far_recv,
-    first_send,
-    first_recv,
-    fresh_send,
-    fresh_recv,
+    ask_send,
+    ask_recv,
+    answer_send,
+    answer_recv,
     share_send,
     share_recv,
     done_send,
@@ -429,7 +444,6 @@
 
     lax.fori_loop(1, shards, greet_shard, 0)
     lax.fori_loop(1, groups, greet_group, 0)
-    pl.semaphore_wait(barrier, shards + groups - 2)
 
     def copy_to(src, dst, send_sem, recv_sem, to):
         return pltpu.make_async_remote_copy(
@@ -441,31 +455,35 @@
             device_id_type=MESH,
         )
 
-    def first_copy(d):
-        to = lax.rem(shard + d, shards)
-        return copy_to(
-            pages.at[to], first_stop.at[shard], first_send.at[d], first_recv.at[d], {"tp": to}
-        )
-
-    def fresh_copy(d):
+    contract = (((1,), (1,)), ((), ()))
+    per = 4 * dec_seqs
+
+    def ask_copy(d):
         to = lax.rem(group + d, groups)
         return copy_to(
-            first_stop.at[:, to], fresh.at[group], fresh_send.at[d], fresh_recv.at[d], {"group": to}
+            asked.at[group], asked.at[group], ask_send.at[d], ask_recv.at[d], {"group": to}
+        )
+
+    def answer_copy(d):
+        to = lax.rem(group + d, groups)
+        return copy_to(
+            answers.at[to],
+            shares.at[shards + group],
+            answer_send.at[d],
+            answer_recv.at[d],
+            {"group": to},
         )
 
     def share_copy(d):
         to = lax.rem(shard + d, shards)
         return copy_to(
-            partial.at[to], shares.at[shard], share_send.at[d], share_recv.at[d], {"tp": to}
-        )
-
-    def result_of(of):
-        return results.at[:, pl.ds(pl.multiple_of(of * width, width), width)]
+            old_share.at[to], shares.at[shard], share_send.at[d], share_recv.at[d], {"tp": to}
+        )
 
     def done_copy(d):
         to = lax.rem(shard + d, shards)
         return copy_to(
-            result_of(shard), result_of(shard), done_send.at[d], done_recv.at[d], {"tp": to}
+            results.at[shard], results.at[shard], done_send.at[d], done_recv.at[d], {"tp": to}
         )
 
     def each(count, act):
@@ -475,13 +493,28 @@
 
         lax.fori_loop(1, count, body, 0)
 
-    def source(d, count, of):
-        return lax.rem(of + count - d, count)
+    def arrive(count, of, axis, place, send_sem, recv_sem):
+        def take(d):
+            frm = lax.rem(of + count - d, count)
+            ref = place(frm)
+            copy_to(ref, ref, send_sem.at[d], recv_sem.at[d], {axis: frm}).wait_recv()
+
+        each(count, take)
 
     def dec_begin():
+        parts = []
+        for h in range(4):
+            cols = pl.ds(pl.multiple_of(shard * width + h * HD, HD), HD)
+            parts.append(dec_q[:, cols].astype(F32))
+        asked[group] = jnp.concatenate(parts, axis=0).astype(BF)
+        each(groups, lambda d: ask_copy(d).start())
+        shares[shard] = old_share[shard]
+        each(shards, lambda d: share_copy(d).start())
+
+    def dec_answer():
+        arrive(groups, group, "group", lambda frm: asked.at[frm], ask_send, ask_recv)
+        count = owner.shape[1]
         old_rows = kv.shape[1] - rows_all
-        turn_of = lax.broadcasted_iota(jnp.int32, (1, rows_all), 1)
-        count = owner.shape[1]
         both = jnp.concatenate(
             [
                 jnp.broadcast_to(owner[...], (8, count)),
@@ -493,126 +526,57 @@
         page_of = lax.broadcasted_iota(jnp.int32, (count, rows_all), 1) // PAGE
         spread = jnp.where(page == page_of, 1.0, 0.0).astype(BF)
         by_token = jnp.dot(both.astype(BF), spread, preferred_element_type=F32).astype(jnp.int32)
-        names, seqs = by_token[0:1, :], by_token[8:9, :]
-        column = jnp.transpose(jnp.broadcast_to(owner[...].astype(F32), (HD, count)))
-        column = column[:, 0:1].astype(jnp.int32)
-        before = page < page_of
-        slot = jnp.sum(
-            jnp.where((column == names) & before, 1, 0), axis=0, keepdims=True
-        )
-        place = (lax.rem(names, shards) * groups + names // shards) * 16
-        spot = slot * PAGE + lax.rem(turn_of, PAGE)
-        live = turn_of // PAGE * PAGE < live_len[0]
-        target = jnp.where(live, place + spot, -1)
-        tag = jnp.where(live, place + 12, -1)
-        lane = lax.broadcasted_iota(jnp.int32, (HD, rows_all), 0)
-        mark = jnp.where(
-            (lane == group * 16 + spot) & (turn_of < live_len[0]), seqs + 1, 0
-        )
-        mark = mark.astype(F32).astype(BF)
-        block = 16 * groups
-
-        def fill(b, carry):
-            row = lax.broadcasted_iota(jnp.int32, (block, rows_all), 0) + b * block
-            chosen = jnp.where(row == target, 1.0, 0.0).astype(BF)
-            tagged = jnp.where(row == tag, 1.0, 0.0).astype(BF)
-            made = jnp.dot(
-                chosen, kv[core, pl.ds(old_rows, rows_all), :], preferred_element_type=F32
-            ) + lax.dot_general(tagged, mark, contract, preferred_element_type=F32)
-            pages[b] = made.astype(BF).reshape(groups, 16, HD)
-            return carry
-
-        lax.fori_loop(0, shards, fill, 0)
-        first_stop[shard] = pages[shard]
-        each(shards, lambda d: first_copy(d).start())
-
-    def dec_forward():
-        def take(d):
-            frm = source(d, shards, shard)
-            ref = first_stop.at[frm]
-            copy_to(ref, ref, first_send.at[d], first_recv.at[d], {"tp": frm}).wait_recv()
-
-        each(shards, take)
-        fresh[group] = first_stop[:, pl.ds(group, 1)].reshape(shards, 16, HD)
-        each(groups, lambda d: fresh_copy(d).start())
-
-    def dec_arrive():
-        def take(d):
-            frm = source(d, groups, group)
-            ref = fresh.at[frm]
-            copy_to(ref, ref, fresh_send.at[d], fresh_recv.at[d], {"group": frm}).wait_recv()
-
-        each(groups, take)
-
-    contract = (((1,), (1,)), ((), ()))
-
-    count = dec_seqs * 8
-    seq_row = lax.rem(lax.broadcasted_iota(jnp.int32, (count, HD), 0), 8)
-
-    def dec_settle(k):
-        spots = fresh.shape[0] * 16
-        mark = fresh[0, 0].astype(F32)
-        for g in range(1, fresh.shape[0]):
-            mark = mark + fresh[g, 0].astype(F32)
-        mark = mark[12:13, :]
-        held = mark == (seq_row + 1).astype(F32)
-        key = fresh[:, pl.ds(2 * k, 1)].reshape(spots, HD)
-        value = fresh[:, pl.ds(2 * k + 1, 1)].reshape(spots, HD)
-        new = lax.dot_general(heads[k], key, contract, preferred_element_type=F32)
-        new = jnp.where(held, new * LOG_SCALE, NEG_BIG)
-        old_top = old_stat[k, :, pl.ds(0, 1)]
-        old_total = old_stat[k, :, pl.ds(HD // 2, 1)]
-        top = jnp.maximum(jnp.max(new, axis=-1, keepdims=True), old_top)
-        new = jnp.where(held, jnp.exp2(new - top), 0.0)
-        keep = jnp.exp2(old_top - top)
-        total = jnp.sum(new, axis=-1, keepdims=True) + keep * old_total
-        accum = jnp.dot(new.astype(BF), value, preferred_element_type=F32) + keep * old_sum[k]
-        lane = lax.broadcasted_iota(jnp.int32, (8, HD), 1) // 16
-        for half_of_heads in range(2):
-            low = half_of_heads * 32
-            stat = jnp.zeros((8, HD), F32)
-            for h in range(4):
-                rows = slice(low + h * 8, low + h * 8 + 8)
-                stat = jnp.where(lane == h, top[rows], stat)
-                stat = jnp.where(lane == 4 + h, total[rows], stat)
-            partial[2 * k + half_of_heads, pl.ds(0, 32), :] = accum[low : low + 32]
-            partial[2 * k + half_of_heads, pl.ds(32, 8), :] = stat
-
-    def dec_share():
-        shares[shard] = partial[shard]
-        each(shards, lambda d: share_copy(d).start())
+        token = lax.broadcasted_iota(jnp.int32, (1, rows_all), 1)
+        code = by_token[0:1, :] // shards * dec_seqs + by_token[8:9, :]
+        code = jnp.where(token < live_len[0], code, -1)
+        row = lax.broadcasted_iota(jnp.int32, (groups * per, rows_all), 0)
+        held = code == row // per * dec_seqs + lax.rem(row, dec_seqs)
+        query = asked[...].reshape(groups * per, HD)
+        score = lax.dot_general(
+            query, kv[0, pl.ds(old_rows, rows_all), :], contract, preferred_element_type=F32
+        )
+        score = jnp.where(held, score * LOG_SCALE, NEG_BIG)
+        top = jnp.max(score, axis=-1, keepdims=True)
+        expo = jnp.where(held, jnp.exp2(score - top), 0.0)
+        total = jnp.sum(expo, axis=-1, keepdims=True)
+        accum = jnp.dot(
+            expo.astype(BF), kv[1, pl.ds(old_rows, rows_all), :], preferred_element_type=F32
+        )
+        for g in range(answers.shape[0]):
+            write_share(answers.at[g], accum, top, total, g * per)
+        shares[shards + group] = answers[group]
+        each(groups, lambda d: answer_copy(d).start())
 
     def dec_combine():
-        def take(d):
-            frm = source(d, shards, shard)
-            ref = shares.at[frm]
-            copy_to(ref, ref, share_send.at[d], share_recv.at[d], {"tp": frm}).wait_recv()
-
-        each(shards, take)
+        arrive(shards, shard, "tp", lambda frm: shares.at[frm], share_send, share_recv)
+        arrive(
+            groups, group, "group", lambda frm: shares.at[shards + frm], answer_send, answer_recv
+        )
         stat = shares[:, pl.ds(32, 8), :]
-        lane = lax.broadcasted_iota(jnp.int32, (shards, 8, HD), 2) // 16
+        lane = lax.broadcasted_iota(jnp.int32, stat.shape, 2) // 16
+        parts = []
         for h in range(4):
             top = jnp.max(jnp.where(lane == h, stat, NEG_BIG), axis=-1, keepdims=True)
             total = jnp.max(jnp.where(lane == 4 + h, stat, 0.0), axis=-1, keepdims=True)
             factor = jnp.exp2(top - jnp.max(top, axis=0, keepdims=True))
             whole = jnp.sum(factor * total, axis=0)
             accum = jnp.sum(factor * shares[:, pl.ds(h * 8, 8), :], axis=0)
-            cols = pl.ds(pl.multiple_of(shard * width + h * HD, HD), HD)
-            results[:, cols] = accum / whole
+            parts.append(accum / whole)
+        results[shard] = jnp.concatenate(parts, axis=0).astype(BF)
         each(shards, lambda d: done_copy(d).start())
 
     def dec_end():
-        def take(d):
-            frm = source(d, shards, shard)
-            ref = result_of(frm)
-            copy_to(ref, ref, done_send.at[d], done_recv.at[d], {"tp": frm}).wait_recv()
-
-        each(shards, take)
-        dec_out[...] = results[...].astype(BF)
-        for copy in (first_copy, share_copy, done_copy):
+        arrive(shards, shard, "tp", lambda frm: results.at[frm], done_send, done_recv)
+        for t in range(results.shape[0]):
+            block = results[t].astype(F32)
+            for h in range(4):
+                dec_out[:, (t * 4 + h) * HD : (t * 4 + h + 1) * HD] = block[
+                    h * 8 : h * 8 + 8
+                ].astype(BF)
+        for copy in (share_copy, done_copy):
             each(shards, lambda d, copy=copy: copy(d).wait_send())
-        each(groups, lambda d: fresh_copy(d).wait_send())
-
+        for copy in (ask_copy, answer_copy):
+            each(groups, lambda d, copy=copy: copy(d).wait_send())
 
     def rows_of(j):
         return pl.ds(pl.multiple_of(j * chunk, chunk), chunk)
@@ -657,7 +621,7 @@
     def term(far, step, other):
         slot = at(far, step, other)
         cols = pl.ds(pl.multiple_of(slot * width, width), width)
-        return jnp.dot(att[...], wo[:, cols], preferred_element_type=F32).astype(BF)
+        return jnp.dot(att[...], wo[:, cols], preferred_element_type=F32)
 
     def add_into(dst, src):
         dst[...] = (dst[...].astype(F32) + src[...].astype(F32)).astype(BF)
@@ -717,33 +681,36 @@
             device_id_type=MESH,
         )
 
-    kinds = ((1, 2), (0, 2), (1, 1), (1, 3), (0, 1), (0, 3), (1, 0), (0, 0))
-    lag = 2
+    kinds = ((1, 2), (1, 1), (1, 3), (0, 2), (0, 1), (0, 3), (1, 0), (0, 0))
+    ahead = 4
 
     def produce(j):
         rows = rows_of(j)
-        for k in range(len(kinds) + lag):
-            if k < len(kinds):
-                far, step = kinds[k]
-                kind = far * 4 + step
-                lend[kind, rows, :] = term(far, step, 1)
-                lend_copy(kind, j).start()
-                mine[kind, rows, :] = term(far, step, 0)
-            if k >= lag:
-                far, step = kinds[k - lag]
-                kind = far * 4 + step
-                lend_copy(kind, j).wait_recv()
-                add_into(mine.at[kind, rows, :], borrowed.at[kind, rows, :])
-                if (far, step) == (1, 2):
-                    far_copy(j).start()
-                if step == 1:
-                    near_copy(far, 0, 1, j).start()
-                    if far:
-                        near_copy(far, 0, 0, j).start()
-                if step == 3:
-                    near_copy(far, 1, 0, j).start()
-                    if far:
-                        near_copy(far, 1, 1, j).start()
+
+        def offer(far, step):
+            kind = far * 4 + step
+            lend[kind, rows, :] = term(far, step, 1).astype(BF)
+            lend_copy(kind, j).start()
+
+        for far, step in kinds[:ahead]:
+            offer(far, step)
+        for k, (far, step) in enumerate(kinds):
+            if k + ahead < len(kinds):
+                offer(*kinds[k + ahead])
+            kind = far * 4 + step
+            own = term(far, step, 0)
+            lend_copy(kind, j).wait_recv()
+            mine[kind, rows, :] = (own + borrowed[kind, rows, :].astype(F32)).astype(BF)
+            if (far, step) == (1, 2):
+                far_copy(j).start()
+            if step == 1:
+                near_copy(far, 0, 1, j).start()
+                if far:
+                    near_copy(far, 0, 0, j).start()
+            if step == 3:
+                near_copy(far, 1, 0, j).start()
+                if far:
+                    near_copy(far, 1, 1, j).start()
 
     def pass_on(j):
         far_copy(j).wait_recv()
@@ -786,8 +753,12 @@
             )
         ).astype(BF)
 
+    pl.semaphore_wait(barrier, shards + groups - 2)
+    dec_begin()
+    attend(0, old, 2 * chunk)
+
     def turn(j, carry):
-        @pl.when(j < n)
+        @pl.when((j >= 1) & (j < n))
         def _():
             attention(j)
 
@@ -818,31 +789,15 @@
 
         @pl.when(j == 1)
         def _():
-            dec_begin()
-
-        @pl.when(j == 3)
+            dec_answer()
+
+        @pl.when(j == 4)
         def _():
-            dec_forward()
-
-        @pl.when(j == 5)
-        def _():
-            dec_arrive()
-
-        @pl.when((j >= 5) & (j < 7))
-        def _():
-            def settle(k, carry):
-                dec_settle(k)
-                return carry
-
-            lax.fori_loop((j - 5) * 4, (j - 4) * 4, settle, 0)
-
-        @pl.when(j == 6)
-        def _():
-            dec_share()
+            dec_combine()
 
         @pl.when(j == 8)
         def _():
-            dec_combine()
+            dec_end()
 
         return carry
 
@@ -862,17 +817,16 @@
         return carry
 
     lax.fori_loop(0, n, drain, 0)
-    dec_end()
 
 
 def attend_scatter(
-    tokens, queries, kv, heads, old_sum, old_stat, owner, seq_of_page, live_len, out_weight, groups
+    tokens, queries, kv, dec_q, old_share, owner, seq_of_page, live_len, out_weight, groups
 ):
     rows, width = tokens.shape
     vmem = pl.BlockSpec(memory_space=pltpu.VMEM)
     dma = pltpu.SemaphoreType.DMA
     n = SCATTER_CHUNKS
-    seqs = heads.shape[1] // 8
+    seqs = dec_q.shape[0]
     shards = 2 * RING * SIDES
     return pl.pallas_call(
         attend_kernel,
@@ -881,7 +835,6 @@
             jax.ShapeDtypeStruct((seqs, HEADS * HD), BF),
         ),
         in_specs=[
-            vmem,
             vmem,
             vmem,
             vmem,
@@ -904,12 +857,10 @@
             pltpu.VMEM((rows, width), BF),
             pltpu.VMEM((rows, width), BF),
             pltpu.VMEM((rows, width), BF),
-            pltpu.VMEM((shards, groups, 16, HD), BF),
-            pltpu.VMEM((shards, groups, 16, HD), BF),
-            pltpu.VMEM((groups, shards, 16, HD), BF),
-            pltpu.VMEM((shards, 40, HD), F32),
-            pltpu.VMEM((shards, 40, HD), F32),
-            pltpu.VMEM((seqs, HEADS * HD), F32),
+            pltpu.VMEM((groups, 4 * seqs, HD), BF),
+            pltpu.VMEM((groups, SHARE_ROWS, HD), F32),
+            pltpu.VMEM((shards + groups, SHARE_ROWS, HD), F32),
+            pltpu.VMEM((shards, 4 * seqs, HD), BF),
             dma((2,)),
             dma((8, n)),
             dma((8, n)),
@@ -921,8 +872,8 @@
             dma((n,)),
             dma((n,)),
             dma((n,)),
-            dma((shards,)),
-            dma((shards,)),
+            dma((groups,)),
+            dma((groups,)),
             dma((groups,)),
             dma((groups,)),
             dma((shards,)),
@@ -939,7 +890,7 @@
             transcendentals=4 * rows * kv.shape[1],
         ),
         name="attend_scatter",
-    )(queries, kv, heads, old_sum, old_stat, owner, seq_of_page, live_len, tokens, out_weight)
+    )(queries, kv, dec_q, old_share, owner, seq_of_page, live_len, tokens, out_weight)
 
 
 def hand_on_kernel(hidden, dec, hidden_out, dec_out, sem):
@@ -981,16 +932,15 @@
     dec_cache,
     dec_len,
 ):
-    queries, kv_both, heads, old_sum, old_stat = gather_multiply(
+    queries, kv_both, old_share = gather_multiply(
         tokens, norm_gain, prefix_cache, query_weight, kv_weight, dec_queries, dec_len, dec_cache
     )
     hidden_out, dec_out = attend_scatter(
         tokens,
         queries,
         kv_both,
-        heads,
-        old_sum,
-        old_stat,
+        dec_queries,
+        old_share,
         page_owner.reshape(1, -1),
         page_seq.reshape(1, -1),
         prompt_len,

time: 179 us -> 159 us (0.89)
  Pallas kernels: 177 us -> 157 us
    pallas_call x1, Pallas kernels: 102 us -> 84.1 us  [attend_scatter(): pl.pallas_call(attend_kernel, out_shape=(jax.ShapeDtypeStruct((rows, widt...]
where the time goes in v5:
time: 159 us
  Pallas kernels  157 us (99%)
    pallas_call x1, Pallas kernels, attend_scatter(): pl.pallas_call(attend_kernel, out_shape=(jax.ShapeDtypeStruct((rows, widt...  84.1 us
    pallas_call x1, Pallas kernels, gather_multiply(): pl.pallas_call(gather_kernel, out_shape=(jax.ShapeDtypeStruct((query_weig...  71 us

profile of v5, /device:TPU:0, one launch (start us, length us, event | category | flops | bytes accessed | tf_op | source)
XLA Modules:
  0.0 158.9 jit_solution(15267428198384628244)
XLA Ops:
  1.3 71.0 %gather_multiply.1 = (bf16[4,1024,128]{2,1,0:T(8,128)(2,1)}, bf16[2,2048,128]{2,1,0:T(8,128)(2,1)}, f32[16,40,128]{2,1,0:T(8,128)}) custom-call(bf16[1,512]{1,0:T(2,128)(2,1)} %gain.1, bf16[8,8192]{1,0:T(8,128)(2,1)} %dec_q.3, s32[8]{0:T(128)} %dec_len.1, bf16[1024,512]{1,0:T(8,128)(2,1)} %tok_hbm.1, bf16[1024,128]{1,0:T(8,128)(2,1)} %prefix.1, ...), custom_call_target="tpu_custom_call" | custom-call | flops 10737418240 | bytes 16777216 | tf_op jit(solution)/shard_map/gather_multiply/pallas_call | solution.py:320
  72.3 84.1 %attend_scatter.1 = (bf16[1024,512]{1,0:T(8,128)(2,1)}, bf16[8,8192]{1,0:T(8,128)(2,1)}) custom-call(bf16[4,1024,128]{2,1,0:T(8,128)(2,1)} %get-tuple-element.7.q, bf16[2,2048,128]{2,1,0:T(8,128)(2,1)} %get-tuple-element.8.kv, bf16[8,8192]{1,0:T(8,128)(2,1)} %dec_q.3, f32[16,40,128]{2,1,0:T(8,128)} %get-tuple-element.9.old_share, s32[1,256]{1,0:T(1,128)} %bitcast.2, ...), custom_call_target="tpu_custom_call" | custom-call | flops 17179869184 | bytes 12582912 | tf_op jit(solution)/shard_map/attend_scatter/pallas_call | solution.py:831
  156.4 2.2 %hand_on.1 = (bf16[1024,512]{1,0:T(8,128)(2,1)}, bf16[8,8192]{1,0:T(8,128)(2,1)}) custom-call(bf16[1024,512]{1,0:T(8,128)(2,1)} %get-tuple-element.10.hidden, bf16[8,8192]{1,0:T(8,128)(2,1)} %get-tuple-element.11.dec), custom_call_target="tpu_custom_call" | custom-call | tf_op jit(solution)/shard_map/hand_on/pallas_call | solution.py:908

commit v6 on v5

--- a/solution.py
+++ b/solution.py
@@ -280,18 +280,7 @@
         ("X", 0), ("X", 1), ("X", 2), ("X", 3), ("F", 0), ("F", 1), ("F", 2), ("F", 3),
         ("P", 0), ("P", 1), ("G", 0), ("P", 2), ("G", 1), ("G", 2), ("P", 3), ("G", 3),
     )
-    late = []
-    for name, i in order:
-        fresh = event(name, i)
-        if name in ("Z", "X"):
-            dec_old(i + (4 if name == "X" else 0))
-        for item in late:
-            from_sibling(*item)
-        late = fresh
-    for item in late:
-        from_sibling(*item)
-
-    for i in range(GATHER_CHUNKS):
+    def settle(i):
         rows = pl.ds(i * chunk, chunk)
         total = jnp.sum(power[rows, :], axis=-1, keepdims=True) / (width * 2 * RING * SIDES)
         factor = lax.rsqrt(total + EPSILON)
@@ -302,6 +291,21 @@
         queries = (acc_q[rows, :] * (factor * LOG_SCALE)).astype(BF)
         for h in range(q_out.shape[0]):
             q_out[h, rows, :] = queries[:, h * HD : (h + 1) * HD]
+
+    late = []
+    for name, i in order:
+        fresh = event(name, i)
+        if name in ("Z", "X"):
+            dec_old(i + (4 if name == "X" else 0))
+        for item in late:
+            from_sibling(*item)
+        for far, step, k in late:
+            if (far, step) == (1, 2):
+                settle(k)
+        late = fresh
+    for item in late:
+        from_sibling(*item)
+    settle(GATHER_CHUNKS - 1)
     landed(kv_out.at[1 - core, pl.ds(0, prefix_rows), :], kv_recv.at[0], sib)
     for i in range(GATHER_CHUNKS):
         new = pl.ds(prefix_rows + i * chunk, chunk)
@@ -753,9 +757,8 @@
             )
         ).astype(BF)
 
+    attend(0, old, 2 * chunk)
     pl.semaphore_wait(barrier, shards + groups - 2)
-    dec_begin()
-    attend(0, old, 2 * chunk)
 
     def turn(j, carry):
         @pl.when((j >= 1) & (j < n))
@@ -787,11 +790,15 @@
         def _():
             finish(j - 4)
 
-        @pl.when(j == 1)
+        @pl.when(j == 0)
+        def _():
+            dec_begin()
+
+        @pl.when(j == 2)
         def _():
             dec_answer()
 
-        @pl.when(j == 4)
+        @pl.when(j == 5)
         def _():
             dec_combine()
 

time: 159 us -> 157 us (0.987)
    pallas_call x1, Pallas kernels: 84.1 us -> 82.3 us  [attend_scatter(): pl.pallas_call(attend_kernel, out_shape=(jax.ShapeDtypeStruct((rows, widt...]
where the time goes in v6:
time: 157 us
  Pallas kernels  156 us (99%)
    pallas_call x1, Pallas kernels, attend_scatter(): pl.pallas_call(attend_kernel, out_shape=(jax.ShapeDtypeStruct((rows, widt...  82.3 us
    pallas_call x1, Pallas kernels, gather_multiply(): pl.pallas_call(gather_kernel, out_shape=(jax.ShapeDtypeStruct((query_weig...  71 us

profile of v6, /device:TPU:0, one launch (start us, length us, event | category | flops | bytes accessed | tf_op | source)
XLA Modules:
  0.0 157.0 jit_solution(11307599707960313793)
XLA Ops:
  1.3 71.0 %gather_multiply.1 = (bf16[4,1024,128]{2,1,0:T(8,128)(2,1)}, bf16[2,2048,128]{2,1,0:T(8,128)(2,1)}, f32[16,40,128]{2,1,0:T(8,128)}) custom-call(bf16[1,512]{1,0:T(2,128)(2,1)} %gain.1, bf16[8,8192]{1,0:T(8,128)(2,1)} %dec_q.3, s32[8]{0:T(128)} %dec_len.1, bf16[1024,512]{1,0:T(8,128)(2,1)} %tok_hbm.1, bf16[1024,128]{1,0:T(8,128)(2,1)} %prefix.1, ...), custom_call_target="tpu_custom_call" | custom-call | flops 10737418240 | bytes 16777216 | tf_op jit(solution)/shard_map/gather_multiply/pallas_call | solution.py:324
  72.3 82.3 %attend_scatter.1 = (bf16[1024,512]{1,0:T(8,128)(2,1)}, bf16[8,8192]{1,0:T(8,128)(2,1)}) custom-call(bf16[4,1024,128]{2,1,0:T(8,128)(2,1)} %get-tuple-element.7.q, bf16[2,2048,128]{2,1,0:T(8,128)(2,1)} %get-tuple-element.8.kv, bf16[8,8192]{1,0:T(8,128)(2,1)} %dec_q.3, f32[16,40,128]{2,1,0:T(8,128)} %get-tuple-element.9.old_share, s32[1,256]{1,0:T(1,128)} %bitcast.2, ...), custom_call_target="tpu_custom_call" | custom-call | flops 17179869184 | bytes 12582912 | tf_op jit(solution)/shard_map/attend_scatter/pallas_call | solution.py:838
  154.6 2.2 %hand_on.1 = (bf16[1024,512]{1,0:T(8,128)(2,1)}, bf16[8,8192]{1,0:T(8,128)(2,1)}) custom-call(bf16[1024,512]{1,0:T(8,128)(2,1)} %get-tuple-element.10.hidden, bf16[8,8192]{1,0:T(8,128)(2,1)} %get-tuple-element.11.dec), custom_call_target="tpu_custom_call" | custom-call | tf_op jit(solution)/shard_map/hand_on/pallas_call | solution.py:915

commit v7 on v6

--- a/solution.py
+++ b/solution.py
@@ -364,6 +364,7 @@
 
 
 SCATTER_CHUNKS = 8
+SIDE_CHUNK = 1
 
 
 def attend_kernel(
@@ -387,6 +388,7 @@
     near,
     last,
     far_in,
+    side_in,
     tok,
     asked,
     answers,
@@ -403,6 +405,8 @@
     last_recv,
     far_send,
     far_recv,
+    side_send,
+    side_recv,
     ask_send,
     ask_recv,
     answer_send,
@@ -707,16 +711,40 @@
             mine[kind, rows, :] = (own + borrowed[kind, rows, :].astype(F32)).astype(BF)
             if (far, step) == (1, 2):
                 far_copy(j).start()
-            if step == 1:
-                near_copy(far, 0, 1, j).start()
+            if step in (1, 3):
+
+                @pl.when(j != SIDE_CHUNK)
+                def _(far=far, way=step // 2):
+                    near_copy(far, way, 1 - way, j).start()
+                    if far:
+                        near_copy(far, way, way, j).start()
+
                 if far:
-                    near_copy(far, 0, 0, j).start()
-            if step == 3:
-                near_copy(far, 1, 0, j).start()
-                if far:
-                    near_copy(far, 1, 1, j).start()
+
+                    @pl.when(j == SIDE_CHUNK)
+                    def _(way=step // 2):
+                        side_copy(way).start()
+
+
+    def side_copy(way):
+        rows = pl.ds(SIDE_CHUNK * chunk, chunk)
+        return pltpu.make_async_remote_copy(
+            src_ref=mine.at[7 if way else 5, rows, :],
+            dst_ref=side_in.at[way],
+            send_sem=side_send.at[way],
+            recv_sem=side_recv.at[way],
+            device_id={"tp": across},
+            device_id_type=MESH,
+        )
 
     def pass_on(j):
+        @pl.when(j == SIDE_CHUNK)
+        def _():
+            for way in (0, 1):
+                side_copy(way).wait_recv()
+                add_into(mine.at[3 if way else 1, rows_of(j), :], side_in.at[way])
+                near_copy(0, way, 1 - way, j).start()
+
         far_copy(j).wait_recv()
         rows = rows_of(j)
         add_into(mine.at[2, rows, :], far_in.at[rows, :])
@@ -736,11 +764,17 @@
                 near_copy(far, way, k, j).wait_recv()
 
     def cross(j):
-        near_wait(1, j)
         rows = rows_of(j)
-        mine[4, rows, :] = (
-            mine[4, rows, :].astype(F32) + near[2, rows, :].astype(F32) + near[3, rows, :].astype(F32)
-        ).astype(BF)
+
+        @pl.when(j != SIDE_CHUNK)
+        def _():
+            near_wait(1, j)
+            mine[4, rows, :] = (
+                mine[4, rows, :].astype(F32)
+                + near[2, rows, :].astype(F32)
+                + near[3, rows, :].astype(F32)
+            ).astype(BF)
+
         last_copy(j).start()
 
     def finish(j):
@@ -813,10 +847,16 @@
     def drain(j, carry):
         for kind in range(8):
             lend_copy(kind, j).wait_send()
-        for far in (0, 1):
+        for way in (0, 1):
+            for k in (0, 1):
+                near_copy(0, way, k, j).wait_send()
+
+        @pl.when(j != SIDE_CHUNK)
+        def _():
             for way in (0, 1):
                 for k in (0, 1):
-                    near_copy(far, way, k, j).wait_send()
+                    near_copy(1, way, k, j).wait_send()
+
         last_copy(j).wait_send()
         far_copy(j).wait_send()
         mid_copy(0, j).wait_send()
@@ -824,6 +864,8 @@
         return carry
 
     lax.fori_loop(0, n, drain, 0)
+    side_copy(0).wait_send()
+    side_copy(1).wait_send()
 
 
 def attend_scatter(
@@ -863,6 +905,7 @@
             pltpu.VMEM((4, rows, width), BF),
             pltpu.VMEM((rows, width), BF),
             pltpu.VMEM((rows, width), BF),
+            pltpu.VMEM((2, rows // n, width), BF),
             pltpu.VMEM((rows, width), BF),
             pltpu.VMEM((groups, 4 * seqs, HD), BF),
             pltpu.VMEM((groups, SHARE_ROWS, HD), F32),
@@ -879,6 +922,8 @@
             dma((n,)),
             dma((n,)),
             dma((n,)),
+            dma((2,)),
+            dma((2,)),
             dma((groups,)),
             dma((groups,)),
             dma((groups,)),
@@ -900,17 +945,24 @@
     )(queries, kv, dec_q, old_share, owner, seq_of_page, live_len, tokens, out_weight)
 
 
-def hand_on_kernel(hidden, dec, hidden_out, dec_out, sem):
-    first = pltpu.make_async_copy(hidden, hidden_out, sem.at[0])
-    second = pltpu.make_async_copy(dec, dec_out, sem.at[1])
-    first.start()
-    second.start()
-    first.wait()
-    second.wait()
+def hand_on_kernel(hidden, dec, hidden_out, dec_out, buffer, dec_buffer, sem_in, sem_out):
+    part = hidden.shape[0] // 4
+    moves = [(dec, dec_buffer, dec_out)]
+    for k in range(4):
+        rows = pl.ds(k * part, part)
+        moves.append((hidden.at[rows], buffer.at[rows], hidden_out.at[rows]))
+    loads = [pltpu.make_async_copy(a, b, sem_in.at[k]) for k, (a, b, _) in enumerate(moves)]
+    stores = [pltpu.make_async_copy(b, c, sem_out.at[k]) for k, (_, b, c) in enumerate(moves)]
+    for load in loads:
+        load.start()
+    for load, store in zip(loads, stores):
+        load.wait()
+        store.start()
+    for store in stores:
+        store.wait()
 
 
 def hand_on(hidden, dec):
-    vmem = pl.BlockSpec(memory_space=pltpu.VMEM)
     hbm = pl.BlockSpec(memory_space=pltpu.HBM)
     return pl.pallas_call(
         hand_on_kernel,
@@ -918,9 +970,14 @@
             jax.ShapeDtypeStruct(hidden.shape, hidden.dtype),
             jax.ShapeDtypeStruct(dec.shape, dec.dtype),
         ),
-        in_specs=[vmem, vmem],
+        in_specs=[hbm, hbm],
         out_specs=(hbm, hbm),
-        scratch_shapes=[pltpu.SemaphoreType.DMA((2,))],
+        scratch_shapes=[
+            pltpu.VMEM(hidden.shape, hidden.dtype),
+            pltpu.VMEM(dec.shape, dec.dtype),
+            pltpu.SemaphoreType.DMA((5,)),
+            pltpu.SemaphoreType.DMA((5,)),
+        ],
         name="hand_on",
     )(hidden, dec)
 

time: 157 us -> 163 us (1.038)
  Pallas kernels: 156 us -> 161 us
    pallas_call x1, Pallas kernels: 82.3 us -> 88 us  [attend_scatter(): pl.pallas_call(attend_kernel, out_shape=(jax.ShapeDtypeStruct((rows, widt...]
where the time goes in v7:
time: 163 us
  Pallas kernels  161 us (99%)
    pallas_call x1, Pallas kernels, attend_scatter(): pl.pallas_call(attend_kernel, out_shape=(jax.ShapeDtypeStruct((rows, widt...  88 us
    pallas_call x1, Pallas kernels, gather_multiply(): pl.pallas_call(gather_kernel, out_shape=(jax.ShapeDtypeStruct((query_weig...  71 us

profile of v7, /device:TPU:0, one launch (start us, length us, event | category | flops | bytes accessed | tf_op | source)
XLA Modules:
  0.0 162.5 jit_solution(4237700026816417730)
XLA Ops:
  1.3 71.0 %gather_multiply.1 = (bf16[4,1024,128]{2,1,0:T(8,128)(2,1)}, bf16[2,2048,128]{2,1,0:T(8,128)(2,1)}, f32[16,40,128]{2,1,0:T(8,128)}) custom-call(bf16[1,512]{1,0:T(2,128)(2,1)} %gain.1, bf16[8,8192]{1,0:T(8,128)(2,1)} %dec_q.3, s32[8]{0:T(128)} %dec_len.1, bf16[1024,512]{1,0:T(8,128)(2,1)} %tok_hbm.1, bf16[1024,128]{1,0:T(8,128)(2,1)} %prefix.1, ...), custom_call_target="tpu_custom_call" | custom-call | flops 10737418240 | bytes 16777216 | tf_op jit(solution)/shard_map/gather_multiply/pallas_call | solution.py:324
  72.3 88.0 %attend_scatter.1 = (bf16[1024,512]{1,0:T(8,128)(2,1)}, bf16[8,8192]{1,0:T(8,128)(2,1)}) custom-call(bf16[4,1024,128]{2,1,0:T(8,128)(2,1)} %get-tuple-element.7.q, bf16[2,2048,128]{2,1,0:T(8,128)(2,1)} %get-tuple-element.8.kv, bf16[8,8192]{1,0:T(8,128)(2,1)} %dec_q.3, f32[16,40,128]{2,1,0:T(8,128)} %get-tuple-element.9.old_share, s32[1,256]{1,0:T(1,128)} %bitcast.2, ...), custom_call_target="tpu_custom_call" | custom-call | flops 17179869184 | bytes 12582912 | tf_op jit(solution)/shard_map/attend_scatter/pallas_call | solution.py:880
  160.3 2.1 %hand_on.1 = (bf16[1024,512]{1,0:T(8,128)(2,1)}, bf16[8,8192]{1,0:T(8,128)(2,1)}) custom-call(bf16[1024,512]{1,0:T(8,128)(2,1)} %get-tuple-element.10.hidden, bf16[8,8192]{1,0:T(8,128)(2,1)} %get-tuple-element.11.dec), custom_call_target="tpu_custom_call" | custom-call | tf_op jit(solution)/shard_map/hand_on/pallas_call | solution.py:967

commit v8 on v6

--- a/solution.py
+++ b/solution.py
@@ -770,25 +770,25 @@
             load.wait()
             load_tok.wait()
 
+        @pl.when(j < n)
+        def _():
+            produce(j)
+
         @pl.when((j >= 1) & (j < n + 1))
         def _():
             pass_on(j - 1)
 
-        @pl.when(j < n)
-        def _():
-            produce(j)
-
-        @pl.when((j >= 2) & (j < n + 2))
-        def _():
-            relay(j - 2)
-
         @pl.when((j >= 3) & (j < n + 3))
         def _():
-            cross(j - 3)
-
-        @pl.when(j >= 4)
-        def _():
-            finish(j - 4)
+            relay(j - 3)
+
+        @pl.when((j >= 4) & (j < n + 4))
+        def _():
+            cross(j - 4)
+
+        @pl.when(j >= 5)
+        def _():
+            finish(j - 5)
 
         @pl.when(j == 0)
         def _():
@@ -808,7 +808,7 @@
 
         return carry
 
-    lax.fori_loop(0, n + 4, turn, 0)
+    lax.fori_loop(0, n + 5, turn, 0)
 
     def drain(j, carry):
         for kind in range(8):
@@ -900,17 +900,24 @@
     )(queries, kv, dec_q, old_share, owner, seq_of_page, live_len, tokens, out_weight)
 
 
-def hand_on_kernel(hidden, dec, hidden_out, dec_out, sem):
-    first = pltpu.make_async_copy(hidden, hidden_out, sem.at[0])
-    second = pltpu.make_async_copy(dec, dec_out, sem.at[1])
-    first.start()
-    second.start()
-    first.wait()
-    second.wait()
+def hand_on_kernel(hidden, dec, hidden_out, dec_out, buffer, dec_buffer, sem_in, sem_out):
+    part = hidden.shape[0] // 4
+    moves = [(dec, dec_buffer, dec_out)]
+    for k in range(4):
+        rows = pl.ds(k * part, part)
+        moves.append((hidden.at[rows], buffer.at[rows], hidden_out.at[rows]))
+    loads = [pltpu.make_async_copy(a, b, sem_in.at[k]) for k, (a, b, _) in enumerate(moves)]
+    stores = [pltpu.make_async_copy(b, c, sem_out.at[k]) for k, (_, b, c) in enumerate(moves)]
+    for load in loads:
+        load.start()
+    for load, store in zip(loads, stores):
+        load.wait()
+        store.start()
+    for store in stores:
+        store.wait()
 
 
 def hand_on(hidden, dec):
-    vmem = pl.BlockSpec(memory_space=pltpu.VMEM)
     hbm = pl.BlockSpec(memory_space=pltpu.HBM)
     return pl.pallas_call(
         hand_on_kernel,
@@ -918,9 +925,14 @@
             jax.ShapeDtypeStruct(hidden.shape, hidden.dtype),
             jax.ShapeDtypeStruct(dec.shape, dec.dtype),
         ),
-        in_specs=[vmem, vmem],
+        in_specs=[hbm, hbm],
         out_specs=(hbm, hbm),
-        scratch_shapes=[pltpu.SemaphoreType.DMA((2,))],
+        scratch_shapes=[
+            pltpu.VMEM(hidden.shape, hidden.dtype),
+            pltpu.VMEM(dec.shape, dec.dtype),
+            pltpu.SemaphoreType.DMA((5,)),
+            pltpu.SemaphoreType.DMA((5,)),
+        ],
         name="hand_on",
     )(hidden, dec)
 

time: 157 us -> 156 us (level)
  Pallas kernels: 156 us -> 154 us
where the time goes in v8:
time: 156 us
  Pallas kernels  154 us (99%)
    pallas_call x1, Pallas kernels, attend_scatter(): pl.pallas_call(attend_kernel, out_shape=(jax.ShapeDtypeStruct((rows, widt...  81.3 us
    pallas_call x1, Pallas kernels, gather_multiply(): pl.pallas_call(gather_kernel, out_shape=(jax.ShapeDtypeStruct((query_weig...  71 us

profile of v8, /device:TPU:0, one launch (start us, length us, event | category | flops | bytes accessed | tf_op | source)
XLA Modules:
  0.0 155.8 jit_solution(17918127018239164514)
XLA Ops:
  1.3 71.0 %gather_multiply.1 = (bf16[4,1024,128]{2,1,0:T(8,128)(2,1)}, bf16[2,2048,128]{2,1,0:T(8,128)(2,1)}, f32[16,40,128]{2,1,0:T(8,128)}) custom-call(bf16[1,512]{1,0:T(2,128)(2,1)} %gain.1, bf16[8,8192]{1,0:T(8,128)(2,1)} %dec_q.3, s32[8]{0:T(128)} %dec_len.1, bf16[1024,512]{1,0:T(8,128)(2,1)} %tok_hbm.1, bf16[1024,128]{1,0:T(8,128)(2,1)} %prefix.1, ...), custom_call_target="tpu_custom_call" | custom-call | flops 10737418240 | bytes 16777216 | tf_op jit(solution)/shard_map/gather_multiply/pallas_call | solution.py:324
  72.3 81.3 %attend_scatter.1 = (bf16[1024,512]{1,0:T(8,128)(2,1)}, bf16[8,8192]{1,0:T(8,128)(2,1)}) custom-call(bf16[4,1024,128]{2,1,0:T(8,128)(2,1)} %get-tuple-element.7.q, bf16[2,2048,128]{2,1,0:T(8,128)(2,1)} %get-tuple-element.8.kv, bf16[8,8192]{1,0:T(8,128)(2,1)} %dec_q.3, f32[16,40,128]{2,1,0:T(8,128)} %get-tuple-element.9.old_share, s32[1,256]{1,0:T(1,128)} %bitcast.2, ...), custom_call_target="tpu_custom_call" | custom-call | flops 17179869184 | bytes 12582912 | tf_op jit(solution)/shard_map/attend_scatter/pallas_call | solution.py:838
  153.6 2.1 %hand_on.1 = (bf16[1024,512]{1,0:T(8,128)(2,1)}, bf16[8,8192]{1,0:T(8,128)(2,1)}) custom-call(bf16[1024,512]{1,0:T(8,128)(2,1)} %get-tuple-element.10.hidden, bf16[8,8192]{1,0:T(8,128)(2,1)} %get-tuple-element.11.dec), custom_call_target="tpu_custom_call" | custom-call | tf_op jit(solution)/shard_map/hand_on/pallas_call | solution.py:922
